TPU v7x, 128 devices: a whole 4x4x4 slice. The times are simulated.
128 devices in a mesh: clus: 2 (over core), help: 64 (over z, y, x).
Axes of the slice: x: 4, y: 4, z: 4, core: 2. Of those that a mesh axis runs over, the one named last changes fastest.
Arguments:
- embeddings: bfloat16 [2, 64, 512, 1024], P('clus', 'help'), may hold values from -100 to 100, as said below
- row_mask: int32 [2, 64, 512], P('clus', 'help'), may hold values 0 or 1
- tile_counts: int32 [2], P('clus'), may hold values from 1 to 64, as said below
Outputs:
- max_similarity: float32 [2, 64, 512], P('clus', 'help')
Inputs may be any that keep to these rules, and one draw needn't show every extreme that they name: `embeddings`: finite values; rows of any scale. `tile_counts`: some cluster has all 64 tiles live.
All inputs are finite; a program needn't handle non-finite values. No bound on the sum of `row_mask` on one device may be relied on, other than what follows from the above.
Results may differ from a plain program's by a relative error of at most 0.00054.
Values may be sent and summed in bfloat16 or wider, within the bound.
No kernel may reach another device: no remote copies, remote signals or barrier semaphores. Data moves between devices by JAX's collectives and lax.ppermute only.
A program may use at most 192 MiB of HBM per device.

v0:
```python
import jax
import jax.numpy as jnp
from jax import lax
from jax.sharding import PartitionSpec as P

EPS = 1e-06


def unit_rows(values):
    widths = values.astype(jnp.float32)
    meansq = jnp.mean(widths * widths, axis=-1, keepdims=True)
    scaled = widths * lax.rsqrt(meansq + EPS) * (1.0 / values.shape[-1] ** 0.5)
    return scaled.astype(jnp.bfloat16)


def row_best(queries, keys, allowed):
    sims = jnp.einsum("crd,csd->crs", queries, keys, preferred_element_type=jnp.float32)
    return jnp.max(jnp.where(allowed, sims, jnp.float32(-1.0)), axis=2)


def on_device(embeddings, row_mask, tile_counts):
    clusters = embeddings.shape[0]
    rows = embeddings.shape[2]
    width = embeddings.shape[3]
    place = lax.axis_index("help")
    units = unit_rows(embeddings[:, 0])
    flags = ((row_mask[:, 0] == 1) & (place < tile_counts[:, None])).astype(jnp.int32)
    offsets = jnp.arange(rows, dtype=jnp.int32)
    empty = jnp.full((clusters, rows), -1.0, jnp.float32)
    piece_units = lax.all_gather(units[:, None], "help", axis=1, tiled=True)
    piece_flags = lax.all_gather(flags[:, None], "help", axis=1, tiled=True)
    count = piece_units.shape[1]
    keys = piece_units.reshape(clusters, count * rows, width)
    key_pos = jnp.arange(count * rows, dtype=jnp.int32)
    row_pos = place * rows + offsets
    allowed = (key_pos[None, :] < row_pos[:, None])[None] & (
        piece_flags.reshape(clusters, count * rows)[:, None, :] == 1
    )
    best = jnp.maximum(empty, row_best(units, keys, allowed))
    return best[:, None]


def solution(mesh):
    in_specs = (P("clus", "help", None, None), P("clus", "help", None), P("clus"))
    out_specs = P("clus", "help", None)
    return jax.shard_map(
        on_device, mesh=mesh, in_specs=in_specs, out_specs=out_specs, check_vma=False
    )
```

profile of v0, /device:TPU:0, one launch (start us, length us, event | category | flops | bytes accessed | tf_op | source)
XLA Modules:
  0.0 344.8 jit_solution(593641223723483454)
XLA Ops:
  6.5 0.0 all-gather.2.cloned.1.call-start
  6.5 1.5 fusion.4
  8.0 2.5 fusion.6
  10.6 0.0 all-gather.2.cloned.1.call-update
  11.2 0.7 fusion.12
  11.9 181.0 %all_gather.6 = s32[1,64,512]{2,0,1:T(1,128)S(1)} all-gather(s32[1,1,512]{2,0,1:T(1,128)S(1)} %fusion.12), channel_id=1, replica_groups=mesh['clus'=2,'help'=64] {'help'}, dimensions={1}, use_global_device_ids=true | all-gather | bytes 133120 | tf_op jit(solution)/shard_map/all_gather | solution.py:31
  193.0 0.4 compare_reduce_fusion
  193.4 97.3 %all-gather.2.cloned.1.call-done = bf16[1,64,512,1024]{3,2,0,1:T(8,128)(2,1)} async-done(((bf16[1,1,512,1024]{3,2,0,1:T(8,128)(2,1)}), bf16[1,64,512,1024]{3,2,0,1:T(8,128)(2,1)}) %all-gather.2.cloned.1.call-update) | async-done | bytes 67108880 | tf_op jit(solution)/shard_map/all_gather | solution.py:30
  290.7 46.7 %select_reduce_fusion = f32[512]{0:T(512)S(1)} fusion(bf16[32768,1024]{1,0:T(8,128)(2,1)} %bitcast.8, s32[512]{0:T(512)S(1)} %iota_add_fusion, pred[32768]{0:T(1024)(128)(4,1)S(1)} %bitcast.43, bf16[1,1,512,1024]{3,2,1,0:T(8,128)(2,1)} %param.3, f32[512]{0:T(512)S(1)} %add_rsqrt_fusion), kind=kOutput, calls=%fused_computation | convolution fusion | flops 34428944384 | bytes 68196352 | tf_op jit(solution)/shard_map/crd,csd->crs/dot_general | solution.py:17
  337.4 0.6 broadcast_maximum_fusion
  (3 shorter events, 0.0 us)
Async XLA Ops:
  6.5 284.2 %all-gather.2.cloned.1.call-start = ((), (), s32[]{:S(2)}) async-start(), calls=%async_computation | async-start | bytes 68157440 | tf_op jit(solution)/shard_map/all_gather | solution.py:30
Sparse Core Ops, SparseCore 0:
  10.7 279.9 all-gather.1
where the time goes:
time: 346 us; the launch traced here: 345 us
  blocking collectives  181 us (52%)
  waiting for transfers between devices  97.3 us (28%)
  matrix products  46.7 us (13%)
  between operations  14.1 us (4%)
  other arithmetic  5.7 us (2%)
    all_gather x1, blocking collectives, on_device(): piece_flags = lax.all_gather(flags[:, None], 'help', axis=1, tiled=True)  181 us
    all_gather x1, waiting for transfers between devices, on_device(): piece_units = lax.all_gather(units[:, None], 'help', axis=1, tiled=True)  97.3 us
    dot_general x1, matrix products, row_best(): jnp.einsum('crd,csd->crs', queries, keys, preferred_element_type=jnp.floa...  46.7 us
  transfers between devices with their start and end apart: 1, of which 1 were waited for; matrix products, arithmetic and copies ran while one was open for 0% of the time, Pallas kernels for 0%

commit v1 on v0

v1 whole, which is shorter than its diff:
```python
import functools

import jax
import jax.numpy as jnp
import numpy as np
from jax import lax
from jax.experimental import pallas as pl
from jax.experimental.pallas import tpu as pltpu
from jax.sharding import PartitionSpec as P

EPS = 1e-06
SIDE = 4
FLAG_ROWS = 16
DEAD = -4.0

PLAN = [
    ((1, 0, 0), (0, 0, 0)),
    ((3, 0, 1), (0, 0, 0)),
    ((0, 1, 0), (0, 0, 0)),
    ((0, 3, 3), (0, 0, 0)),
    ((1, 1, 0), (1, 0, 0)),
    ((0, 3, 0), (0, 0, 0)),
    ((3, 0, 2), (3, 0, 1)),
    ((3, 3, 3), (0, 3, 3)),
    ((0, 3, 2), (0, 3, 3)),
    ((2, 1, 0), (1, 1, 0)),
]
OFFSETS = [(0, 0, 0)] + [d for d, _ in PLAN]
STAGES = [2, 4, 6, 8, 10]


def turned(d):
    return (d[1], d[0], -d[2])


def place_of(v):
    return ((v[0] % SIDE) * SIDE + v[1] % SIDE) * SIDE + v[2] % SIDE


def cube():
    return [(z, y, x) for z in range(SIDE) for y in range(SIDE) for x in range(SIDE)]


def add(a, b):
    return tuple(x + y for x, y in zip(a, b))


def sub(a, b):
    return tuple((x - y) % SIDE for x, y in zip(a, b))


def moves(step):
    pairs = []
    for c in range(2):
        s = turned(step) if c else step
        for v in cube():
            pairs.append((c * SIDE**3 + place_of(add(v, s)), c * SIDE**3 + place_of(v)))
    return pairs


def choose_pairs():
    best = {}
    for a in range(len(OFFSETS)):
        for b in range(a):
            g = sub(OFFSETS[a], OFFSETS[b])
            key = min(g, sub((0, 0, 0), g))
            if key not in best:
                best[key] = (a, b)
    assert len(best) == (SIDE**3 - 1 + 7) // 2
    return sorted(best.values())


def work_table():
    stages = [[] for _ in STAGES]
    for a, b in choose_pairs():
        stage = next(i for i, n in enumerate(STAGES) if a <= n)
        twin = all((2 * g) % SIDE == 0 for g in sub(OFFSETS[a], OFFSETS[b]))
        stages[stage].extend([(a, b, -1)] if twin else [(a, b, 0), (a, b, 1)])
    units = [u for s in stages for u in s]
    table = np.zeros((2, SIDE**3, len(units) * 3), np.int32)
    for c in range(2):
        offs = [turned(d) if c else d for d in OFFSETS]
        for v in cube():
            for n, (a, b, half) in enumerate(units):
                first = place_of(add(v, offs[a])) < place_of(add(v, offs[b]))
                k, q = (a, b) if first else (b, a)
                h = half if half >= 0 else int(first)
                table[c, place_of(v), 3 * n : 3 * n + 3] = (k, q, h)
    return table, [len(s) for s in stages], stages


def unit_kernel(alive, x_ref, mask_ref, out_ref):
    rows, width = x_ref.shape
    x = x_ref[...].astype(jnp.float32)
    meansq = jnp.mean(x * x, axis=-1, keepdims=True)
    out_ref[:rows, :] = (x * lax.rsqrt(meansq + EPS) * (1.0 / width**0.5)).astype(jnp.bfloat16)
    live = (mask_ref[...] == 1) & (alive[0] == 1)
    bias = jnp.broadcast_to(jnp.where(live, 0.0, DEAD), (FLAG_ROWS, rows))
    top = lax.broadcasted_iota(jnp.int32, (FLAG_ROWS, rows), 0) == 0
    out_ref[rows:, :] = jnp.zeros((FLAG_ROWS, width), jnp.bfloat16)
    out_ref[rows:, :rows] = jnp.where(top, bias, 0.0).astype(jnp.bfloat16)


def dot_t(a, b):
    return lax.dot_general(a, b, (((1,), (1,)), ((), ())), preferred_element_type=jnp.float32)


def key_bias(flags):
    ones = jnp.ones((flags.shape[0], 128), jnp.bfloat16)
    return lax.dot_general(flags, ones, (((0,), (0,)), ((), ())), preferred_element_type=jnp.float32)


def fold_rows(s):
    n, w = s.shape
    return jnp.max(s.reshape(n // 8, 8, w), axis=0)


def self_kernel(t_ref, acc_ref, *, slots):
    rows = t_ref.shape[0] - FLAG_ROWS
    half = rows // 2
    bias = key_bias(t_ref[rows:, :rows])
    acc_ref[...] = jnp.full(acc_ref.shape, -1.0, jnp.float32)
    for h in range(2):
        n = half * (h + 1)
        s = dot_t(t_ref[:n, :], t_ref[h * half : (h + 1) * half, :])
        key = lax.broadcasted_iota(jnp.int32, (n, half), 0)
        query = lax.broadcasted_iota(jnp.int32, (n, half), 1) + h * half
        s = jnp.where(key < query, s + jnp.tile(bias[:n], (1, half // 128)), -1.0)
        acc_ref[0, h] = jnp.maximum(acc_ref[0, h], fold_rows(s))


def pair_kernel(tab, *refs, slots, first, stage_units, last):
    n = len(slots)
    tiles, acc_in, outs = refs[:n], refs[n], refs[n + 1 : -4]
    stack, biases, acc, sems = refs[-4:]
    rows = stack.shape[1] - FLAG_ROWS
    half = rows // 2
    order = sorted(range(n), key=lambda i: first[i])
    for i in order:
        pltpu.make_async_copy(tiles[i], stack.at[slots[i]], sems.at[i]).start()
    acc[...] = acc_in[...]
    start, count = stage_units

    def unit(u, carry):
        for i in range(n):

            @pl.when(u == first[i])
            def _():
                pltpu.make_async_copy(tiles[i], stack.at[slots[i]], sems.at[i]).wait()
                biases[slots[i]] = key_bias(stack[slots[i], rows:, :rows])

        at = 3 * (start + u)
        k, q, h = tab[at], tab[at + 1], tab[at + 2]
        query = stack[q, pl.ds(pl.multiple_of(h * half, half), half), :]
        s = dot_t(stack[k, :rows, :], query)
        s = s + jnp.tile(biases[k], (1, half // 128))
        acc[q, h] = jnp.maximum(acc[q, h], fold_rows(s))
        return carry

    lax.fori_loop(0, count, unit, 0)
    if last:
        for s in range(acc.shape[0]):
            for h in range(2):
                outs[s][:, h * half : (h + 1) * half] = jnp.max(acc[s, h], axis=0, keepdims=True)
    else:
        outs[0][...] = acc[...]


def on_device(embeddings, row_mask, tile_counts):
    rows, width = embeddings.shape[2:]
    half = rows // 2
    clus, place = lax.axis_index("clus"), lax.axis_index("help")
    table, unit_counts, stages = work_table()
    tab = jnp.asarray(table)[clus, place]
    alive = (place < tile_counts).astype(jnp.int32)
    slots = len(OFFSETS)
    vmem, smem, hbm = (pl.BlockSpec(memory_space=m) for m in (pltpu.VMEM, pltpu.SMEM, pl.ANY))
    tile_shape = (rows + FLAG_ROWS, width)
    acc_shape = (slots, 2, 8, half)

    own = pl.pallas_call(
        unit_kernel,
        out_shape=jax.ShapeDtypeStruct(tile_shape, jnp.bfloat16),
        in_specs=[smem, vmem, vmem],
        out_specs=vmem,
    )(alive, embeddings[0, 0], row_mask[0])
    held = {OFFSETS[0]: own}
    for d, source in PLAN:
        held[d] = lax.ppermute(held[source], ("clus", "help"), moves(sub(d, source)))

    acc = pl.pallas_call(
        functools.partial(self_kernel, slots=slots),
        out_shape=jax.ShapeDtypeStruct(acc_shape, jnp.float32),
        in_specs=[vmem],
        out_specs=vmem,
        cost_estimate=pl.CostEstimate(flops=2 * rows * rows * width, bytes_accessed=2 * rows * width, transcendentals=0),
    )(own)
    start = 0
    for i, units in enumerate(stages):
        used = sorted({s for a, b, _ in units for s in (a, b)})
        first = [next(n for n, u in enumerate(units) if s in u[:2]) for s in used]
        last = i == len(stages) - 1
        shapes = [(1, rows)] * slots if last else [acc_shape]
        acc = pl.pallas_call(
            functools.partial(pair_kernel, slots=used, first=first, stage_units=(start, len(units)), last=last),
            out_shape=[jax.ShapeDtypeStruct(s, jnp.float32) for s in shapes],
            in_specs=[smem] + [hbm] * len(used) + [vmem],
            out_specs=[vmem] * len(shapes),
            scratch_shapes=[
                pltpu.VMEM((slots, *tile_shape), jnp.bfloat16),
                pltpu.VMEM((slots, rows, 128), jnp.float32),
                pltpu.VMEM(acc_shape, jnp.float32),
                pltpu.SemaphoreType.DMA((len(used),)),
            ],
            compiler_params=pltpu.CompilerParams(vmem_limit_bytes=32 * 2**20),
            cost_estimate=pl.CostEstimate(
                flops=len(units) * rows * rows * width, bytes_accessed=2 * len(used) * rows * width, transcendentals=0
            ),
        )(tab, *[held[OFFSETS[s]] for s in used], *([acc] if i == 0 else acc))
        start += len(units)
    best = acc[0]
    for s in range(1, slots):
        best = jnp.maximum(best, lax.ppermute(acc[s], ("clus", "help"), moves(sub((0, 0, 0), OFFSETS[s]))))
    return best[None]


def solution(mesh):
    in_specs = (P("clus", "help", None, None), P("clus", "help", None), P("clus"))
    out_specs = P("clus", "help", None)
    return jax.shard_map(on_device, mesh=mesh, in_specs=in_specs, out_specs=out_specs, check_vma=False)
```

time: 346 us -> 117 us (0.34)
  blocking collectives: 181 us -> 0 us
  waiting for transfers between devices: 97.3 us -> 27.6 us
  Pallas kernels: 0 us -> 50.5 us
  matrix products: 46.7 us -> 0 us
  starting transfers between devices: 0.01 us -> 35.8 us
  between operations: 14.1 us -> 0.78 us
  other arithmetic: 5.7 us -> 0.59 us
    all_gather x1 -> x0, blocking collectives: 181 us -> none  [on_device(): piece_flags = lax.all_gather(flags[:, None], 'help', axis=1, tiled=True)]
    all_gather x1 -> x0, waiting for transfers between devices: 97.3 us -> none  [on_device(): piece_units = lax.all_gather(units[:, None], 'help', axis=1, tiled=True)]
    pallas_call x0 -> x7, Pallas kernels: none -> 50.5 us  [the longest x5 45.4 us: on_device(): pl.pallas_call(functools.partial(pair_kernel, slots=used, first=first, st...]
    dot_general x1 -> x0, matrix products: 46.7 us -> none  [row_best(): jnp.einsum('crd,csd->crs', queries, keys, preferred_element_type=jnp.floa...]
    ppermute x0 -> x20, starting transfers between devices: none -> 35.8 us  [the longest x10 18.3 us: on_device(): lax.ppermute(acc[s], ('clus', 'help'), moves(sub((0, 0, 0), OFFSETS[s])))]
    ppermute x0 -> x20, waiting for transfers between devices: none -> 27.6 us  [the longest x10 21.6 us: on_device(): lax.ppermute(held[source], ('clus', 'help'), moves(sub(d, source)))]
  transfers between devices with their start and end apart: 1 -> 20, of which waited for: 1 -> 6; matrix products, arithmetic and copies ran while one was open for 0% -> 1% of each run, Pallas kernels for 0% -> 34%
where the time goes in v1:
time: 117 us
  Pallas kernels  50.5 us (43%)
  starting transfers between devices  35.8 us (31%)
  waiting for transfers between devices  27.6 us (24%)
  local copies, waits for them, and re-layouts  1.63 us (1%)
    pallas_call x5, Pallas kernels, on_device(): pl.pallas_call(functools.partial(pair_kernel, slots=used, first=first, st...  45.4 us
    ppermute x10, waiting for transfers between devices, on_device(): lax.ppermute(held[source], ('clus', 'help'), moves(sub(d, source)))  21.6 us
    ppermute x10, starting transfers between devices, on_device(): lax.ppermute(acc[s], ('clus', 'help'), moves(sub((0, 0, 0), OFFSETS[s])))  18.3 us
    ppermute x10, starting transfers between devices, on_device(): lax.ppermute(held[source], ('clus', 'help'), moves(sub(d, source)))  17.4 us
    ppermute x10, waiting for transfers between devices, on_device(): lax.ppermute(acc[s], ('clus', 'help'), moves(sub((0, 0, 0), OFFSETS[s])))  6 us
    pallas_call x1, Pallas kernels, on_device(): pl.pallas_call(unit_kernel, out_shape=jax.ShapeDtypeStruct(tile_shape, jn...  2.6 us
    pallas_call x1, Pallas kernels, on_device(): pl.pallas_call(functools.partial(self_kernel, slots=slots), out_shape=jax...  2.58 us
  transfers between devices with their start and end apart: 20, of which 6 were waited for; matrix products, arithmetic and copies ran while one was open for 1% of the time, Pallas kernels for 34%

profile of v1, /device:TPU:0, one launch (start us, length us, event | category | flops | bytes accessed | tf_op | source)
XLA Modules:
  0.0 116.9 jit_solution(8602425307439722869)
XLA Ops:
  0.7 2.6 %shard_map.46.t_ref.refs_0_ = bf16[528,1024]{1,0:T(8,128)(2,1)} custom-call(s32[1]{0:T(128)S(6)} %convert_element_type.3.alive, bf16[512,1024]{1,0:T(8,128)(2,1)} %bitcast.11, s32[1,512]{1,0:T(1,128)} %bitcast.12), custom_call_target="tpu_custom_call" | custom-call | tf_op jit(solution)/shard_map/pallas_call | solution.py:181
  3.3 0.0 copy-start
  3.3 4.1 %collective-permute-start.1 = (bf16[528,1024]{1,0:T(8,128)(2,1)}, bf16[528,1024]{1,0:T(8,128)(2,1)}, u32[]{:S(2)}, u32[]{:S(2)}) collective-permute-start(bf16[528,1024]{1,0:T(8,128)(2,1)} %shard_map.46.t_ref.refs_0_), channel_id=1, source_target_pairs={{16,0},{17,1},{18,2},{19,3},{20,4},{21,5},{22,6},{23,7},{24,8},{25... | collective-permute-start | bytes 3244040 | tf_op jit(solution)/shard_map/ppermute | solution.py:189
  7.4 2.5 %collective-permute-start.4 = (bf16[528,1024]{1,0:T(8,128)(2,1)}, bf16[528,1024]{1,0:T(8,128)(2,1)}, u32[]{:S(2)}, u32[]{:S(2)}) collective-permute-start(bf16[528,1024]{1,0:T(8,128)(2,1)} %shard_map.46.t_ref.refs_0_), channel_id=1, source_target_pairs={{15,0},{12,1},{13,2},{14,3},{3,4},{0,5},{1,6},{2,7},{7,8},{4,9},{5... | collective-permute-start | bytes 3244040 | tf_op jit(solution)/shard_map/ppermute | solution.py:189
  9.9 0.0 collective-permute-start.8
  9.9 1.7 %collective-permute-start = (bf16[528,1024]{1,0:T(8,128)(2,1)}, bf16[528,1024]{1,0:T(8,128)(2,1)S(1)}, u32[]{:S(2)}, u32[]{:S(2)}) collective-permute-start(bf16[528,1024]{1,0:T(8,128)(2,1)} %shard_map.46.t_ref.refs_0_), channel_id=1, source_target_pairs={{4,0},{5,1},{6,2},{7,3},{8,4},{9,5},{10,6},{11,7},{12,8},{13,9},{1... | collective-permute-start | bytes 3244040 | tf_op jit(solution)/shard_map/ppermute | solution.py:189
  11.5 17.6 %collective-permute-done.1.refs_1_ = bf16[528,1024]{1,0:T(8,128)(2,1)} collective-permute-done((bf16[528,1024]{1,0:T(8,128)(2,1)}, bf16[528,1024]{1,0:T(8,128)(2,1)}, u32[]{:S(2)}, u32[]{:S(2)}) %collective-permute-start.1) | collective-permute-done | bytes 1081376 | tf_op jit(solution)/shard_map/ppermute | solution.py:189
  29.2 3.3 %collective-permute-start.2 = (bf16[528,1024]{1,0:T(8,128)(2,1)}, bf16[528,1024]{1,0:T(8,128)(2,1)S(1)}, u32[]{:S(2)}, u32[]{:S(2)}) collective-permute-start(bf16[528,1024]{1,0:T(8,128)(2,1)} %collective-permute-done.1.refs_1_), channel_id=1, source_target_pairs={{4,0},{5,1},{6,2},{7,3},{8,4},{9,5},{10,6},{11,7},{12,8},{13,9},{1... | collective-permute-start | bytes 3244040 | tf_op jit(solution)/shard_map/ppermute | solution.py:189
  32.4 0.0 collective-permute-start.3
  32.4 3.9 %collective-permute-done.4.refs_4_.refs_3_ = bf16[528,1024]{1,0:T(8,128)(2,1)} collective-permute-done((bf16[528,1024]{1,0:T(8,128)(2,1)}, bf16[528,1024]{1,0:T(8,128)(2,1)}, u32[]{:S(2)}, u32[]{:S(2)}) %collective-permute-start.4) | collective-permute-done | bytes 1081376 | tf_op jit(solution)/shard_map/ppermute | solution.py:189
  36.3 0.0 collective-permute-start.5
  36.3 0.0 collective-permute-done.8.refs_2_.refs_1_
  36.3 2.5 %collective-permute-start.9 = (bf16[528,1024]{1,0:T(8,128)(2,1)}, bf16[528,1024]{1,0:T(8,128)(2,1)}, u32[]{:S(2)}, u32[]{:S(2)}) collective-permute-start(bf16[528,1024]{1,0:T(8,128)(2,1)} %collective-permute-done.8.refs_2_.refs_1_), channel_id=1, source_target_pairs={{1,0},{2,1},{3,2},{0,3},{5,4},{6,5},{7,6},{4,7},{9,8},{10,9},{11,1... | collective-permute-start | bytes 3244040 | tf_op jit(solution)/shard_map/ppermute | solution.py:189
  38.8 2.6 %shard_map.47.refs_3_ = f32[11,2,8,256]{3,2,1,0:T(8,128)} custom-call(bf16[528,1024]{1,0:T(8,128)(2,1)} %shard_map.46.t_ref.refs_0_), custom_call_target="tpu_custom_call" | custom-call | flops 536870912 | bytes 1048576 | tf_op jit(solution)/shard_map/pallas_call | solution.py:191
  41.4 0.7 constant_dynamic-slice_fusion
  42.1 0.0 copy-done
  42.1 0.0 copy-start.1
  42.1 0.9 copy-done.1
  43.0 5.3 %shard_map.48.refs_5_ = f32[11,2,8,256]{3,2,1,0:T(8,128)S(1)} custom-call(s32[189]{0:T(256)S(1)} %bitcast.6, bf16[528,1024]{1,0:T(8,128)(2,1)S(1)} %copy-done, bf16[528,1024]{1,0:T(8,128)(2,1)} %collective-permute-done.1.refs_1_, bf16[528,1024]{1,0:T(8,128)(2,1)} %collective-permute-done.8.refs_2_.refs_1_, f32[11,2,8,256]{3,2,1,0:T(8,128)S(1)} %copy-done.1), custom_call_target="tpu_custom_call" | custom-call | flops 1610612736 | bytes 3145728 | tf_op jit(solution)/shard_map/pallas_call | solution.py:204
  48.4 0.0 collective-permute-done.refs_3_.refs_2_.refs_1_
  48.4 0.1 collective-permute-start.6
  48.5 0.0 collective-permute-done.2.refs_4_.refs_5_.refs_2_
  48.5 3.3 %collective-permute-start.7 = (bf16[528,1024]{1,0:T(8,128)(2,1)S(1)}, bf16[528,1024]{1,0:T(8,128)(2,1)S(1)}, u32[]{:S(2)}, u32[]{:S(2)}) collective-permute-start(bf16[528,1024]{1,0:T(8,128)(2,1)S(1)} %collective-permute-done.2.refs_4_.refs_5_.refs_2_), channel_id=1, source_target_pairs={{16,0},{17,1},{18,2},{19,3},{20,4},{21,5},{22,6},{23,7},{24,8},{25... | collective-permute-start | bytes 3244040 | tf_op jit(solution)/shard_map/ppermute | solution.py:189
  51.8 9.0 %shard_map.49.refs_6_ = f32[11,2,8,256]{3,2,1,0:T(8,128)S(1)} custom-call(s32[189]{0:T(256)S(1)} %bitcast.7, bf16[528,1024]{1,0:T(8,128)(2,1)S(1)} %copy-done, bf16[528,1024]{1,0:T(8,128)(2,1)} %collective-permute-done.1.refs_1_, bf16[528,1024]{1,0:T(8,128)(2,1)} %collective-permute-done.8.refs_2_.refs_1_, ...), custom_call_target="tpu_custom_call" | custom-call | flops 3758096384 | bytes 5242880 | tf_op jit(solution)/shard_map/pallas_call | solution.py:204
  60.8 0.1 collective-permute-done.3.refs_5_.refs_6_.refs_3_
  60.9 8.9 %shard_map.50.refs_9_ = f32[11,2,8,256]{3,2,1,0:T(8,128)S(1)} custom-call(s32[189]{0:T(256)S(1)} %bitcast.8, bf16[528,1024]{1,0:T(8,128)(2,1)S(1)} %copy-done, bf16[528,1024]{1,0:T(8,128)(2,1)} %collective-permute-done.8.refs_2_.refs_1_, bf16[528,1024]{1,0:T(8,128)(2,1)S(1)} %collective-permute-done.refs_3_.refs_2_.refs_1_, ...), custom_call_target="tpu_custom_call" | custom-call | flops 3489660928 | bytes 6291456 | tf_op jit(solution)/shard_map/pallas_call | solution.py:204
  69.8 0.0 collective-permute-done.5.refs_8_.refs_4_
  69.8 0.0 collective-permute-done.9.refs_7_
  69.9 13.7 %shard_map.51.refs_7_ = f32[11,2,8,256]{3,2,1,0:T(8,128)S(1)} custom-call(s32[189]{0:T(256)S(1)} %bitcast.9, bf16[528,1024]{1,0:T(8,128)(2,1)S(1)} %copy-done, bf16[528,1024]{1,0:T(8,128)(2,1)} %collective-permute-done.1.refs_1_, bf16[528,1024]{1,0:T(8,128)(2,1)} %collective-permute-done.8.refs_2_.refs_1_, ...), custom_call_target="tpu_custom_call" | custom-call | flops 5100273664 | bytes 9437184 | tf_op jit(solution)/shard_map/pallas_call | solution.py:204
  83.6 0.0 collective-permute-done.6.refs_5_
  83.6 0.0 collective-permute-done.7.refs_6_
  83.6 8.4 %shard_map.52 = (f32[1,512]{1,0:T(1,128)S(1)}, f32[1,512]{1,0:T(1,128)S(1)}, f32[1,512]{1,0:T(1,128)S(1)}, f32[1,512]{1,0:T(1,128)S(1)}, f32[1,512]{1,0:T(1,128)...) custom-call(s32[189]{0:T(256)S(1)} %bitcast.10, ...), custom_call_target="tpu_custom_call" | custom-call | flops 2952790016 | bytes 7340032 | tf_op jit(solution)/shard_map/pallas_call | solution.py:204
  92.0 0.1 collective-permute-start.10
  92.1 3.1 %collective-permute-start.11 = (f32[1,512]{1,0:T(1,128)S(1)}, f32[1,512]{1,0:T(1,128)S(1)}, u32[]{:S(2)}, u32[]{:S(2)}) collective-permute-start(f32[1,512]{1,0:T(1,128)S(1)} %get-tuple-element.18), channel_id=1, source_target_pairs={{19,0},{16,1},{17,2},{18,3},{23,4},{20,5},{21,6},{22,7},{27,8},{24... | collective-permute-start | bytes 6152 | tf_op jit(solution)/shard_map/ppermute | solution.py:223
  95.2 0.6 collective-permute-start.12
  95.7 4.9 %collective-permute-start.13 = (f32[1,512]{1,0:T(1,128)S(1)}, f32[1,512]{1,0:T(1,128)S(1)}, u32[]{:S(2)}, u32[]{:S(2)}) collective-permute-start(f32[1,512]{1,0:T(1,128)S(1)} %get-tuple-element.20), channel_id=1, source_target_pairs={{5,0},{6,1},{7,2},{4,3},{9,4},{10,5},{11,6},{8,7},{13,8},{14,9},{1... | collective-permute-start | bytes 6152 | tf_op jit(solution)/shard_map/ppermute | solution.py:223
  100.7 0.0 collective-permute-start.14
  100.7 0.0 collective-permute-done.10
  100.7 1.5 %collective-permute-start.15 = (f32[1,512]{1,0:T(1,128)S(1)}, f32[1,512]{1,0:T(1,128)S(1)}, u32[]{:S(2)}, u32[]{:S(2)}) collective-permute-start(f32[1,512]{1,0:T(1,128)S(1)} %get-tuple-element.22), channel_id=1, source_target_pairs={{4,0},{5,1},{6,2},{7,3},{8,4},{9,5},{10,6},{11,7},{12,8},{13,9},{1... | collective-permute-start | bytes 6152 | tf_op jit(solution)/shard_map/ppermute | solution.py:223
  102.2 0.0 collective-permute-done.11
  102.2 4.9 %collective-permute-start.16 = (f32[1,512]{1,0:T(1,128)S(1)}, f32[1,512]{1,0:T(1,128)S(1)}, u32[]{:S(2)}, u32[]{:S(2)}) collective-permute-start(f32[1,512]{1,0:T(1,128)S(1)} %get-tuple-element.23), channel_id=1, source_target_pairs={{18,0},{19,1},{16,2},{17,3},{22,4},{23,5},{20,6},{21,7},{26,8},{27... | collective-permute-start | bytes 6152 | tf_op jit(solution)/shard_map/ppermute | solution.py:223
  107.1 0.0 collective-permute-done.12
  107.1 0.5 collective-permute-start.17
  107.6 0.0 collective-permute-done.13
  107.6 1.6 %collective-permute-start.18 = (f32[1,512]{1,0:T(1,128)S(1)}, f32[1,512]{1,0:T(1,128)S(1)}, u32[]{:S(2)}, u32[]{:S(2)}) collective-permute-start(f32[1,512]{1,0:T(1,128)S(1)} %get-tuple-element.25), channel_id=1, source_target_pairs={{6,0},{7,1},{4,2},{5,3},{10,4},{11,5},{8,6},{9,7},{14,8},{15,9},{1... | collective-permute-start | bytes 6152 | tf_op jit(solution)/shard_map/ppermute | solution.py:223
  109.1 0.0 collective-permute-done.14
  109.1 1.2 %collective-permute-start.19 = (f32[1,512]{1,0:T(1,128)S(1)}, f32[1,512]{1,0:T(1,128)S(1)}, u32[]{:S(2)}, u32[]{:S(2)}) collective-permute-start(f32[1,512]{1,0:T(1,128)S(1)} %get-tuple-element.26), channel_id=1, source_target_pairs={{44,0},{45,1},{46,2},{47,3},{32,4},{33,5},{34,6},{35,7},{36,8},{37... | collective-permute-start | bytes 6152 | tf_op jit(solution)/shard_map/ppermute | solution.py:223
  110.4 0.0 collective-permute-done.15
  110.4 0.0 collective-permute-done.16
  110.4 2.1 %collective-permute-done.17 = f32[1,512]{1,0:T(1,128)S(1)} collective-permute-done((f32[1,512]{1,0:T(1,128)S(1)}, f32[1,512]{1,0:T(1,128)S(1)}, u32[]{:S(2)}, u32[]{:S(2)}) %collective-permute-start.17) | collective-permute-done | bytes 2080 | tf_op jit(solution)/shard_map/ppermute | solution.py:223
  112.5 1.1 collective-permute-done.18
  113.6 2.8 %collective-permute-done.19 = f32[1,512]{1,0:T(1,128)S(1)} collective-permute-done((f32[1,512]{1,0:T(1,128)S(1)}, f32[1,512]{1,0:T(1,128)S(1)}, u32[]{:S(2)}, u32[]{:S(2)}) %collective-permute-start.19) | collective-permute-done | bytes 2080 | tf_op jit(solution)/shard_map/ppermute | solution.py:223
  116.3 0.6 maximum_bitcast_fusion
Async XLA Ops:
  3.3 38.9 %copy-start = (bf16[528,1024]{1,0:T(8,128)(2,1)S(1)}, bf16[528,1024]{1,0:T(8,128)(2,1)}, u32[]{:S(2)}) copy-start(bf16[528,1024]{1,0:T(8,128)(2,1)} %shard_map.46.t_ref.refs_0_) | copy-start | bytes 3244036
  3.3 25.9 %collective-permute-start.1 = (bf16[528,1024]{1,0:T(8,128)(2,1)}, bf16[528,1024]{1,0:T(8,128)(2,1)}, u32[]{:S(2)}, u32[]{:S(2)}) collective-permute-start(bf16[528,1024]{1,0:T(8,128)(2,1)} %shard_map.46.t_ref.refs_0_), channel_id=1, source_target_pairs={{16,0},{17,1},{18,2},{19,3},{20,4},{21,5},{22,6},{23,7},{24,8},{25... | collective-permute-start | bytes 3244040 | tf_op jit(solution)/shard_map/ppermute | solution.py:189
  7.4 28.9 %collective-permute-start.4 = (bf16[528,1024]{1,0:T(8,128)(2,1)}, bf16[528,1024]{1,0:T(8,128)(2,1)}, u32[]{:S(2)}, u32[]{:S(2)}) collective-permute-start(bf16[528,1024]{1,0:T(8,128)(2,1)} %shard_map.46.t_ref.refs_0_), channel_id=1, source_target_pairs={{15,0},{12,1},{13,2},{14,3},{3,4},{0,5},{1,6},{2,7},{7,8},{4,9},{5... | collective-permute-start | bytes 3244040 | tf_op jit(solution)/shard_map/ppermute | solution.py:189
  9.9 26.4 %collective-permute-start.8 = (bf16[528,1024]{1,0:T(8,128)(2,1)}, bf16[528,1024]{1,0:T(8,128)(2,1)}, u32[]{:S(2)}, u32[]{:S(2)}) collective-permute-start(bf16[528,1024]{1,0:T(8,128)(2,1)} %shard_map.46.t_ref.refs_0_), channel_id=1, source_target_pairs={{49,0},{50,1},{51,2},{48,3},{53,4},{54,5},{55,6},{52,7},{57,8},{58... | collective-permute-start | bytes 3244040 | tf_op jit(solution)/shard_map/ppermute | solution.py:189
  9.9 38.5 %collective-permute-start = (bf16[528,1024]{1,0:T(8,128)(2,1)}, bf16[528,1024]{1,0:T(8,128)(2,1)S(1)}, u32[]{:S(2)}, u32[]{:S(2)}) collective-permute-start(bf16[528,1024]{1,0:T(8,128)(2,1)} %shard_map.46.t_ref.refs_0_), channel_id=1, source_target_pairs={{4,0},{5,1},{6,2},{7,3},{8,4},{9,5},{10,6},{11,7},{12,8},{13,9},{1... | collective-permute-start | bytes 3244040 | tf_op jit(solution)/shard_map/ppermute | solution.py:189
  29.2 19.3 %collective-permute-start.2 = (bf16[528,1024]{1,0:T(8,128)(2,1)}, bf16[528,1024]{1,0:T(8,128)(2,1)S(1)}, u32[]{:S(2)}, u32[]{:S(2)}) collective-permute-start(bf16[528,1024]{1,0:T(8,128)(2,1)} %collective-permute-done.1.refs_1_), channel_id=1, source_target_pairs={{4,0},{5,1},{6,2},{7,3},{8,4},{9,5},{10,6},{11,7},{12,8},{13,9},{1... | collective-permute-start | bytes 3244040 | tf_op jit(solution)/shard_map/ppermute | solution.py:189
  32.4 28.5 %collective-permute-start.3 = (bf16[528,1024]{1,0:T(8,128)(2,1)}, bf16[528,1024]{1,0:T(8,128)(2,1)}, u32[]{:S(2)}, u32[]{:S(2)}) collective-permute-start(bf16[528,1024]{1,0:T(8,128)(2,1)} %shard_map.46.t_ref.refs_0_), channel_id=1, source_target_pairs={{12,0},{13,1},{14,2},{15,3},{0,4},{1,5},{2,6},{3,7},{4,8},{5,9},{6... | collective-permute-start | bytes 3244040 | tf_op jit(solution)/shard_map/ppermute | solution.py:189
  36.3 33.5 %collective-permute-start.5 = (bf16[528,1024]{1,0:T(8,128)(2,1)}, bf16[528,1024]{1,0:T(8,128)(2,1)}, u32[]{:S(2)}, u32[]{:S(2)}) collective-permute-start(bf16[528,1024]{1,0:T(8,128)(2,1)} %collective-permute-done.4.refs_4_.refs_3_), channel_id=1, source_target_pairs={{48,0},{49,1},{50,2},{51,3},{52,4},{53,5},{54,6},{55,7},{56,8},{57... | collective-permute-start | bytes 3244040 | tf_op jit(solution)/shard_map/ppermute | solution.py:189
  36.3 33.5 %collective-permute-start.9 = (bf16[528,1024]{1,0:T(8,128)(2,1)}, bf16[528,1024]{1,0:T(8,128)(2,1)}, u32[]{:S(2)}, u32[]{:S(2)}) collective-permute-start(bf16[528,1024]{1,0:T(8,128)(2,1)} %collective-permute-done.8.refs_2_.refs_1_), channel_id=1, source_target_pairs={{1,0},{2,1},{3,2},{0,3},{5,4},{6,5},{7,6},{4,7},{9,8},{10,9},{11,1... | collective-permute-start | bytes 3244040 | tf_op jit(solution)/shard_map/ppermute | solution.py:189
  42.1 0.9 copy-start.1
  48.4 35.2 %collective-permute-start.6 = (bf16[528,1024]{1,0:T(8,128)(2,1)}, bf16[528,1024]{1,0:T(8,128)(2,1)S(1)}, u32[]{:S(2)}, u32[]{:S(2)}) collective-permute-start(bf16[528,1024]{1,0:T(8,128)(2,1)} %collective-permute-done.4.refs_4_.refs_3_), channel_id=1, source_target_pairs={{3,0},{0,1},{1,2},{2,3},{7,4},{4,5},{5,6},{6,7},{11,8},{8,9},{9,10... | collective-permute-start | bytes 3244040 | tf_op jit(solution)/shard_map/ppermute | solution.py:189
  48.5 35.1 %collective-permute-start.7 = (bf16[528,1024]{1,0:T(8,128)(2,1)S(1)}, bf16[528,1024]{1,0:T(8,128)(2,1)S(1)}, u32[]{:S(2)}, u32[]{:S(2)}) collective-permute-start(bf16[528,1024]{1,0:T(8,128)(2,1)S(1)} %collective-permute-done.2.refs_4_.refs_5_.refs_2_), channel_id=1, source_target_pairs={{16,0},{17,1},{18,2},{19,3},{20,4},{21,5},{22,6},{23,7},{24,8},{25... | collective-permute-start | bytes 3244040 | tf_op jit(solution)/shard_map/ppermute | solution.py:189
  92.0 8.7 %collective-permute-start.10 = (f32[1,512]{1,0:T(1,128)S(1)}, f32[1,512]{1,0:T(1,128)S(1)}, u32[]{:S(2)}, u32[]{:S(2)}) collective-permute-start(f32[1,512]{1,0:T(1,128)S(1)} %get-tuple-element.17), channel_id=1, source_target_pairs={{48,0},{49,1},{50,2},{51,3},{52,4},{53,5},{54,6},{55,7},{56,8},{57... | collective-permute-start | bytes 6152 | tf_op jit(solution)/shard_map/ppermute | solution.py:223
  92.1 10.1 %collective-permute-start.11 = (f32[1,512]{1,0:T(1,128)S(1)}, f32[1,512]{1,0:T(1,128)S(1)}, u32[]{:S(2)}, u32[]{:S(2)}) collective-permute-start(f32[1,512]{1,0:T(1,128)S(1)} %get-tuple-element.18), channel_id=1, source_target_pairs={{19,0},{16,1},{17,2},{18,3},{23,4},{20,5},{21,6},{22,7},{27,8},{24... | collective-permute-start | bytes 6152 | tf_op jit(solution)/shard_map/ppermute | solution.py:223
  95.2 11.9 %collective-permute-start.12 = (f32[1,512]{1,0:T(1,128)S(1)}, f32[1,512]{1,0:T(1,128)S(1)}, u32[]{:S(2)}, u32[]{:S(2)}) collective-permute-start(f32[1,512]{1,0:T(1,128)S(1)} %get-tuple-element.19), channel_id=1, source_target_pairs={{12,0},{13,1},{14,2},{15,3},{0,4},{1,5},{2,6},{3,7},{4,8},{5,9},{6... | collective-permute-start | bytes 6152 | tf_op jit(solution)/shard_map/ppermute | solution.py:223
  95.7 11.9 %collective-permute-start.13 = (f32[1,512]{1,0:T(1,128)S(1)}, f32[1,512]{1,0:T(1,128)S(1)}, u32[]{:S(2)}, u32[]{:S(2)}) collective-permute-start(f32[1,512]{1,0:T(1,128)S(1)} %get-tuple-element.20), channel_id=1, source_target_pairs={{5,0},{6,1},{7,2},{4,3},{9,4},{10,5},{11,6},{8,7},{13,8},{14,9},{1... | collective-permute-start | bytes 6152 | tf_op jit(solution)/shard_map/ppermute | solution.py:223
  100.7 8.5 %collective-permute-start.14 = (f32[1,512]{1,0:T(1,128)S(1)}, f32[1,512]{1,0:T(1,128)S(1)}, u32[]{:S(2)}, u32[]{:S(2)}) collective-permute-start(f32[1,512]{1,0:T(1,128)S(1)} %get-tuple-element.21), channel_id=1, source_target_pairs={{60,0},{61,1},{62,2},{63,3},{48,4},{49,5},{50,6},{51,7},{52,8},{53... | collective-permute-start | bytes 6152 | tf_op jit(solution)/shard_map/ppermute | solution.py:223
  100.7 9.7 %collective-permute-start.15 = (f32[1,512]{1,0:T(1,128)S(1)}, f32[1,512]{1,0:T(1,128)S(1)}, u32[]{:S(2)}, u32[]{:S(2)}) collective-permute-start(f32[1,512]{1,0:T(1,128)S(1)} %get-tuple-element.22), channel_id=1, source_target_pairs={{4,0},{5,1},{6,2},{7,3},{8,4},{9,5},{10,6},{11,7},{12,8},{13,9},{1... | collective-permute-start | bytes 6152 | tf_op jit(solution)/shard_map/ppermute | solution.py:223
  102.2 8.1 %collective-permute-start.16 = (f32[1,512]{1,0:T(1,128)S(1)}, f32[1,512]{1,0:T(1,128)S(1)}, u32[]{:S(2)}, u32[]{:S(2)}) collective-permute-start(f32[1,512]{1,0:T(1,128)S(1)} %get-tuple-element.23), channel_id=1, source_target_pairs={{18,0},{19,1},{16,2},{17,3},{22,4},{23,5},{20,6},{21,7},{26,8},{27... | collective-permute-start | bytes 6152 | tf_op jit(solution)/shard_map/ppermute | solution.py:223
  107.1 5.4 %collective-permute-start.17 = (f32[1,512]{1,0:T(1,128)S(1)}, f32[1,512]{1,0:T(1,128)S(1)}, u32[]{:S(2)}, u32[]{:S(2)}) collective-permute-start(f32[1,512]{1,0:T(1,128)S(1)} %get-tuple-element.24), channel_id=1, source_target_pairs={{21,0},{22,1},{23,2},{20,3},{25,4},{26,5},{27,6},{24,7},{29,8},{30... | collective-permute-start | bytes 6152 | tf_op jit(solution)/shard_map/ppermute | solution.py:223
  107.6 6.0 %collective-permute-start.18 = (f32[1,512]{1,0:T(1,128)S(1)}, f32[1,512]{1,0:T(1,128)S(1)}, u32[]{:S(2)}, u32[]{:S(2)}) collective-permute-start(f32[1,512]{1,0:T(1,128)S(1)} %get-tuple-element.25), channel_id=1, source_target_pairs={{6,0},{7,1},{4,2},{5,3},{10,4},{11,5},{8,6},{9,7},{14,8},{15,9},{1... | collective-permute-start | bytes 6152 | tf_op jit(solution)/shard_map/ppermute | solution.py:223
  109.1 7.2 %collective-permute-start.19 = (f32[1,512]{1,0:T(1,128)S(1)}, f32[1,512]{1,0:T(1,128)S(1)}, u32[]{:S(2)}, u32[]{:S(2)}) collective-permute-start(f32[1,512]{1,0:T(1,128)S(1)} %get-tuple-element.26), channel_id=1, source_target_pairs={{44,0},{45,1},{46,2},{47,3},{32,4},{33,5},{34,6},{35,7},{36,8},{37... | collective-permute-start | bytes 6152 | tf_op jit(solution)/shard_map/ppermute | solution.py:223

commit v2 on v1

v2 whole, which is shorter than its diff:
```python
import functools

import jax
import jax.numpy as jnp
import numpy as np
from jax import lax
from jax.experimental import pallas as pl
from jax.experimental.pallas import tpu as pltpu
from jax.sharding import PartitionSpec as P

EPS = 1e-06
SIDE = 4
UNROLL = 8
FLAG_ROWS = 16
DEAD = -4.0
NORM_PARTS = 4

PLAN = [
    ((0, 1, 0), (0, 0, 0)),
    ((3, 0, 1), (0, 0, 0)),
    ((1, 0, 0), (0, 0, 0)),
    ((0, 3, 3), (0, 0, 0)),
    ((1, 1, 0), (0, 1, 0)),
    ((0, 3, 0), (0, 0, 0)),
    ((3, 0, 2), (3, 0, 1)),
    ((0, 3, 2), (0, 3, 3)),
    ((3, 3, 3), (0, 3, 3)),
    ((2, 1, 0), (1, 1, 0)),
]
OFFSETS = [(0, 0, 0)] + [d for d, _ in PLAN]
STAGES = [4, 6, 8, 10]


def turned(d):
    return (d[1], d[0], -d[2])


def place_of(v):
    return ((v[0] % SIDE) * SIDE + v[1] % SIDE) * SIDE + v[2] % SIDE


def cube():
    return [(z, y, x) for z in range(SIDE) for y in range(SIDE) for x in range(SIDE)]


def add(a, b):
    return tuple(x + y for x, y in zip(a, b))


def sub(a, b):
    return tuple((x - y) % SIDE for x, y in zip(a, b))


def moves(step):
    pairs = []
    for c in range(2):
        s = turned(step) if c else step
        for v in cube():
            pairs.append((c * SIDE**3 + place_of(add(v, s)), c * SIDE**3 + place_of(v)))
    return pairs


def choose_pairs():
    best = {}
    for a in range(len(OFFSETS)):
        for b in range(a):
            g = sub(OFFSETS[a], OFFSETS[b])
            key = min(g, sub((0, 0, 0), g))
            if key not in best:
                best[key] = (a, b)
    assert len(best) == (SIDE**3 - 1 + 7) // 2
    return sorted(best.values())


def work_table():
    stages = [[] for _ in STAGES]
    for a, b in choose_pairs():
        stage = next(i for i, n in enumerate(STAGES) if a <= n)
        twin = all((2 * g) % SIDE == 0 for g in sub(OFFSETS[a], OFFSETS[b]))
        stages[stage].extend([(a, b, -1)] if twin else [(a, b, 0), (a, b, 1)])
    loops = []
    for s in stages:
        steps = -(-len(s) // UNROLL)
        unroll = -(-len(s) // steps)
        loops.append((steps, unroll))
        s.extend([s[-1]] * (steps * unroll - len(s)))
    units = [u for s in stages for u in s]
    table = np.zeros((2, SIDE**3, len(OFFSETS) + len(units) * 3), np.int32)
    for c in range(2):
        offs = [turned(d) if c else d for d in OFFSETS]
        for v in cube():
            table[c, place_of(v), : len(OFFSETS)] = [place_of(add(v, d)) for d in offs]
            for n, (a, b, half) in enumerate(units):
                first = place_of(add(v, offs[a])) < place_of(add(v, offs[b]))
                k, q = (a, b) if first else (b, a)
                h = half if half >= 0 else int(first)
                at = len(OFFSETS) + 3 * n
                table[c, place_of(v), at : at + 3] = (k, q, h)
    return table, loops


def unit_kernel(alive, x_hbm, mask_hbm, out_ref, x_ref, mask_ref, sems):
    rows, width = x_ref.shape
    part = rows // NORM_PARTS
    copies = []
    for i in range(NORM_PARTS):
        at = pl.ds(i * part, part)
        copies.append(pltpu.make_async_copy(x_hbm.at[at], x_ref.at[at], sems.at[i]))
        copies[-1].start()
    copies.append(pltpu.make_async_copy(mask_hbm, mask_ref, sems.at[NORM_PARTS]))
    copies[-1].start()
    copies[-1].wait()
    live = (mask_ref[...] == 1) & (alive[0] == 1)
    bias = jnp.broadcast_to(jnp.where(live, 0.0, DEAD), (FLAG_ROWS, rows))
    top = lax.broadcasted_iota(jnp.int32, (FLAG_ROWS, rows), 0) == 0
    out_ref[rows:, :] = jnp.zeros((FLAG_ROWS, width), jnp.bfloat16)
    out_ref[rows:, :rows] = jnp.where(top, bias, 0.0).astype(jnp.bfloat16)
    for i in range(NORM_PARTS):
        copies[i].wait()
        at = slice(i * part, (i + 1) * part)
        x = x_ref[at, :].astype(jnp.float32)
        meansq = jnp.mean(x * x, axis=-1, keepdims=True)
        out_ref[at, :] = (x * lax.rsqrt(meansq + EPS) * (1.0 / width**0.5)).astype(jnp.bfloat16)


def dot_t(a, b):
    return lax.dot_general(a, b, (((1,), (1,)), ((), ())), preferred_element_type=jnp.float32)


def key_bias(flags):
    ones = jnp.ones((flags.shape[0], 128), jnp.bfloat16)
    return lax.dot_general(flags, ones, (((0,), (0,)), ((), ())), preferred_element_type=jnp.float32)


def fold_rows(s):
    n, w = s.shape
    return jnp.max(s.reshape(n // 8, 8, w), axis=0)


def unit_work(tab, at, stack, biases, acc):
    half = stack.shape[1] // 2
    k, q, h = tab[at], tab[at + 1], tab[at + 2]
    s = dot_t(stack[k], stack[q, pl.ds(pl.multiple_of(h * half, half), half), :])
    s = s + jnp.tile(biases[k], (1, half // 128))
    acc[q, h] = jnp.maximum(acc[q, h], fold_rows(s))


def self_kernel(t_ref, tab, stack, biases, acc, turn):
    rows = stack.shape[1]
    half = rows // 2
    stack[0] = t_ref[:rows, :]
    biases[0] = key_bias(t_ref[rows:, :rows])
    acc[...] = jnp.full(acc.shape, -1.0, jnp.float32)
    for h in range(2):
        n = half * (h + 1)
        s = dot_t(t_ref[:n, :], t_ref[h * half : (h + 1) * half, :])
        key = lax.broadcasted_iota(jnp.int32, (n, half), 0)
        query = lax.broadcasted_iota(jnp.int32, (n, half), 1) + h * half
        s = jnp.where(key < query, s + jnp.tile(biases[0, :n], (1, half // 128)), -1.0)
        acc[0, h] = jnp.maximum(acc[0, h], fold_rows(s))
    turn[...] = jnp.full(turn.shape, tab[0], jnp.int32)


def pair_kernel(tab, turn, *refs, new, start, steps, unroll, last):
    n = len(new)
    tiles = refs[:n]
    n_out = int(last)
    stack, biases, acc = refs[n + 3 : n + 6]
    outs = refs[n + 6 : n + 6 + n_out]
    sems = refs[n + 6 + n_out]
    rows = stack.shape[1]
    half = rows // 2
    copies = []
    for i, slot in enumerate(new):
        copies.append(pltpu.make_async_copy(tiles[i].at[pl.ds(0, rows)], stack.at[slot], sems.at[i]))
    for c in copies:
        c.start()
    for i, slot in enumerate(new):
        biases[slot] = key_bias(tiles[i][rows:, :rows])
    for c in copies:
        c.wait()

    def step(u, carry):
        for j in range(unroll):
            unit_work(tab, len(OFFSETS) + 3 * (start + u * unroll + j), stack, biases, acc)
        return carry

    lax.fori_loop(0, steps, step, 0)
    if last:
        outs[0][...] = jnp.full(outs[0].shape, -1.0, jnp.float32)
        for s in range(acc.shape[0]):
            for h in range(2):
                outs[0][pl.ds(tab[s], 1), h * half : (h + 1) * half] = jnp.max(acc[s, h], axis=0, keepdims=True)


def on_device(embeddings, row_mask, tile_counts):
    rows, width = embeddings.shape[2:]
    half = rows // 2
    clus, place = lax.axis_index("clus"), lax.axis_index("help")
    table, loops = work_table()
    tab = jnp.asarray(table)[clus, place]
    alive = (place < tile_counts).astype(jnp.int32)
    slots = len(OFFSETS)
    vmem, smem, hbm = (pl.BlockSpec(memory_space=m) for m in (pltpu.VMEM, pltpu.SMEM, pltpu.HBM))
    state = [
        pltpu.VMEM((slots, rows, width), jnp.bfloat16),
        pltpu.VMEM((slots, rows, 128), jnp.float32),
        pltpu.VMEM((slots, 2, 8, half), jnp.float32),
    ]

    own = pl.pallas_call(
        unit_kernel,
        out_shape=pltpu.VMEM((rows + FLAG_ROWS, width), jnp.bfloat16),
        in_specs=[smem, hbm, hbm],
        out_specs=vmem,
        scratch_shapes=[
            pltpu.VMEM((rows, width), jnp.bfloat16),
            pltpu.VMEM((1, rows), jnp.int32),
            pltpu.SemaphoreType.DMA((NORM_PARTS + 1,)),
        ],
        compiler_params=pltpu.CompilerParams(vmem_limit_bytes=24 * 2**20),
    )(alive, embeddings[0, 0], row_mask[0])
    *held_state, turn = pl.pallas_call(
        self_kernel,
        out_shape=state + [jax.ShapeDtypeStruct((8, 128), jnp.int32)],
        in_specs=[vmem, smem],
        out_specs=[vmem] * 4,
        compiler_params=pltpu.CompilerParams(vmem_limit_bytes=24 * 2**20),
        cost_estimate=pl.CostEstimate(flops=1000, bytes_accessed=1000, transcendentals=0),
    )(own, tab)
    held = {OFFSETS[0]: own}
    for d, source in PLAN:
        if source != OFFSETS[0] and source == PLAN[0][0]:
            held[source], turn = lax.optimization_barrier((held[source], turn))
        held[d] = lax.ppermute(held[source], ("clus", "help"), moves(sub(d, source)))

    start, arrived = 0, 0
    for i, (steps, unroll) in enumerate(loops):
        new = list(range(arrived + 1, STAGES[i] + 1))
        last = i == len(loops) - 1
        outs = [jax.ShapeDtypeStruct((SIDE**3, rows), jnp.float32)] * int(last)
        results = pl.pallas_call(
            functools.partial(pair_kernel, new=new, start=start, steps=steps, unroll=unroll, last=last),
            out_shape=state + outs,
            in_specs=[smem] + [vmem] * (len(new) + 4),
            out_specs=[vmem] * (3 + len(outs)),
            input_output_aliases={2 + len(new) + j: j for j in range(3)},
            scratch_shapes=[pltpu.SemaphoreType.DMA((len(new),))],
            compiler_params=pltpu.CompilerParams(vmem_limit_bytes=24 * 2**20),
            cost_estimate=pl.CostEstimate(
                flops=1000, bytes_accessed=1000, transcendentals=0
            ),
        )(tab, turn, *[held[OFFSETS[s]] for s in new], *held_state)
        held_state, finals = results[:3], results[3:]
        start += steps * unroll
        arrived = STAGES[i]
    parts = lax.all_to_all(finals[0], "help", 0, 0, tiled=True)
    return jnp.max(parts, axis=0)[None, None]


def solution(mesh):
    in_specs = (P("clus", "help", None, None), P("clus", "help", None), P("clus"))
    out_specs = P("clus", "help", None)
    return jax.shard_map(on_device, mesh=mesh, in_specs=in_specs, out_specs=out_specs, check_vma=False)
```

time: 117 us -> 95.6 us (0.82)
  Pallas kernels: 50.5 us -> 27.5 us
  blocking collectives: 0 us -> 19.7 us
  starting transfers between devices: 35.8 us -> 22.4 us
  waiting for transfers between devices: 27.6 us -> 21.5 us
    pallas_call x7 -> x6, Pallas kernels: 50.5 us -> 27.5 us  [the longest x4 25.5 us: on_device(): pl.pallas_call(functools.partial(pair_kernel, new=new, start=start, steps...]
    all_to_all x0 -> x1, blocking collectives: none -> 19.7 us  [on_device(): parts = lax.all_to_all(finals[0], 'help', 0, 0, tiled=True)]
    ppermute x10 -> x0, starting transfers between devices: 18.3 us -> none  [on_device(): lax.ppermute(acc[s], ('clus', 'help'), moves(sub((0, 0, 0), OFFSETS[s])))]
    ppermute x10 -> x0, waiting for transfers between devices: 6 us -> none  [on_device(): lax.ppermute(acc[s], ('clus', 'help'), moves(sub((0, 0, 0), OFFSETS[s])))]
    ppermute x10, starting transfers between devices: 17.4 us -> 22.4 us  [on_device(): lax.ppermute(held[source], ('clus', 'help'), moves(sub(d, source)))]
  transfers between devices with their start and end apart: 20 -> 10, of which waited for: 6 -> 4; matrix products, arithmetic and copies ran while one was open for 1% -> 1% of each run, Pallas kernels for 34% -> 22%
where the time goes in v2:
time: 95.6 us; the launch traced here: 95.4 us
  Pallas kernels  27.5 us (29%)
  starting transfers between devices  22.4 us (23%)
  waiting for transfers between devices  21.5 us (22%)
  blocking collectives  19.7 us (21%)
  local copies, waits for them, and re-layouts  2.74 us (3%)
    pallas_call x4, Pallas kernels, on_device(): pl.pallas_call(functools.partial(pair_kernel, new=new, start=start, steps...  25.5 us
    ppermute x10, starting transfers between devices, on_device(): lax.ppermute(held[source], ('clus', 'help'), moves(sub(d, source)))  22.4 us
    ppermute x10, waiting for transfers between devices, on_device(): lax.ppermute(held[source], ('clus', 'help'), moves(sub(d, source)))  21.5 us
    all_to_all x1, blocking collectives, on_device(): parts = lax.all_to_all(finals[0], 'help', 0, 0, tiled=True)  19.7 us
  transfers between devices with their start and end apart: 10, of which 4 were waited for; matrix products, arithmetic and copies ran while one was open for 1% of the time, Pallas kernels for 22%

profile of v2, /device:TPU:0, one launch (start us, length us, event | category | flops | bytes accessed | tf_op | source)
XLA Modules:
  0.0 95.4 jit_solution(14336999846966145321)
XLA Ops:
  0.7 0.0 copy-start
  0.7 1.2 %copy-done = bf16[1,1,512,1024]{3,2,1,0:T(8,128)(2,1)S(1)} copy-done((bf16[1,1,512,1024]{3,2,1,0:T(8,128)(2,1)S(1)}, bf16[1,1,512,1024]{3,2,1,0:T(8,128)(2,1)}, u32[]{:S(2)}) %copy-start) | copy-done | bytes 1048600
  1.9 0.0 copy-start.1
  1.9 0.7 copy-done.1
  2.6 0.8 shard_map.46.t_ref
  3.3 3.2 %collective-permute-start = (bf16[528,1024]{1,0:T(8,128)(2,1)S(1)}, bf16[528,1024]{1,0:T(8,128)(2,1)}, u32[]{:S(2)}, u32[]{:S(2)}) collective-permute-start(bf16[528,1024]{1,0:T(8,128)(2,1)S(1)} %shard_map.46.t_ref), channel_id=1, source_target_pairs={{4,0},{5,1},{6,2},{7,3},{8,4},{9,5},{10,6},{11,7},{12,8},{13,9},{1... | collective-permute-start | bytes 3244040 | tf_op jit(solution)/shard_map/ppermute | solution.py:235
  6.5 0.0 collective-permute-start.1
  6.5 4.1 %collective-permute-start.5 = (bf16[528,1024]{1,0:T(8,128)(2,1)S(1)}, bf16[528,1024]{1,0:T(8,128)(2,1)S(1)}, u32[]{:S(2)}, u32[]{:S(2)}) collective-permute-start(bf16[528,1024]{1,0:T(8,128)(2,1)S(1)} %shard_map.46.t_ref), channel_id=1, source_target_pairs={{49,0},{50,1},{51,2},{48,3},{53,4},{54,5},{55,6},{52,7},{57,8},{58... | collective-permute-start | bytes 3244040 | tf_op jit(solution)/shard_map/ppermute | solution.py:235
  10.6 1.3 %collective-permute-start.9 = (bf16[528,1024]{1,0:T(8,128)(2,1)S(1)}, bf16[528,1024]{1,0:T(8,128)(2,1)}, u32[]{:S(2)}, u32[]{:S(2)}) collective-permute-start(bf16[528,1024]{1,0:T(8,128)(2,1)S(1)} %shard_map.46.t_ref), channel_id=1, source_target_pairs={{16,0},{17,1},{18,2},{19,3},{20,4},{21,5},{22,6},{23,7},{24,8},{25... | collective-permute-start | bytes 3244040 | tf_op jit(solution)/shard_map/ppermute | solution.py:235
  11.9 0.7 constant_dynamic-slice_fusion
  12.6 1.2 %shard_map.47 = (bf16[11,512,1024]{2,1,0:T(8,128)(2,1)S(1)}, f32[11,512,128]{2,1,0:T(8,128)S(1)}, f32[11,2,8,256]{3,2,1,0:T(8,128)S(1)}, s32[8,128]{1,0:T(8,128)S(1)}) custom-call(bf16[528,1024]{1,0:T(8,128)(2,1)S(1)} %shard_map.46.t_ref, s32[212]{0:T(256)S(1)} %bitcast.8), custom_call_target="tpu_custom_call" | custom-call | flops 1000 | bytes 1000 | tf_op jit(solution)/shard_map/pallas_call | solution.py:223
  13.9 13.3 %collective-permute-done.refs_0_ = bf16[528,1024]{1,0:T(8,128)(2,1)} collective-permute-done((bf16[528,1024]{1,0:T(8,128)(2,1)S(1)}, bf16[528,1024]{1,0:T(8,128)(2,1)}, u32[]{:S(2)}, u32[]{:S(2)}) %collective-permute-start) | collective-permute-done | bytes 1081376 | tf_op jit(solution)/shard_map/ppermute | solution.py:235
  27.2 3.8 %collective-permute-start.3 = (bf16[528,1024]{1,0:T(8,128)(2,1)}, bf16[528,1024]{1,0:T(8,128)(2,1)S(1)}, u32[]{:S(2)}, u32[]{:S(2)}) collective-permute-start(bf16[528,1024]{1,0:T(8,128)(2,1)} %collective-permute-done.refs_0_), channel_id=1, source_target_pairs={{16,0},{17,1},{18,2},{19,3},{20,4},{21,5},{22,6},{23,7},{24,8},{25... | collective-permute-start | bytes 3244040 | tf_op jit(solution)/shard_map/ppermute | solution.py:235
  31.0 1.1 %collective-permute-start.8 = (bf16[528,1024]{1,0:T(8,128)(2,1)S(1)}, bf16[528,1024]{1,0:T(8,128)(2,1)S(1)}, u32[]{:S(2)}, u32[]{:S(2)}) collective-permute-start(bf16[528,1024]{1,0:T(8,128)(2,1)S(1)} %shard_map.46.t_ref), channel_id=1, source_target_pairs={{12,0},{13,1},{14,2},{15,3},{0,4},{1,5},{2,6},{3,7},{4,8},{5,9},{6... | collective-permute-start | bytes 3244040 | tf_op jit(solution)/shard_map/ppermute | solution.py:235
  32.1 4.2 %collective-permute-done.1.refs_3_ = bf16[528,1024]{1,0:T(8,128)(2,1)S(1)} collective-permute-done((bf16[528,1024]{1,0:T(8,128)(2,1)S(1)}, bf16[528,1024]{1,0:T(8,128)(2,1)S(1)}, u32[]{:S(2)}, u32[]{:S(2)}) %collective-permute-start.1) | collective-permute-done | bytes 1081376 | tf_op jit(solution)/shard_map/ppermute | solution.py:235
  36.3 0.1 collective-permute-start.7
  36.4 0.0 collective-permute-done.5.refs_1_
  36.4 3.1 %collective-permute-start.6 = (bf16[528,1024]{1,0:T(8,128)(2,1)S(1)}, bf16[528,1024]{1,0:T(8,128)(2,1)S(1)}, u32[]{:S(2)}, u32[]{:S(2)}) collective-permute-start(bf16[528,1024]{1,0:T(8,128)(2,1)S(1)} %collective-permute-done.5.refs_1_), channel_id=1, source_target_pairs={{1,0},{2,1},{3,2},{0,3},{5,4},{6,5},{7,6},{4,7},{9,8},{10,9},{11,1... | collective-permute-start | bytes 3244040 | tf_op jit(solution)/shard_map/ppermute | solution.py:235
  39.6 0.0 collective-permute-done.9.refs_2_
  39.6 2.0 %collective-permute-start.2 = (bf16[528,1024]{1,0:T(8,128)(2,1)S(1)}, bf16[528,1024]{1,0:T(8,128)(2,1)S(1)}, u32[]{:S(2)}, u32[]{:S(2)}) collective-permute-start(bf16[528,1024]{1,0:T(8,128)(2,1)S(1)} %collective-permute-done.1.refs_3_), channel_id=1, source_target_pairs={{48,0},{49,1},{50,2},{51,3},{52,4},{53,5},{54,6},{55,7},{56,8},{57... | collective-permute-start | bytes 3244040 | tf_op jit(solution)/shard_map/ppermute | solution.py:235
  41.6 2.4 %collective-permute-done.3.refs_0_ = bf16[528,1024]{1,0:T(8,128)(2,1)S(1)} collective-permute-done((bf16[528,1024]{1,0:T(8,128)(2,1)}, bf16[528,1024]{1,0:T(8,128)(2,1)S(1)}, u32[]{:S(2)}, u32[]{:S(2)}) %collective-permute-start.3) | collective-permute-done | bytes 1081376 | tf_op jit(solution)/shard_map/ppermute | solution.py:235
  44.0 3.6 %collective-permute-start.4 = (bf16[528,1024]{1,0:T(8,128)(2,1)S(1)}, bf16[528,1024]{1,0:T(8,128)(2,1)S(1)}, u32[]{:S(2)}, u32[]{:S(2)}) collective-permute-start(bf16[528,1024]{1,0:T(8,128)(2,1)S(1)} %collective-permute-done.3.refs_0_), channel_id=1, source_target_pairs={{16,0},{17,1},{18,2},{19,3},{20,4},{21,5},{22,6},{23,7},{24,8},{25... | collective-permute-start | bytes 3244040 | tf_op jit(solution)/shard_map/ppermute | solution.py:235
  47.5 8.6 %shard_map.48 = (bf16[11,512,1024]{2,1,0:T(8,128)(2,1)S(1)}, f32[11,512,128]{2,1,0:T(8,128)S(1)}, f32[11,2,8,256]{3,2,1,0:T(8,128)S(1)}) custom-call(s32[212]{0:T(256)S(1)} %bitcast.9, s32[8,128]{1,0:T(8,128)S(1)} %get-tuple-element.22.turn, ...), custom_call_target="tpu_custom_call", output_to_operand_aliasing={{0}: (6, {}), {1}: (7, {}), {2}: (8, {})} | custom-call | flops 1000 | bytes 1000 | tf_op jit(solution)/shard_map/pallas_call | solution.py:242
  56.2 0.0 collective-permute-done.8.refs_1_
  56.2 5.2 %shard_map.49 = (bf16[11,512,1024]{2,1,0:T(8,128)(2,1)S(1)}, f32[11,512,128]{2,1,0:T(8,128)S(1)}, f32[11,2,8,256]{3,2,1,0:T(8,128)S(1)}) custom-call(s32[212]{0:T(256)S(1)} %bitcast.10, s32[8,128]{1,0:T(8,128)S(1)} %get-tuple-element.22.turn, ...), custom_call_target="tpu_custom_call", output_to_operand_aliasing={{0}: (4, {}), {1}: (5, {}), {2}: (6, {})} | custom-call | flops 1000 | bytes 1000 | tf_op jit(solution)/shard_map/pallas_call | solution.py:242
  61.4 1.6 %collective-permute-done.7.refs_1_ = bf16[528,1024]{1,0:T(8,128)(2,1)S(1)} collective-permute-done((bf16[528,1024]{1,0:T(8,128)(2,1)S(1)}, bf16[528,1024]{1,0:T(8,128)(2,1)S(1)}, u32[]{:S(2)}, u32[]{:S(2)}) %collective-permute-start.7) | collective-permute-done | bytes 1081376 | tf_op jit(solution)/shard_map/ppermute | solution.py:235
  63.1 0.0 collective-permute-done.6.refs_0_
  63.1 5.8 %shard_map.50 = (bf16[11,512,1024]{2,1,0:T(8,128)(2,1)S(1)}, f32[11,512,128]{2,1,0:T(8,128)S(1)}, f32[11,2,8,256]{3,2,1,0:T(8,128)S(1)}) custom-call(s32[212]{0:T(256)S(1)} %bitcast.11, s32[8,128]{1,0:T(8,128)S(1)} %get-tuple-element.22.turn, ...), custom_call_target="tpu_custom_call", output_to_operand_aliasing={{0}: (4, {}), {1}: (5, {}), {2}: (6, {})} | custom-call | flops 1000 | bytes 1000 | tf_op jit(solution)/shard_map/pallas_call | solution.py:242
  68.9 0.0 collective-permute-done.2.refs_0_
  68.9 0.0 collective-permute-done.4.refs_1_
  68.9 5.9 %shard_map.51 = (bf16[11,512,1024]{2,1,0:T(8,128)(2,1)S(1)}, f32[11,512,128]{2,1,0:T(8,128)S(1)}, f32[11,2,8,256]{3,2,1,0:T(8,128)S(1)}, f32[64,512]{1,0:T(8,128)S(1)}) custom-call(s32[212]{0:T(256)S(1)} %bitcast.12, s32[8,128]{1,0:T(8,128)S(1)} %get-tuple-element.22.turn, ...), custom_call_target="tpu_custom_call", output_to_operand_aliasing={{0}: (4, {}), {1}: (5, {}), {2}: (6, {})} | custom-call | flops 1000 | bytes 1000 | tf_op jit(solution)/shard_map/pallas_call | solution.py:242
  74.8 0.1 copy.17
  74.9 19.7 %all_to_all.9 = f32[64,1,512]{2,1,0:T(1,128)S(1)} all-to-all(f32[64,1,512]{2,1,0:T(1,128)S(1)} %copy.17), channel_id=1, replica_groups=mesh['clus'=2,'help'=64] {'help'}, dimensions={0} | all-to-all | bytes 262144 | tf_op jit(solution)/shard_map/all_to_all | solution.py:257
  94.7 0.7 reduce_max.9
Async XLA Ops:
  0.7 1.2 %copy-start = (bf16[1,1,512,1024]{3,2,1,0:T(8,128)(2,1)S(1)}, bf16[1,1,512,1024]{3,2,1,0:T(8,128)(2,1)}, u32[]{:S(2)}) copy-start(bf16[1,1,512,1024]{3,2,1,0:T(8,128)(2,1)} %param.4) | copy-start | bytes 3145732
  1.9 0.7 copy-start.1
  3.3 23.9 %collective-permute-start = (bf16[528,1024]{1,0:T(8,128)(2,1)S(1)}, bf16[528,1024]{1,0:T(8,128)(2,1)}, u32[]{:S(2)}, u32[]{:S(2)}) collective-permute-start(bf16[528,1024]{1,0:T(8,128)(2,1)S(1)} %shard_map.46.t_ref), channel_id=1, source_target_pairs={{4,0},{5,1},{6,2},{7,3},{8,4},{9,5},{10,6},{11,7},{12,8},{13,9},{1... | collective-permute-start | bytes 3244040 | tf_op jit(solution)/shard_map/ppermute | solution.py:235
  6.5 29.8 %collective-permute-start.1 = (bf16[528,1024]{1,0:T(8,128)(2,1)S(1)}, bf16[528,1024]{1,0:T(8,128)(2,1)S(1)}, u32[]{:S(2)}, u32[]{:S(2)}) collective-permute-start(bf16[528,1024]{1,0:T(8,128)(2,1)S(1)} %shard_map.46.t_ref), channel_id=1, source_target_pairs={{15,0},{12,1},{13,2},{14,3},{3,4},{0,5},{1,6},{2,7},{7,8},{4,9},{5... | collective-permute-start | bytes 3244040 | tf_op jit(solution)/shard_map/ppermute | solution.py:235
  6.5 29.9 %collective-permute-start.5 = (bf16[528,1024]{1,0:T(8,128)(2,1)S(1)}, bf16[528,1024]{1,0:T(8,128)(2,1)S(1)}, u32[]{:S(2)}, u32[]{:S(2)}) collective-permute-start(bf16[528,1024]{1,0:T(8,128)(2,1)S(1)} %shard_map.46.t_ref), channel_id=1, source_target_pairs={{49,0},{50,1},{51,2},{48,3},{53,4},{54,5},{55,6},{52,7},{57,8},{58... | collective-permute-start | bytes 3244040 | tf_op jit(solution)/shard_map/ppermute | solution.py:235
  10.6 29.0 %collective-permute-start.9 = (bf16[528,1024]{1,0:T(8,128)(2,1)S(1)}, bf16[528,1024]{1,0:T(8,128)(2,1)}, u32[]{:S(2)}, u32[]{:S(2)}) collective-permute-start(bf16[528,1024]{1,0:T(8,128)(2,1)S(1)} %shard_map.46.t_ref), channel_id=1, source_target_pairs={{16,0},{17,1},{18,2},{19,3},{20,4},{21,5},{22,6},{23,7},{24,8},{25... | collective-permute-start | bytes 3244040 | tf_op jit(solution)/shard_map/ppermute | solution.py:235
  27.2 16.8 %collective-permute-start.3 = (bf16[528,1024]{1,0:T(8,128)(2,1)}, bf16[528,1024]{1,0:T(8,128)(2,1)S(1)}, u32[]{:S(2)}, u32[]{:S(2)}) collective-permute-start(bf16[528,1024]{1,0:T(8,128)(2,1)} %collective-permute-done.refs_0_), channel_id=1, source_target_pairs={{16,0},{17,1},{18,2},{19,3},{20,4},{21,5},{22,6},{23,7},{24,8},{25... | collective-permute-start | bytes 3244040 | tf_op jit(solution)/shard_map/ppermute | solution.py:235
  31.0 25.2 %collective-permute-start.8 = (bf16[528,1024]{1,0:T(8,128)(2,1)S(1)}, bf16[528,1024]{1,0:T(8,128)(2,1)S(1)}, u32[]{:S(2)}, u32[]{:S(2)}) collective-permute-start(bf16[528,1024]{1,0:T(8,128)(2,1)S(1)} %shard_map.46.t_ref), channel_id=1, source_target_pairs={{12,0},{13,1},{14,2},{15,3},{0,4},{1,5},{2,6},{3,7},{4,8},{5,9},{6... | collective-permute-start | bytes 3244040 | tf_op jit(solution)/shard_map/ppermute | solution.py:235
  36.3 26.8 %collective-permute-start.7 = (bf16[528,1024]{1,0:T(8,128)(2,1)S(1)}, bf16[528,1024]{1,0:T(8,128)(2,1)S(1)}, u32[]{:S(2)}, u32[]{:S(2)}) collective-permute-start(bf16[528,1024]{1,0:T(8,128)(2,1)S(1)} %collective-permute-done.1.refs_3_), channel_id=1, source_target_pairs={{3,0},{0,1},{1,2},{2,3},{7,4},{4,5},{5,6},{6,7},{11,8},{8,9},{9,10... | collective-permute-start | bytes 3244040 | tf_op jit(solution)/shard_map/ppermute | solution.py:235
  36.4 26.6 %collective-permute-start.6 = (bf16[528,1024]{1,0:T(8,128)(2,1)S(1)}, bf16[528,1024]{1,0:T(8,128)(2,1)S(1)}, u32[]{:S(2)}, u32[]{:S(2)}) collective-permute-start(bf16[528,1024]{1,0:T(8,128)(2,1)S(1)} %collective-permute-done.5.refs_1_), channel_id=1, source_target_pairs={{1,0},{2,1},{3,2},{0,3},{5,4},{6,5},{7,6},{4,7},{9,8},{10,9},{11,1... | collective-permute-start | bytes 3244040 | tf_op jit(solution)/shard_map/ppermute | solution.py:235
  39.6 29.3 %collective-permute-start.2 = (bf16[528,1024]{1,0:T(8,128)(2,1)S(1)}, bf16[528,1024]{1,0:T(8,128)(2,1)S(1)}, u32[]{:S(2)}, u32[]{:S(2)}) collective-permute-start(bf16[528,1024]{1,0:T(8,128)(2,1)S(1)} %collective-permute-done.1.refs_3_), channel_id=1, source_target_pairs={{48,0},{49,1},{50,2},{51,3},{52,4},{53,5},{54,6},{55,7},{56,8},{57... | collective-permute-start | bytes 3244040 | tf_op jit(solution)/shard_map/ppermute | solution.py:235
  44.0 24.9 %collective-permute-start.4 = (bf16[528,1024]{1,0:T(8,128)(2,1)S(1)}, bf16[528,1024]{1,0:T(8,128)(2,1)S(1)}, u32[]{:S(2)}, u32[]{:S(2)}) collective-permute-start(bf16[528,1024]{1,0:T(8,128)(2,1)S(1)} %collective-permute-done.3.refs_0_), channel_id=1, source_target_pairs={{16,0},{17,1},{18,2},{19,3},{20,4},{21,5},{22,6},{23,7},{24,8},{25... | collective-permute-start | bytes 3244040 | tf_op jit(solution)/shard_map/ppermute | solution.py:235

commit v3 on v2

--- a/solution.py
+++ b/solution.py
@@ -10,29 +10,31 @@
 
 EPS = 1e-06
 SIDE = 4
-UNROLL = 8
+UNROLL = 12
 FLAG_ROWS = 16
 DEAD = -4.0
 NORM_PARTS = 4
 
 PLAN = [
-    ((0, 1, 0), (0, 0, 0)),
-    ((3, 0, 1), (0, 0, 0)),
+    ((0, 0, 1), (0, 0, 0)),
+    ((3, 1, 0), (0, 0, 0)),
+    ((0, 3, 1), (0, 0, 1)),
     ((1, 0, 0), (0, 0, 0)),
-    ((0, 3, 3), (0, 0, 0)),
-    ((1, 1, 0), (0, 1, 0)),
-    ((0, 3, 0), (0, 0, 0)),
-    ((3, 0, 2), (3, 0, 1)),
-    ((0, 3, 2), (0, 3, 3)),
-    ((3, 3, 3), (0, 3, 3)),
-    ((2, 1, 0), (1, 1, 0)),
+    ((3, 0, 3), (0, 0, 0)),
+    ((3, 1, 3), (3, 1, 0)),
+    ((3, 1, 1), (3, 1, 0)),
+    ((1, 3, 1), (0, 3, 1)),
+    ((1, 1, 0), (1, 0, 0)),
+    ((3, 3, 3), (3, 0, 3)),
 ]
 OFFSETS = [(0, 0, 0)] + [d for d, _ in PLAN]
-STAGES = [4, 6, 8, 10]
+STAGES = [2, 5, 7, 9, 10]
+GATES = {(0, 3, 1): 0, (1, 3, 1): 1}
+AFTER = {(1, 0, 0): (0, 0, 1), (3, 0, 3): (0, 0, 1)}
 
 
 def turned(d):
-    return (d[1], d[0], -d[2])
+    return (-d[0], -d[2], -d[1])
 
 
 def place_of(v):
@@ -161,13 +163,14 @@
     turn[...] = jnp.full(turn.shape, tab[0], jnp.int32)
 
 
-def pair_kernel(tab, turn, *refs, new, start, steps, unroll, last):
+def pair_kernel(tab, turn_in, *refs, new, start, steps, unroll, last):
     n = len(new)
     tiles = refs[:n]
-    n_out = int(last)
+    n_out = 3 * last
     stack, biases, acc = refs[n + 3 : n + 6]
-    outs = refs[n + 6 : n + 6 + n_out]
-    sems = refs[n + 6 + n_out]
+    turn = refs[n + 6]
+    outs = refs[n + 7 : n + 7 + n_out]
+    sems = refs[n + 7 + n_out]
     rows = stack.shape[1]
     half = rows // 2
     copies = []
@@ -175,8 +178,13 @@
         copies.append(pltpu.make_async_copy(tiles[i].at[pl.ds(0, rows)], stack.at[slot], sems.at[i]))
     for c in copies:
         c.start()
+    flags = jnp.concatenate([t[rows:, :rows] for t in tiles], axis=0)
+    shape = (n * FLAG_ROWS, n * 128)
+    row, lane = (lax.broadcasted_iota(jnp.int32, shape, a) for a in range(2))
+    spread = (row == lane // 128 * FLAG_ROWS).astype(jnp.bfloat16)
+    columns = lax.dot_general(flags, spread, (((0,), (0,)), ((), ())), preferred_element_type=jnp.float32)
     for i, slot in enumerate(new):
-        biases[slot] = key_bias(tiles[i][rows:, :rows])
+        biases[slot] = columns[:, i * 128 : (i + 1) * 128]
     for c in copies:
         c.wait()
 
@@ -186,11 +194,16 @@
         return carry
 
     lax.fori_loop(0, steps, step, 0)
+    turn[...] = turn_in[...]
     if last:
-        outs[0][...] = jnp.full(outs[0].shape, -1.0, jnp.float32)
-        for s in range(acc.shape[0]):
+        for out in outs:
+            out[...] = jnp.full(out.shape, -1.0, jnp.float32)
+        for s, (z, y, x) in enumerate(OFFSETS):
+            row = 3 * (y % 3 + y // 3 * 2) + x % 3 + x // 3 * 2
             for h in range(2):
-                outs[0][pl.ds(tab[s], 1), h * half : (h + 1) * half] = jnp.max(acc[s, h], axis=0, keepdims=True)
+                outs[z % 3 + z // 3 * 2][row : row + 1, h * half : (h + 1) * half] = jnp.max(
+                    acc[s, h], axis=0, keepdims=True
+                )
 
 
 def on_device(embeddings, row_mask, tile_counts):
@@ -218,7 +231,7 @@
             pltpu.VMEM((1, rows), jnp.int32),
             pltpu.SemaphoreType.DMA((NORM_PARTS + 1,)),
         ],
-        compiler_params=pltpu.CompilerParams(vmem_limit_bytes=24 * 2**20),
+        compiler_params=pltpu.CompilerParams(vmem_limit_bytes=56 * 2**20),
     )(alive, embeddings[0, 0], row_mask[0])
     *held_state, turn = pl.pallas_call(
         self_kernel,
@@ -229,16 +242,23 @@
         cost_estimate=pl.CostEstimate(flops=1000, bytes_accessed=1000, transcendentals=0),
     )(own, tab)
     held = {OFFSETS[0]: own}
+    turns = [turn]
+    start, arrived = 0, 0
     for d, source in PLAN:
-        if source != OFFSETS[0] and source == PLAN[0][0]:
-            held[source], turn = lax.optimization_barrier((held[source], turn))
-        held[d] = lax.ppermute(held[source], ("clus", "help"), moves(sub(d, source)))
-
-    start, arrived = 0, 0
-    for i, (steps, unroll) in enumerate(loops):
+        if d in GATES:
+            held[source], turns[GATES[d]] = lax.optimization_barrier((held[source], turns[GATES[d]]))
+        sent = held[source]
+        if d in AFTER:
+            sent, held[AFTER[d]] = lax.optimization_barrier((sent, held[AFTER[d]]))
+        held[d] = lax.ppermute(sent, ("clus", "help"), moves(sub(d, source)))
+        i = len(turns) - 1
+        if len(held) - 1 < STAGES[i]:
+            continue
+        steps, unroll = loops[i]
         new = list(range(arrived + 1, STAGES[i] + 1))
         last = i == len(loops) - 1
-        outs = [jax.ShapeDtypeStruct((SIDE**3, rows), jnp.float32)] * int(last)
+        outs = [jax.ShapeDtypeStruct((8, 128), jnp.int32)]
+        outs += [jax.ShapeDtypeStruct((9, rows), jnp.float32)] * (3 * last)
         results = pl.pallas_call(
             functools.partial(pair_kernel, new=new, start=start, steps=steps, unroll=unroll, last=last),
             out_shape=state + outs,
@@ -247,15 +267,25 @@
             input_output_aliases={2 + len(new) + j: j for j in range(3)},
             scratch_shapes=[pltpu.SemaphoreType.DMA((len(new),))],
             compiler_params=pltpu.CompilerParams(vmem_limit_bytes=24 * 2**20),
-            cost_estimate=pl.CostEstimate(
-                flops=1000, bytes_accessed=1000, transcendentals=0
-            ),
-        )(tab, turn, *[held[OFFSETS[s]] for s in new], *held_state)
-        held_state, finals = results[:3], results[3:]
+            cost_estimate=pl.CostEstimate(flops=1000, bytes_accessed=1000, transcendentals=0),
+        )(tab, turns[i], *[held[OFFSETS[s]] for s in new], *held_state)
+        held_state, finals = results[:3], results[4:]
+        turns.append(results[3])
         start += steps * unroll
         arrived = STAGES[i]
-    parts = lax.all_to_all(finals[0], "help", 0, 0, tiled=True)
-    return jnp.max(parts, axis=0)[None, None]
+    own_part, ahead, behind = finals
+    for axis in range(3):
+        step = [0, 0, 0]
+        step[axis] = 1
+        back = [0, 0, 0]
+        back[axis] = 3
+        ahead = lax.ppermute(ahead, ("clus", "help"), moves(back))
+        behind = lax.ppermute(behind, ("clus", "help"), moves(step))
+        merged = jnp.maximum(own_part, jnp.maximum(ahead, behind))
+        n = merged.shape[0] // 3
+        if axis < 2:
+            own_part, ahead, behind = merged[:n], merged[n : 2 * n], merged[2 * n :]
+    return merged[None]
 
 
 def solution(mesh):

time: 95.6 us -> 91.3 us (0.955); the launches traced: 95.4 us -> 90 us
  blocking collectives: 19.7 us -> 0 us
  starting transfers between devices: 22.4 us -> 37.4 us
  local copies, waits for them, and re-layouts: 2.74 us -> 0.71 us
  waiting for transfers between devices: 21.5 us -> 22.6 us
    all_to_all x1 -> x0, blocking collectives: 19.7 us -> none  [on_device(): parts = lax.all_to_all(finals[0], 'help', 0, 0, tiled=True)]
    ppermute x10 -> x16, starting transfers between devices: 22.4 us -> 37.4 us  [the longest x10 25 us: on_device(): held[d] = lax.ppermute(sent, ('clus', 'help'), moves(sub(d, source)))]
    unnamed x4 -> x0, local copies, waits for them, and re-layouts: 1.9 us -> none
    ppermute x10 -> x16, waiting for transfers between devices: 21.5 us -> 22.6 us  [the longest x10 17.7 us: on_device(): held[d] = lax.ppermute(sent, ('clus', 'help'), moves(sub(d, source)))]
    pallas_call x4 -> x5, Pallas kernels: 25.5 us -> 25 us  [on_device(): pl.pallas_call(functools.partial(pair_kernel, new=new, start=start, steps...]
  transfers between devices with their start and end apart: 10 -> 16, of which waited for: 4 -> 6; matrix products, arithmetic and copies ran while one was open for 1% -> 1% of each run, Pallas kernels for 22% -> 25%
where the time goes in v3:
time: 91.3 us; the launch traced here: 90 us
  starting transfers between devices  37.4 us (41%)
  Pallas kernels  27.9 us (31%)
  waiting for transfers between devices  22.6 us (25%)
    ppermute x10, starting transfers between devices, on_device(): held[d] = lax.ppermute(sent, ('clus', 'help'), moves(sub(d, source)))  25 us
    pallas_call x5, Pallas kernels, on_device(): pl.pallas_call(functools.partial(pair_kernel, new=new, start=start, steps...  25 us
    ppermute x10, waiting for transfers between devices, on_device(): held[d] = lax.ppermute(sent, ('clus', 'help'), moves(sub(d, source)))  17.7 us
    ppermute x3, starting transfers between devices, on_device(): behind = lax.ppermute(behind, ('clus', 'help'), moves(step))  9.31 us
    ppermute x3, waiting for transfers between devices, on_device(): ahead = lax.ppermute(ahead, ('clus', 'help'), moves(back))  4.92 us
    ppermute x3, starting transfers between devices, on_device(): ahead = lax.ppermute(ahead, ('clus', 'help'), moves(back))  3.04 us
  transfers between devices with their start and end apart: 16, of which 6 were waited for; matrix products, arithmetic and copies ran while one was open for 1% of the time, Pallas kernels for 25%

profile of v3, /device:TPU:0, one launch (start us, length us, event | category | flops | bytes accessed | tf_op | source)
XLA Modules:
  0.0 90.0 jit_solution(11257879830840898105)
XLA Ops:
  0.7 1.7 %shard_map.46.t_ref = bf16[528,1024]{1,0:T(8,128)(2,1)S(1)} custom-call(s32[1]{0:T(128)S(6)} %convert_element_type.3.alive, bf16[512,1024]{1,0:T(8,128)(2,1)} %bitcast.12, s32[1,512]{1,0:T(1,128)} %bitcast.13), custom_call_target="tpu_custom_call" | custom-call | tf_op jit(solution)/shard_map/pallas_call | solution.py:224
  2.3 2.9 %collective-permute-start = (bf16[528,1024]{1,0:T(8,128)(2,1)S(1)}, bf16[528,1024]{1,0:T(8,128)(2,1)S(1)}, u32[]{:S(2)}, u32[]{:S(2)}) collective-permute-start(bf16[528,1024]{1,0:T(8,128)(2,1)S(1)} %shard_map.46.t_ref), channel_id=1, source_target_pairs={{1,0},{2,1},{3,2},{0,3},{5,4},{6,5},{7,6},{4,7},{9,8},{10,9},{11,1... | collective-permute-start | bytes 3244040 | tf_op jit(solution)/shard_map/ppermute | solution.py:253
  5.2 4.4 %collective-permute-start.1 = (bf16[528,1024]{1,0:T(8,128)(2,1)S(1)}, bf16[528,1024]{1,0:T(8,128)(2,1)S(1)}, u32[]{:S(2)}, u32[]{:S(2)}) collective-permute-start(bf16[528,1024]{1,0:T(8,128)(2,1)S(1)} %shard_map.46.t_ref), channel_id=1, source_target_pairs={{52,0},{53,1},{54,2},{55,3},{56,4},{57,5},{58,6},{59,7},{60,8},{61... | collective-permute-start | bytes 3244040 | tf_op jit(solution)/shard_map/ppermute | solution.py:253
  9.6 0.7 constant_dynamic-slice_fusion
  10.3 1.2 %shard_map.47 = (bf16[11,512,1024]{2,1,0:T(8,128)(2,1)S(1)}, f32[11,512,128]{2,1,0:T(8,128)S(1)}, f32[11,2,8,256]{3,2,1,0:T(8,128)S(1)}, s32[8,128]{1,0:T(8,128)S(1)}) custom-call(bf16[528,1024]{1,0:T(8,128)(2,1)S(1)} %shard_map.46.t_ref, s32[206]{0:T(256)S(1)} %bitcast.6), custom_call_target="tpu_custom_call" | custom-call | flops 1000 | bytes 1000 | tf_op jit(solution)/shard_map/pallas_call | solution.py:236
  11.6 6.4 %collective-permute-done.refs_0_ = bf16[528,1024]{1,0:T(8,128)(2,1)S(1)} collective-permute-done((bf16[528,1024]{1,0:T(8,128)(2,1)S(1)}, bf16[528,1024]{1,0:T(8,128)(2,1)S(1)}, u32[]{:S(2)}, u32[]{:S(2)}) %collective-permute-start) | collective-permute-done | bytes 1081376 | tf_op jit(solution)/shard_map/ppermute | solution.py:253
  17.9 1.6 %collective-permute-start.2 = (bf16[528,1024]{1,0:T(8,128)(2,1)S(1)}, bf16[528,1024]{1,0:T(8,128)(2,1)S(1)}, u32[]{:S(2)}, u32[]{:S(2)}) collective-permute-start(bf16[528,1024]{1,0:T(8,128)(2,1)S(1)} %collective-permute-done.refs_0_), channel_id=1, source_target_pairs={{12,0},{13,1},{14,2},{15,3},{0,4},{1,5},{2,6},{3,7},{4,8},{5,9},{6... | collective-permute-start | bytes 3244040 | tf_op jit(solution)/shard_map/ppermute | solution.py:253
  19.5 4.0 %collective-permute-start.3 = (bf16[528,1024]{1,0:T(8,128)(2,1)S(1)}, bf16[528,1024]{1,0:T(8,128)(2,1)S(1)}, u32[]{:S(2)}, u32[]{:S(2)}) collective-permute-start(bf16[528,1024]{1,0:T(8,128)(2,1)S(1)} %shard_map.46.t_ref), channel_id=1, source_target_pairs={{16,0},{17,1},{18,2},{19,3},{20,4},{21,5},{22,6},{23,7},{24,8},{25... | collective-permute-start | bytes 3244040 | tf_op jit(solution)/shard_map/ppermute | solution.py:253
  23.5 0.0 collective-permute-start.4
  23.5 0.0 collective-permute-done.1.refs_1_
  23.5 1.2 %collective-permute-start.5 = (bf16[528,1024]{1,0:T(8,128)(2,1)S(1)}, bf16[528,1024]{1,0:T(8,128)(2,1)S(1)}, u32[]{:S(2)}, u32[]{:S(2)}) collective-permute-start(bf16[528,1024]{1,0:T(8,128)(2,1)S(1)} %collective-permute-done.1.refs_1_), channel_id=1, source_target_pairs={{3,0},{0,1},{1,2},{2,3},{7,4},{4,5},{5,6},{6,7},{11,8},{8,9},{9,10... | collective-permute-start | bytes 3244040 | tf_op jit(solution)/shard_map/ppermute | solution.py:253
  24.8 2.6 %collective-permute-start.6 = (bf16[528,1024]{1,0:T(8,128)(2,1)S(1)}, bf16[528,1024]{1,0:T(8,128)(2,1)S(1)}, u32[]{:S(2)}, u32[]{:S(2)}) collective-permute-start(bf16[528,1024]{1,0:T(8,128)(2,1)S(1)} %collective-permute-done.1.refs_1_), channel_id=1, source_target_pairs={{1,0},{2,1},{3,2},{0,3},{5,4},{6,5},{7,6},{4,7},{9,8},{10,9},{11,1... | collective-permute-start | bytes 3244040 | tf_op jit(solution)/shard_map/ppermute | solution.py:253
  27.3 2.8 %shard_map.48 = (bf16[11,512,1024]{2,1,0:T(8,128)(2,1)S(1)}, f32[11,512,128]{2,1,0:T(8,128)S(1)}, f32[11,2,8,256]{3,2,1,0:T(8,128)S(1)}, s32[8,128]{1,0:T(8,128)S(1)}) custom-call(s32[206]{0:T(256)S(1)} %bitcast.7, s32[8,128]{1,0:T(8,128)S(1)} %get-tuple-element.31.turn_in, ...), custom_call_target="tpu_custom_call", output_to_operand_aliasing={{0}: (4, {}), {1}: (5, {}), {2}: (6, {})} | custom-call | flops 1000 | bytes 1000 | tf_op jit(solution)/shard_map/pallas_call | solution.py:262
  30.1 8.8 %collective-permute-done.2.refs_0_ = bf16[528,1024]{1,0:T(8,128)(2,1)S(1)} collective-permute-done((bf16[528,1024]{1,0:T(8,128)(2,1)S(1)}, bf16[528,1024]{1,0:T(8,128)(2,1)S(1)}, u32[]{:S(2)}, u32[]{:S(2)}) %collective-permute-start.2) | collective-permute-done | bytes 1081376 | tf_op jit(solution)/shard_map/ppermute | solution.py:253
  38.9 6.3 %collective-permute-start.7 = (bf16[528,1024]{1,0:T(8,128)(2,1)S(1)}, bf16[528,1024]{1,0:T(8,128)(2,1)S(1)}, u32[]{:S(2)}, u32[]{:S(2)}) collective-permute-start(bf16[528,1024]{1,0:T(8,128)(2,1)S(1)} %collective-permute-done.2.refs_0_), channel_id=1, source_target_pairs={{16,0},{17,1},{18,2},{19,3},{20,4},{21,5},{22,6},{23,7},{24,8},{25... | collective-permute-start | bytes 3244040 | tf_op jit(solution)/shard_map/ppermute | solution.py:253
  45.2 2.5 %collective-permute-done.3.refs_1_ = bf16[528,1024]{1,0:T(8,128)(2,1)S(1)} collective-permute-done((bf16[528,1024]{1,0:T(8,128)(2,1)S(1)}, bf16[528,1024]{1,0:T(8,128)(2,1)S(1)}, u32[]{:S(2)}, u32[]{:S(2)}) %collective-permute-start.3) | collective-permute-done | bytes 1081376 | tf_op jit(solution)/shard_map/ppermute | solution.py:253
  47.8 1.7 %collective-permute-start.8 = (bf16[528,1024]{1,0:T(8,128)(2,1)S(1)}, bf16[528,1024]{1,0:T(8,128)(2,1)S(1)}, u32[]{:S(2)}, u32[]{:S(2)}) collective-permute-start(bf16[528,1024]{1,0:T(8,128)(2,1)S(1)} %collective-permute-done.3.refs_1_), channel_id=1, source_target_pairs={{4,0},{5,1},{6,2},{7,3},{8,4},{9,5},{10,6},{11,7},{12,8},{13,9},{1... | collective-permute-start | bytes 3244040 | tf_op jit(solution)/shard_map/ppermute | solution.py:253
  49.4 0.0 collective-permute-done.4.refs_2_
  49.4 0.4 collective-permute-start.9
  49.8 8.1 %shard_map.49 = (bf16[11,512,1024]{2,1,0:T(8,128)(2,1)S(1)}, f32[11,512,128]{2,1,0:T(8,128)S(1)}, f32[11,2,8,256]{3,2,1,0:T(8,128)S(1)}, s32[8,128]{1,0:T(8,128)S(1)}) custom-call(s32[206]{0:T(256)S(1)} %bitcast.8, s32[8,128]{1,0:T(8,128)S(1)} %get-tuple-element.35.turn_in, ...), custom_call_target="tpu_custom_call", output_to_operand_aliasing={{0}: (5, {}), {1}: (6, {}), {2}: (7, {})} | custom-call | flops 1000 | bytes 1000 | tf_op jit(solution)/shard_map/pallas_call | solution.py:262
  58.0 0.0 collective-permute-done.5.refs_0_
  58.0 0.0 collective-permute-done.6.refs_1_
  58.0 5.2 %shard_map.50 = (bf16[11,512,1024]{2,1,0:T(8,128)(2,1)S(1)}, f32[11,512,128]{2,1,0:T(8,128)S(1)}, f32[11,2,8,256]{3,2,1,0:T(8,128)S(1)}, s32[8,128]{1,0:T(8,128)S(1)}) custom-call(s32[206]{0:T(256)S(1)} %bitcast.9, s32[8,128]{1,0:T(8,128)S(1)} %get-tuple-element.41.turn_in, ...), custom_call_target="tpu_custom_call", output_to_operand_aliasing={{0}: (4, {}), {1}: (5, {}), {2}: (6, {})} | custom-call | flops 1000 | bytes 1000 | tf_op jit(solution)/shard_map/pallas_call | solution.py:262
  63.2 0.0 collective-permute-done.7.refs_0_
  63.2 0.0 collective-permute-done.8.refs_1_
  63.2 5.2 %shard_map.51 = (bf16[11,512,1024]{2,1,0:T(8,128)(2,1)S(1)}, f32[11,512,128]{2,1,0:T(8,128)S(1)}, f32[11,2,8,256]{3,2,1,0:T(8,128)S(1)}, s32[8,128]{1,0:T(8,128)S(1)}) custom-call(s32[206]{0:T(256)S(1)} %bitcast.10, s32[8,128]{1,0:T(8,128)S(1)} %get-tuple-element.45.turn_in, ...), custom_call_target="tpu_custom_call", output_to_operand_aliasing={{0}: (4, {}), {1}: (5, {}), {2}: (6, {})} | custom-call | flops 1000 | bytes 1000 | tf_op jit(solution)/shard_map/pallas_call | solution.py:262
  68.5 0.0 collective-permute-done.9.refs_0_
  68.5 3.6 %shard_map.52 = (bf16[11,512,1024]{2,1,0:T(8,128)(2,1)S(1)}, f32[11,512,128]{2,1,0:T(8,128)S(1)}, f32[11,2,8,256]{3,2,1,0:T(8,128)S(1)}, s32[8,128]{1,0:T(8,128)...) custom-call(s32[206]{0:T(256)S(1)} %bitcast.11, ...), custom_call_target="tpu_custom_call", output_to_operand_aliasing={{0}: (3, {}), {1}: (4, {}), {2}: (5, {})} | custom-call | flops 1000 | bytes 1000 | tf_op jit(solution)/shard_map/pallas_call | solution.py:262
  72.1 0.4 collective-permute-start.10
  72.5 3.4 %collective-permute-start.11 = (f32[9,512]{1,0:T(8,128)S(1)}, f32[9,512]{1,0:T(8,128)S(1)}, u32[]{:S(2)}, u32[]{:S(2)}) collective-permute-start(f32[9,512]{1,0:T(8,128)S(1)} %get-tuple-element.56), channel_id=1, source_target_pairs={{16,0},{17,1},{18,2},{19,3},{20,4},{21,5},{22,6},{23,7},{24,8},{25... | collective-permute-start | bytes 55304 | tf_op jit(solution)/shard_map/ppermute | solution.py:283
  75.9 1.8 %collective-permute-done.10 = f32[9,512]{1,0:T(8,128)S(1)} collective-permute-done((f32[9,512]{1,0:T(8,128)S(1)}, f32[9,512]{1,0:T(8,128)S(1)}, u32[]{:S(2)}, u32[]{:S(2)}) %collective-permute-start.10) | collective-permute-done | bytes 18464 | tf_op jit(solution)/shard_map/ppermute | solution.py:282
  77.7 0.0 collective-permute-done.11
  77.8 1.2 %collective-permute-start.12 = (f32[3,512]{1,0:T(4,128)S(1)}, f32[3,512]{1,0:T(4,128)S(1)}, u32[]{:S(2)}, u32[]{:S(2)}) collective-permute-start(f32[3,512]{1,0:T(4,128)S(1)} %get-tuple-element.58), channel_id=1, source_target_pairs={{12,0},{13,1},{14,2},{15,3},{0,4},{1,5},{2,6},{3,7},{4,8},{5,9},{6... | collective-permute-start | bytes 18440 | tf_op jit(solution)/shard_map/ppermute | solution.py:282
  79.0 2.1 %collective-permute-start.13 = (f32[3,512]{1,0:T(4,128)S(1)}, f32[3,512]{1,0:T(4,128)S(1)}, u32[]{:S(2)}, u32[]{:S(2)}) collective-permute-start(f32[3,512]{1,0:T(4,128)S(1)} %get-tuple-element.57), channel_id=1, source_target_pairs={{4,0},{5,1},{6,2},{7,3},{8,4},{9,5},{10,6},{11,7},{12,8},{13,9},{1... | collective-permute-start | bytes 18440 | tf_op jit(solution)/shard_map/ppermute | solution.py:283
  81.1 1.6 %collective-permute-done.12 = f32[3,512]{1,0:T(4,128)S(1)} collective-permute-done((f32[3,512]{1,0:T(4,128)S(1)}, f32[3,512]{1,0:T(4,128)S(1)}, u32[]{:S(2)}, u32[]{:S(2)}) %collective-permute-start.12) | collective-permute-done | bytes 6176 | tf_op jit(solution)/shard_map/ppermute | solution.py:282
  82.7 0.0 collective-permute-done.13
  82.7 1.4 %collective-permute-start.14 = (f32[1,512]{1,0:T(1,128)S(1)}, f32[1,512]{1,0:T(1,128)S(1)}, u32[]{:S(2)}, u32[]{:S(2)}) collective-permute-start(f32[1,512]{1,0:T(1,128)S(1)} %get-tuple-element.60), channel_id=1, source_target_pairs={{3,0},{0,1},{1,2},{2,3},{7,4},{4,5},{5,6},{6,7},{11,8},{8,9},{9,10... | collective-permute-start | bytes 6152 | tf_op jit(solution)/shard_map/ppermute | solution.py:282
  84.1 3.8 %collective-permute-start.15 = (f32[1,512]{1,0:T(1,128)S(1)}, f32[1,512]{1,0:T(1,128)S(1)}, u32[]{:S(2)}, u32[]{:S(2)}) collective-permute-start(f32[1,512]{1,0:T(1,128)S(1)} %get-tuple-element.59), channel_id=1, source_target_pairs={{1,0},{2,1},{3,2},{0,3},{5,4},{6,5},{7,6},{4,7},{9,8},{10,9},{11,1... | collective-permute-start | bytes 6152 | tf_op jit(solution)/shard_map/ppermute | solution.py:283
  87.9 1.5 %collective-permute-done.14 = f32[1,512]{1,0:T(1,128)S(1)} collective-permute-done((f32[1,512]{1,0:T(1,128)S(1)}, f32[1,512]{1,0:T(1,128)S(1)}, u32[]{:S(2)}, u32[]{:S(2)}) %collective-permute-start.14) | collective-permute-done | bytes 2080 | tf_op jit(solution)/shard_map/ppermute | solution.py:282
  89.4 0.0 collective-permute-done.15
  89.4 0.6 fusion
  (4 shorter events, 0.0 us)
Async XLA Ops:
  2.3 15.6 %collective-permute-start = (bf16[528,1024]{1,0:T(8,128)(2,1)S(1)}, bf16[528,1024]{1,0:T(8,128)(2,1)S(1)}, u32[]{:S(2)}, u32[]{:S(2)}) collective-permute-start(bf16[528,1024]{1,0:T(8,128)(2,1)S(1)} %shard_map.46.t_ref), channel_id=1, source_target_pairs={{1,0},{2,1},{3,2},{0,3},{5,4},{6,5},{7,6},{4,7},{9,8},{10,9},{11,1... | collective-permute-start | bytes 3244040 | tf_op jit(solution)/shard_map/ppermute | solution.py:253
  5.2 18.3 %collective-permute-start.1 = (bf16[528,1024]{1,0:T(8,128)(2,1)S(1)}, bf16[528,1024]{1,0:T(8,128)(2,1)S(1)}, u32[]{:S(2)}, u32[]{:S(2)}) collective-permute-start(bf16[528,1024]{1,0:T(8,128)(2,1)S(1)} %shard_map.46.t_ref), channel_id=1, source_target_pairs={{52,0},{53,1},{54,2},{55,3},{56,4},{57,5},{58,6},{59,7},{60,8},{61... | collective-permute-start | bytes 3244040 | tf_op jit(solution)/shard_map/ppermute | solution.py:253
  17.9 21.0 %collective-permute-start.2 = (bf16[528,1024]{1,0:T(8,128)(2,1)S(1)}, bf16[528,1024]{1,0:T(8,128)(2,1)S(1)}, u32[]{:S(2)}, u32[]{:S(2)}) collective-permute-start(bf16[528,1024]{1,0:T(8,128)(2,1)S(1)} %collective-permute-done.refs_0_), channel_id=1, source_target_pairs={{12,0},{13,1},{14,2},{15,3},{0,4},{1,5},{2,6},{3,7},{4,8},{5,9},{6... | collective-permute-start | bytes 3244040 | tf_op jit(solution)/shard_map/ppermute | solution.py:253
  19.5 28.3 %collective-permute-start.3 = (bf16[528,1024]{1,0:T(8,128)(2,1)S(1)}, bf16[528,1024]{1,0:T(8,128)(2,1)S(1)}, u32[]{:S(2)}, u32[]{:S(2)}) collective-permute-start(bf16[528,1024]{1,0:T(8,128)(2,1)S(1)} %shard_map.46.t_ref), channel_id=1, source_target_pairs={{16,0},{17,1},{18,2},{19,3},{20,4},{21,5},{22,6},{23,7},{24,8},{25... | collective-permute-start | bytes 3244040 | tf_op jit(solution)/shard_map/ppermute | solution.py:253
  23.5 25.9 %collective-permute-start.4 = (bf16[528,1024]{1,0:T(8,128)(2,1)S(1)}, bf16[528,1024]{1,0:T(8,128)(2,1)S(1)}, u32[]{:S(2)}, u32[]{:S(2)}) collective-permute-start(bf16[528,1024]{1,0:T(8,128)(2,1)S(1)} %shard_map.46.t_ref), channel_id=1, source_target_pairs={{51,0},{48,1},{49,2},{50,3},{55,4},{52,5},{53,6},{54,7},{59,8},{56... | collective-permute-start | bytes 3244040 | tf_op jit(solution)/shard_map/ppermute | solution.py:253
  23.5 34.4 %collective-permute-start.5 = (bf16[528,1024]{1,0:T(8,128)(2,1)S(1)}, bf16[528,1024]{1,0:T(8,128)(2,1)S(1)}, u32[]{:S(2)}, u32[]{:S(2)}) collective-permute-start(bf16[528,1024]{1,0:T(8,128)(2,1)S(1)} %collective-permute-done.1.refs_1_), channel_id=1, source_target_pairs={{3,0},{0,1},{1,2},{2,3},{7,4},{4,5},{5,6},{6,7},{11,8},{8,9},{9,10... | collective-permute-start | bytes 3244040 | tf_op jit(solution)/shard_map/ppermute | solution.py:253
  24.8 33.2 %collective-permute-start.6 = (bf16[528,1024]{1,0:T(8,128)(2,1)S(1)}, bf16[528,1024]{1,0:T(8,128)(2,1)S(1)}, u32[]{:S(2)}, u32[]{:S(2)}) collective-permute-start(bf16[528,1024]{1,0:T(8,128)(2,1)S(1)} %collective-permute-done.1.refs_1_), channel_id=1, source_target_pairs={{1,0},{2,1},{3,2},{0,3},{5,4},{6,5},{7,6},{4,7},{9,8},{10,9},{11,1... | collective-permute-start | bytes 3244040 | tf_op jit(solution)/shard_map/ppermute | solution.py:253
  38.9 24.3 %collective-permute-start.7 = (bf16[528,1024]{1,0:T(8,128)(2,1)S(1)}, bf16[528,1024]{1,0:T(8,128)(2,1)S(1)}, u32[]{:S(2)}, u32[]{:S(2)}) collective-permute-start(bf16[528,1024]{1,0:T(8,128)(2,1)S(1)} %collective-permute-done.2.refs_0_), channel_id=1, source_target_pairs={{16,0},{17,1},{18,2},{19,3},{20,4},{21,5},{22,6},{23,7},{24,8},{25... | collective-permute-start | bytes 3244040 | tf_op jit(solution)/shard_map/ppermute | solution.py:253
  47.8 15.5 %collective-permute-start.8 = (bf16[528,1024]{1,0:T(8,128)(2,1)S(1)}, bf16[528,1024]{1,0:T(8,128)(2,1)S(1)}, u32[]{:S(2)}, u32[]{:S(2)}) collective-permute-start(bf16[528,1024]{1,0:T(8,128)(2,1)S(1)} %collective-permute-done.3.refs_1_), channel_id=1, source_target_pairs={{4,0},{5,1},{6,2},{7,3},{8,4},{9,5},{10,6},{11,7},{12,8},{13,9},{1... | collective-permute-start | bytes 3244040 | tf_op jit(solution)/shard_map/ppermute | solution.py:253
  49.4 19.1 %collective-permute-start.9 = (bf16[528,1024]{1,0:T(8,128)(2,1)S(1)}, bf16[528,1024]{1,0:T(8,128)(2,1)S(1)}, u32[]{:S(2)}, u32[]{:S(2)}) collective-permute-start(bf16[528,1024]{1,0:T(8,128)(2,1)S(1)} %collective-permute-done.4.refs_2_), channel_id=1, source_target_pairs={{12,0},{13,1},{14,2},{15,3},{0,4},{1,5},{2,6},{3,7},{4,8},{5,9},{6... | collective-permute-start | bytes 3244040 | tf_op jit(solution)/shard_map/ppermute | solution.py:253
  72.1 5.7 %collective-permute-start.10 = (f32[9,512]{1,0:T(8,128)S(1)}, f32[9,512]{1,0:T(8,128)S(1)}, u32[]{:S(2)}, u32[]{:S(2)}) collective-permute-start(f32[9,512]{1,0:T(8,128)S(1)} %get-tuple-element.55), channel_id=1, source_target_pairs={{48,0},{49,1},{50,2},{51,3},{52,4},{53,5},{54,6},{55,7},{56,8},{57... | collective-permute-start | bytes 55304 | tf_op jit(solution)/shard_map/ppermute | solution.py:282
  72.5 5.2 %collective-permute-start.11 = (f32[9,512]{1,0:T(8,128)S(1)}, f32[9,512]{1,0:T(8,128)S(1)}, u32[]{:S(2)}, u32[]{:S(2)}) collective-permute-start(f32[9,512]{1,0:T(8,128)S(1)} %get-tuple-element.56), channel_id=1, source_target_pairs={{16,0},{17,1},{18,2},{19,3},{20,4},{21,5},{22,6},{23,7},{24,8},{25... | collective-permute-start | bytes 55304 | tf_op jit(solution)/shard_map/ppermute | solution.py:283
  77.8 4.9 %collective-permute-start.12 = (f32[3,512]{1,0:T(4,128)S(1)}, f32[3,512]{1,0:T(4,128)S(1)}, u32[]{:S(2)}, u32[]{:S(2)}) collective-permute-start(f32[3,512]{1,0:T(4,128)S(1)} %get-tuple-element.58), channel_id=1, source_target_pairs={{12,0},{13,1},{14,2},{15,3},{0,4},{1,5},{2,6},{3,7},{4,8},{5,9},{6... | collective-permute-start | bytes 18440 | tf_op jit(solution)/shard_map/ppermute | solution.py:282
  79.0 3.7 %collective-permute-start.13 = (f32[3,512]{1,0:T(4,128)S(1)}, f32[3,512]{1,0:T(4,128)S(1)}, u32[]{:S(2)}, u32[]{:S(2)}) collective-permute-start(f32[3,512]{1,0:T(4,128)S(1)} %get-tuple-element.57), channel_id=1, source_target_pairs={{4,0},{5,1},{6,2},{7,3},{8,4},{9,5},{10,6},{11,7},{12,8},{13,9},{1... | collective-permute-start | bytes 18440 | tf_op jit(solution)/shard_map/ppermute | solution.py:283
  82.7 6.7 %collective-permute-start.14 = (f32[1,512]{1,0:T(1,128)S(1)}, f32[1,512]{1,0:T(1,128)S(1)}, u32[]{:S(2)}, u32[]{:S(2)}) collective-permute-start(f32[1,512]{1,0:T(1,128)S(1)} %get-tuple-element.60), channel_id=1, source_target_pairs={{3,0},{0,1},{1,2},{2,3},{7,4},{4,5},{5,6},{6,7},{11,8},{8,9},{9,10... | collective-permute-start | bytes 6152 | tf_op jit(solution)/shard_map/ppermute | solution.py:282
  84.1 5.3 %collective-permute-start.15 = (f32[1,512]{1,0:T(1,128)S(1)}, f32[1,512]{1,0:T(1,128)S(1)}, u32[]{:S(2)}, u32[]{:S(2)}) collective-permute-start(f32[1,512]{1,0:T(1,128)S(1)} %get-tuple-element.59), channel_id=1, source_target_pairs={{1,0},{2,1},{3,2},{0,3},{5,4},{6,5},{7,6},{4,7},{9,8},{10,9},{11,1... | collective-permute-start | bytes 6152 | tf_op jit(solution)/shard_map/ppermute | solution.py:283

commit v4 on v3

--- a/solution.py
+++ b/solution.py
@@ -13,23 +13,23 @@
 UNROLL = 12
 FLAG_ROWS = 16
 DEAD = -4.0
-NORM_PARTS = 4
+NORM_PARTS = 2
 
 PLAN = [
     ((0, 0, 1), (0, 0, 0)),
     ((3, 1, 0), (0, 0, 0)),
     ((0, 3, 1), (0, 0, 1)),
+    ((3, 0, 3), (0, 0, 0)),
     ((1, 0, 0), (0, 0, 0)),
-    ((3, 0, 3), (0, 0, 0)),
     ((3, 1, 3), (3, 1, 0)),
     ((3, 1, 1), (3, 1, 0)),
     ((1, 3, 1), (0, 3, 1)),
+    ((3, 3, 3), (3, 0, 3)),
     ((1, 1, 0), (1, 0, 0)),
-    ((3, 3, 3), (3, 0, 3)),
 ]
 OFFSETS = [(0, 0, 0)] + [d for d, _ in PLAN]
-STAGES = [2, 5, 7, 9, 10]
-GATES = {(0, 3, 1): 0, (1, 3, 1): 1}
+STAGES = [2, 4, 7, 9, 10]
+GATES = {(0, 3, 1): 0, (1, 3, 1): 1, (1, 1, 0): 2}
 AFTER = {(1, 0, 0): (0, 0, 1), (3, 0, 3): (0, 0, 1)}
 
 
@@ -75,29 +75,26 @@
 
 
 def work_table():
-    stages = [[] for _ in STAGES]
+    full, halved = [[] for _ in STAGES], [[] for _ in STAGES]
     for a, b in choose_pairs():
         stage = next(i for i, n in enumerate(STAGES) if a <= n)
         twin = all((2 * g) % SIDE == 0 for g in sub(OFFSETS[a], OFFSETS[b]))
-        stages[stage].extend([(a, b, -1)] if twin else [(a, b, 0), (a, b, 1)])
-    loops = []
-    for s in stages:
-        steps = -(-len(s) // UNROLL)
-        unroll = -(-len(s) // steps)
-        loops.append((steps, unroll))
-        s.extend([s[-1]] * (steps * unroll - len(s)))
-    units = [u for s in stages for u in s]
-    table = np.zeros((2, SIDE**3, len(OFFSETS) + len(units) * 3), np.int32)
+        (halved if twin else full)[stage].append((a, b))
+    loops, units = [], []
+    for f, h in zip(full, halved):
+        steps = -(-len(f) // UNROLL)
+        unroll = -(-len(f) // max(steps, 1))
+        f = f + f[-1:] * (steps * unroll - len(f))
+        loops.append((steps, unroll, len(h)))
+        units += f + h
+    table = np.zeros((2, SIDE**3, len(units) * 3), np.int32)
     for c in range(2):
         offs = [turned(d) if c else d for d in OFFSETS]
         for v in cube():
-            table[c, place_of(v), : len(OFFSETS)] = [place_of(add(v, d)) for d in offs]
-            for n, (a, b, half) in enumerate(units):
+            for n, (a, b) in enumerate(units):
                 first = place_of(add(v, offs[a])) < place_of(add(v, offs[b]))
                 k, q = (a, b) if first else (b, a)
-                h = half if half >= 0 else int(first)
-                at = len(OFFSETS) + 3 * n
-                table[c, place_of(v), at : at + 3] = (k, q, h)
+                table[c, place_of(v), 3 * n : 3 * n + 3] = (k, q, int(first))
     return table, loops
 
 
@@ -139,12 +136,18 @@
     return jnp.max(s.reshape(n // 8, 8, w), axis=0)
 
 
-def unit_work(tab, at, stack, biases, acc):
-    half = stack.shape[1] // 2
+def pair_work(tab, at, stack, biases, acc, halved):
+    rows = stack.shape[1]
+    half = rows // 2
     k, q, h = tab[at], tab[at + 1], tab[at + 2]
-    s = dot_t(stack[k], stack[q, pl.ds(pl.multiple_of(h * half, half), half), :])
-    s = s + jnp.tile(biases[k], (1, half // 128))
-    acc[q, h] = jnp.maximum(acc[q, h], fold_rows(s))
+    query = stack[q, pl.ds(pl.multiple_of(h * half, half), half), :] if halved else stack[q]
+    s = dot_t(stack[k], query)
+    s = fold_rows(s + jnp.tile(biases[k], (1, s.shape[1] // 128)))
+    if halved:
+        acc[q, h] = jnp.maximum(acc[q, h], s)
+    else:
+        for i in range(2):
+            acc[q, i] = jnp.maximum(acc[q, i], s[:, i * half : (i + 1) * half])
 
 
 def self_kernel(t_ref, tab, stack, biases, acc, turn):
@@ -163,21 +166,15 @@
     turn[...] = jnp.full(turn.shape, tab[0], jnp.int32)
 
 
-def pair_kernel(tab, turn_in, *refs, new, start, steps, unroll, last):
+def pair_kernel(tab, turn_in, *refs, new, start, steps, unroll, halved, last):
     n = len(new)
     tiles = refs[:n]
     n_out = 3 * last
     stack, biases, acc = refs[n + 3 : n + 6]
     turn = refs[n + 6]
     outs = refs[n + 7 : n + 7 + n_out]
-    sems = refs[n + 7 + n_out]
     rows = stack.shape[1]
     half = rows // 2
-    copies = []
-    for i, slot in enumerate(new):
-        copies.append(pltpu.make_async_copy(tiles[i].at[pl.ds(0, rows)], stack.at[slot], sems.at[i]))
-    for c in copies:
-        c.start()
     flags = jnp.concatenate([t[rows:, :rows] for t in tiles], axis=0)
     shape = (n * FLAG_ROWS, n * 128)
     row, lane = (lax.broadcasted_iota(jnp.int32, shape, a) for a in range(2))
@@ -185,15 +182,17 @@
     columns = lax.dot_general(flags, spread, (((0,), (0,)), ((), ())), preferred_element_type=jnp.float32)
     for i, slot in enumerate(new):
         biases[slot] = columns[:, i * 128 : (i + 1) * 128]
-    for c in copies:
-        c.wait()
+    for i, slot in enumerate(new):
+        stack[slot] = tiles[i][:rows, :]
 
     def step(u, carry):
         for j in range(unroll):
-            unit_work(tab, len(OFFSETS) + 3 * (start + u * unroll + j), stack, biases, acc)
+            pair_work(tab, 3 * (start + u * unroll + j), stack, biases, acc, False)
         return carry
 
     lax.fori_loop(0, steps, step, 0)
+    for j in range(halved):
+        pair_work(tab, 3 * (start + steps * unroll + j), stack, biases, acc, True)
     turn[...] = turn_in[...]
     if last:
         for out in outs:
@@ -254,24 +253,23 @@
         i = len(turns) - 1
         if len(held) - 1 < STAGES[i]:
             continue
-        steps, unroll = loops[i]
+        steps, unroll, halved = loops[i]
         new = list(range(arrived + 1, STAGES[i] + 1))
         last = i == len(loops) - 1
         outs = [jax.ShapeDtypeStruct((8, 128), jnp.int32)]
         outs += [jax.ShapeDtypeStruct((9, rows), jnp.float32)] * (3 * last)
         results = pl.pallas_call(
-            functools.partial(pair_kernel, new=new, start=start, steps=steps, unroll=unroll, last=last),
+            functools.partial(pair_kernel, new=new, start=start, steps=steps, unroll=unroll, halved=halved, last=last),
             out_shape=state + outs,
             in_specs=[smem] + [vmem] * (len(new) + 4),
             out_specs=[vmem] * (3 + len(outs)),
             input_output_aliases={2 + len(new) + j: j for j in range(3)},
-            scratch_shapes=[pltpu.SemaphoreType.DMA((len(new),))],
             compiler_params=pltpu.CompilerParams(vmem_limit_bytes=24 * 2**20),
             cost_estimate=pl.CostEstimate(flops=1000, bytes_accessed=1000, transcendentals=0),
         )(tab, turns[i], *[held[OFFSETS[s]] for s in new], *held_state)
         held_state, finals = results[:3], results[4:]
         turns.append(results[3])
-        start += steps * unroll
+        start += steps * unroll + halved
         arrived = STAGES[i]
     own_part, ahead, behind = finals
     for axis in range(3):

time: 91.3 us -> 89.4 us (0.979)
  Pallas kernels: 27.9 us -> 25.3 us
  starting transfers between devices: 37.4 us -> 39.6 us
  waiting for transfers between devices: 22.6 us -> 21.5 us
    pallas_call x5, Pallas kernels: 25 us -> 22.5 us  [on_device(): pl.pallas_call(functools.partial(pair_kernel, new=new, start=start, steps...]
    ppermute x3, starting transfers between devices: 3.04 us -> 4.63 us  [on_device(): ahead = lax.ppermute(ahead, ('clus', 'help'), moves(back))]
    ppermute x10, waiting for transfers between devices: 17.7 us -> 16.2 us  [on_device(): held[d] = lax.ppermute(sent, ('clus', 'help'), moves(sub(d, source)))]
    ppermute x10, starting transfers between devices: 25 us -> 26.3 us  [on_device(): held[d] = lax.ppermute(sent, ('clus', 'help'), moves(sub(d, source)))]
  transfers between devices with their start and end apart: 16 -> 16, of which waited for: 6 -> 7; matrix products, arithmetic and copies ran while one was open for 1% -> 1% of each run, Pallas kernels for 25% -> 24%
where the time goes in v4:
time: 89.4 us; the launch traced here: 88.4 us
  starting transfers between devices  39.6 us (44%)
  Pallas kernels  25.3 us (28%)
  waiting for transfers between devices  21.5 us (24%)
    ppermute x10, starting transfers between devices, on_device(): held[d] = lax.ppermute(sent, ('clus', 'help'), moves(sub(d, source)))  26.3 us
    pallas_call x5, Pallas kernels, on_device(): pl.pallas_call(functools.partial(pair_kernel, new=new, start=start, steps...  22.5 us
    ppermute x10, waiting for transfers between devices, on_device(): held[d] = lax.ppermute(sent, ('clus', 'help'), moves(sub(d, source)))  16.2 us
    ppermute x3, starting transfers between devices, on_device(): behind = lax.ppermute(behind, ('clus', 'help'), moves(step))  8.62 us
    ppermute x3, waiting for transfers between devices, on_device(): ahead = lax.ppermute(ahead, ('clus', 'help'), moves(back))  4.99 us
    ppermute x3, starting transfers between devices, on_device(): ahead = lax.ppermute(ahead, ('clus', 'help'), moves(back))  4.63 us
  transfers between devices with their start and end apart: 16, of which 7 were waited for; matrix products, arithmetic and copies ran while one was open for 1% of the time, Pallas kernels for 24%

profile of v4, /device:TPU:0, one launch (start us, length us, event | category | flops | bytes accessed | tf_op | source)
XLA Modules:
  0.0 88.4 jit_solution(10637646210878323962)
XLA Ops:
  0.7 1.5 %shard_map.46.t_ref = bf16[528,1024]{1,0:T(8,128)(2,1)S(1)} custom-call(s32[1]{0:T(128)S(6)} %convert_element_type.3.alive, bf16[512,1024]{1,0:T(8,128)(2,1)} %bitcast.7, s32[1,512]{1,0:T(1,128)} %bitcast.8), custom_call_target="tpu_custom_call" | custom-call | tf_op jit(solution)/shard_map/pallas_call | solution.py:223
  2.2 2.9 %collective-permute-start = (bf16[528,1024]{1,0:T(8,128)(2,1)S(1)}, bf16[528,1024]{1,0:T(8,128)(2,1)S(1)}, u32[]{:S(2)}, u32[]{:S(2)}) collective-permute-start(bf16[528,1024]{1,0:T(8,128)(2,1)S(1)} %shard_map.46.t_ref), channel_id=1, source_target_pairs={{1,0},{2,1},{3,2},{0,3},{5,4},{6,5},{7,6},{4,7},{9,8},{10,9},{11,1... | collective-permute-start | bytes 3244040 | tf_op jit(solution)/shard_map/ppermute | solution.py:252
  5.1 4.4 %collective-permute-start.1 = (bf16[528,1024]{1,0:T(8,128)(2,1)S(1)}, bf16[528,1024]{1,0:T(8,128)(2,1)S(1)}, u32[]{:S(2)}, u32[]{:S(2)}) collective-permute-start(bf16[528,1024]{1,0:T(8,128)(2,1)S(1)} %shard_map.46.t_ref), channel_id=1, source_target_pairs={{52,0},{53,1},{54,2},{55,3},{56,4},{57,5},{58,6},{59,7},{60,8},{61... | collective-permute-start | bytes 3244040 | tf_op jit(solution)/shard_map/ppermute | solution.py:252
  9.4 0.7 dynamic-slice_bitcast_fusion.tab
  10.1 1.2 %shard_map.47 = (bf16[11,512,1024]{2,1,0:T(8,128)(2,1)S(1)}, f32[11,512,128]{2,1,0:T(8,128)S(1)}, f32[11,2,8,256]{3,2,1,0:T(8,128)S(1)}, s32[8,128]{1,0:T(8,128)S(1)}) custom-call(bf16[528,1024]{1,0:T(8,128)(2,1)S(1)} %shard_map.46.t_ref, s32[105]{0:T(128)S(1)} %dynamic-slice_bitcast_fusion.tab), custom_call_target="tpu_custom_call" | custom-call | flops 1000 | bytes 1000 | tf_op jit(solution)/shard_map/pallas_call | solution.py:235
  11.4 6.4 %collective-permute-done.refs_0_ = bf16[528,1024]{1,0:T(8,128)(2,1)S(1)} collective-permute-done((bf16[528,1024]{1,0:T(8,128)(2,1)S(1)}, bf16[528,1024]{1,0:T(8,128)(2,1)S(1)}, u32[]{:S(2)}, u32[]{:S(2)}) %collective-permute-start) | collective-permute-done | bytes 1081376 | tf_op jit(solution)/shard_map/ppermute | solution.py:252
  17.7 1.6 %collective-permute-start.2 = (bf16[528,1024]{1,0:T(8,128)(2,1)S(1)}, bf16[528,1024]{1,0:T(8,128)(2,1)S(1)}, u32[]{:S(2)}, u32[]{:S(2)}) collective-permute-start(bf16[528,1024]{1,0:T(8,128)(2,1)S(1)} %collective-permute-done.refs_0_), channel_id=1, source_target_pairs={{12,0},{13,1},{14,2},{15,3},{0,4},{1,5},{2,6},{3,7},{4,8},{5,9},{6... | collective-permute-start | bytes 3244040 | tf_op jit(solution)/shard_map/ppermute | solution.py:252
  19.3 2.6 %collective-permute-start.3 = (bf16[528,1024]{1,0:T(8,128)(2,1)S(1)}, bf16[528,1024]{1,0:T(8,128)(2,1)S(1)}, u32[]{:S(2)}, u32[]{:S(2)}) collective-permute-start(bf16[528,1024]{1,0:T(8,128)(2,1)S(1)} %shard_map.46.t_ref), channel_id=1, source_target_pairs={{51,0},{48,1},{49,2},{50,3},{55,4},{52,5},{53,6},{54,7},{59,8},{56... | collective-permute-start | bytes 3244040 | tf_op jit(solution)/shard_map/ppermute | solution.py:252
  21.9 1.5 %collective-permute-start.4 = (bf16[528,1024]{1,0:T(8,128)(2,1)S(1)}, bf16[528,1024]{1,0:T(8,128)(2,1)S(1)}, u32[]{:S(2)}, u32[]{:S(2)}) collective-permute-start(bf16[528,1024]{1,0:T(8,128)(2,1)S(1)} %shard_map.46.t_ref), channel_id=1, source_target_pairs={{16,0},{17,1},{18,2},{19,3},{20,4},{21,5},{22,6},{23,7},{24,8},{25... | collective-permute-start | bytes 3244040 | tf_op jit(solution)/shard_map/ppermute | solution.py:252
  23.4 0.0 collective-permute-done.1.refs_1_
  23.4 1.3 %collective-permute-start.5 = (bf16[528,1024]{1,0:T(8,128)(2,1)S(1)}, bf16[528,1024]{1,0:T(8,128)(2,1)S(1)}, u32[]{:S(2)}, u32[]{:S(2)}) collective-permute-start(bf16[528,1024]{1,0:T(8,128)(2,1)S(1)} %collective-permute-done.1.refs_1_), channel_id=1, source_target_pairs={{3,0},{0,1},{1,2},{2,3},{7,4},{4,5},{5,6},{6,7},{11,8},{8,9},{9,10... | collective-permute-start | bytes 3244040 | tf_op jit(solution)/shard_map/ppermute | solution.py:252
  24.7 2.4 %collective-permute-start.6 = (bf16[528,1024]{1,0:T(8,128)(2,1)S(1)}, bf16[528,1024]{1,0:T(8,128)(2,1)S(1)}, u32[]{:S(2)}, u32[]{:S(2)}) collective-permute-start(bf16[528,1024]{1,0:T(8,128)(2,1)S(1)} %collective-permute-done.1.refs_1_), channel_id=1, source_target_pairs={{1,0},{2,1},{3,2},{0,3},{5,4},{6,5},{7,6},{4,7},{9,8},{10,9},{11,1... | collective-permute-start | bytes 3244040 | tf_op jit(solution)/shard_map/ppermute | solution.py:252
  27.1 2.5 %shard_map.48 = (bf16[11,512,1024]{2,1,0:T(8,128)(2,1)S(1)}, f32[11,512,128]{2,1,0:T(8,128)S(1)}, f32[11,2,8,256]{3,2,1,0:T(8,128)S(1)}, s32[8,128]{1,0:T(8,128)S(1)}) custom-call(s32[105]{0:T(128)S(1)} %dynamic-slice_bitcast_fusion.tab, s32[8,128]{1,0:T(8,128)S(1)} %get-tuple-element.32.turn_in, ...), custom_call_target="tpu_custom_call", output_to_operand_aliasing={{0}: (4, {}), {1}: (5, {}), {2}: (6, {})} | custom-call | flops 1000 | bytes 1000 | tf_op jit(solution)/shard_map/pallas_call | solution.py:261
  29.6 9.1 %collective-permute-done.2.refs_0_ = bf16[528,1024]{1,0:T(8,128)(2,1)S(1)} collective-permute-done((bf16[528,1024]{1,0:T(8,128)(2,1)S(1)}, bf16[528,1024]{1,0:T(8,128)(2,1)S(1)}, u32[]{:S(2)}, u32[]{:S(2)}) %collective-permute-start.2) | collective-permute-done | bytes 1081376 | tf_op jit(solution)/shard_map/ppermute | solution.py:252
  38.7 5.1 %collective-permute-start.7 = (bf16[528,1024]{1,0:T(8,128)(2,1)S(1)}, bf16[528,1024]{1,0:T(8,128)(2,1)S(1)}, u32[]{:S(2)}, u32[]{:S(2)}) collective-permute-start(bf16[528,1024]{1,0:T(8,128)(2,1)S(1)} %collective-permute-done.2.refs_0_), channel_id=1, source_target_pairs={{16,0},{17,1},{18,2},{19,3},{20,4},{21,5},{22,6},{23,7},{24,8},{25... | collective-permute-start | bytes 3244040 | tf_op jit(solution)/shard_map/ppermute | solution.py:252
  43.8 0.0 collective-permute-done.3.refs_1_
  43.9 1.0 %collective-permute-start.8 = (bf16[528,1024]{1,0:T(8,128)(2,1)S(1)}, bf16[528,1024]{1,0:T(8,128)(2,1)S(1)}, u32[]{:S(2)}, u32[]{:S(2)}) collective-permute-start(bf16[528,1024]{1,0:T(8,128)(2,1)S(1)} %collective-permute-done.3.refs_1_), channel_id=1, source_target_pairs={{12,0},{13,1},{14,2},{15,3},{0,4},{1,5},{2,6},{3,7},{4,8},{5,9},{6... | collective-permute-start | bytes 3244040 | tf_op jit(solution)/shard_map/ppermute | solution.py:252
  44.9 4.7 %shard_map.49 = (bf16[11,512,1024]{2,1,0:T(8,128)(2,1)S(1)}, f32[11,512,128]{2,1,0:T(8,128)S(1)}, f32[11,2,8,256]{3,2,1,0:T(8,128)S(1)}, s32[8,128]{1,0:T(8,128)S(1)}) custom-call(s32[105]{0:T(128)S(1)} %dynamic-slice_bitcast_fusion.tab, s32[8,128]{1,0:T(8,128)S(1)} %get-tuple-element.36.turn_in, ...), custom_call_target="tpu_custom_call", output_to_operand_aliasing={{0}: (4, {}), {1}: (5, {}), {2}: (6, {})} | custom-call | flops 1000 | bytes 1000 | tf_op jit(solution)/shard_map/pallas_call | solution.py:261
  49.6 0.0 collective-permute-done.4.refs_0_
  49.6 3.6 %collective-permute-start.9 = (bf16[528,1024]{1,0:T(8,128)(2,1)S(1)}, bf16[528,1024]{1,0:T(8,128)(2,1)S(1)}, u32[]{:S(2)}, u32[]{:S(2)}) collective-permute-start(bf16[528,1024]{1,0:T(8,128)(2,1)S(1)} %collective-permute-done.4.refs_0_), channel_id=1, source_target_pairs={{4,0},{5,1},{6,2},{7,3},{8,4},{9,5},{10,6},{11,7},{12,8},{13,9},{1... | collective-permute-start | bytes 3244040 | tf_op jit(solution)/shard_map/ppermute | solution.py:252
  53.2 0.0 collective-permute-done.5.refs_1_
  53.2 0.0 collective-permute-done.6.refs_2_
  53.2 7.4 %shard_map.50 = (bf16[11,512,1024]{2,1,0:T(8,128)(2,1)S(1)}, f32[11,512,128]{2,1,0:T(8,128)S(1)}, f32[11,2,8,256]{3,2,1,0:T(8,128)S(1)}, s32[8,128]{1,0:T(8,128)S(1)}) custom-call(s32[105]{0:T(128)S(1)} %dynamic-slice_bitcast_fusion.tab, s32[8,128]{1,0:T(8,128)S(1)} %get-tuple-element.42.turn_in, ...), custom_call_target="tpu_custom_call", output_to_operand_aliasing={{0}: (5, {}), {1}: (6, {}), {2}: (7, {})} | custom-call | flops 1000 | bytes 1000 | tf_op jit(solution)/shard_map/pallas_call | solution.py:261
  60.6 0.0 collective-permute-done.7.refs_0_
  60.6 0.7 collective-permute-done.8.refs_1_
  61.3 5.1 %shard_map.51 = (bf16[11,512,1024]{2,1,0:T(8,128)(2,1)S(1)}, f32[11,512,128]{2,1,0:T(8,128)S(1)}, f32[11,2,8,256]{3,2,1,0:T(8,128)S(1)}, s32[8,128]{1,0:T(8,128)S(1)}) custom-call(s32[105]{0:T(128)S(1)} %dynamic-slice_bitcast_fusion.tab, s32[8,128]{1,0:T(8,128)S(1)} %get-tuple-element.46.turn_in, ...), custom_call_target="tpu_custom_call", output_to_operand_aliasing={{0}: (4, {}), {1}: (5, {}), {2}: (6, {})} | custom-call | flops 1000 | bytes 1000 | tf_op jit(solution)/shard_map/pallas_call | solution.py:261
  66.4 0.0 collective-permute-done.9.refs_0_
  66.5 2.8 %shard_map.52 = (bf16[11,512,1024]{2,1,0:T(8,128)(2,1)S(1)}, f32[11,512,128]{2,1,0:T(8,128)S(1)}, f32[11,2,8,256]{3,2,1,0:T(8,128)S(1)}, s32[8,128]{1,0:T(8,128)...) custom-call(s32[105]{0:T(128)S(1)} %dynamic-slice_bitcast_fusion.tab, ...), custom_call_target="tpu_custom_call", output_to_operand_aliasing={{0}: (3, {}), {1}: (4, {}), {2}: (5, {})} | custom-call | flops 1000 | bytes 1000 | tf_op jit(solution)/shard_map/pallas_call | solution.py:261
  69.2 0.0 collective-permute-start.10
  69.2 3.2 %collective-permute-start.11 = (f32[9,512]{1,0:T(8,128)S(1)}, f32[9,512]{1,0:T(8,128)S(1)}, u32[]{:S(2)}, u32[]{:S(2)}) collective-permute-start(f32[9,512]{1,0:T(8,128)S(1)} %get-tuple-element.58), channel_id=1, source_target_pairs={{16,0},{17,1},{18,2},{19,3},{20,4},{21,5},{22,6},{23,7},{24,8},{25... | collective-permute-start | bytes 55304 | tf_op jit(solution)/shard_map/ppermute | solution.py:281
  72.5 1.9 %collective-permute-done.10 = f32[9,512]{1,0:T(8,128)S(1)} collective-permute-done((f32[9,512]{1,0:T(8,128)S(1)}, f32[9,512]{1,0:T(8,128)S(1)}, u32[]{:S(2)}, u32[]{:S(2)}) %collective-permute-start.10) | collective-permute-done | bytes 18464 | tf_op jit(solution)/shard_map/ppermute | solution.py:280
  74.4 0.0 collective-permute-done.11
  74.4 1.5 %collective-permute-start.12 = (f32[3,512]{1,0:T(4,128)S(1)}, f32[3,512]{1,0:T(4,128)S(1)}, u32[]{:S(2)}, u32[]{:S(2)}) collective-permute-start(f32[3,512]{1,0:T(4,128)S(1)} %get-tuple-element.60), channel_id=1, source_target_pairs={{12,0},{13,1},{14,2},{15,3},{0,4},{1,5},{2,6},{3,7},{4,8},{5,9},{6... | collective-permute-start | bytes 18440 | tf_op jit(solution)/shard_map/ppermute | solution.py:280
  75.9 1.8 %collective-permute-start.13 = (f32[3,512]{1,0:T(4,128)S(1)}, f32[3,512]{1,0:T(4,128)S(1)}, u32[]{:S(2)}, u32[]{:S(2)}) collective-permute-start(f32[3,512]{1,0:T(4,128)S(1)} %get-tuple-element.59), channel_id=1, source_target_pairs={{4,0},{5,1},{6,2},{7,3},{8,4},{9,5},{10,6},{11,7},{12,8},{13,9},{1... | collective-permute-start | bytes 18440 | tf_op jit(solution)/shard_map/ppermute | solution.py:281
  77.7 1.6 %collective-permute-done.12 = f32[3,512]{1,0:T(4,128)S(1)} collective-permute-done((f32[3,512]{1,0:T(4,128)S(1)}, f32[3,512]{1,0:T(4,128)S(1)}, u32[]{:S(2)}, u32[]{:S(2)}) %collective-permute-start.12) | collective-permute-done | bytes 6176 | tf_op jit(solution)/shard_map/ppermute | solution.py:280
  79.3 0.2 collective-permute-done.13
  79.6 3.1 %collective-permute-start.14 = (f32[1,512]{1,0:T(1,128)S(1)}, f32[1,512]{1,0:T(1,128)S(1)}, u32[]{:S(2)}, u32[]{:S(2)}) collective-permute-start(f32[1,512]{1,0:T(1,128)S(1)} %get-tuple-element.62), channel_id=1, source_target_pairs={{3,0},{0,1},{1,2},{2,3},{7,4},{4,5},{5,6},{6,7},{11,8},{8,9},{9,10... | collective-permute-start | bytes 6152 | tf_op jit(solution)/shard_map/ppermute | solution.py:280
  82.7 3.6 %collective-permute-start.15 = (f32[1,512]{1,0:T(1,128)S(1)}, f32[1,512]{1,0:T(1,128)S(1)}, u32[]{:S(2)}, u32[]{:S(2)}) collective-permute-start(f32[1,512]{1,0:T(1,128)S(1)} %get-tuple-element.61), channel_id=1, source_target_pairs={{1,0},{2,1},{3,2},{0,3},{5,4},{6,5},{7,6},{4,7},{9,8},{10,9},{11,1... | collective-permute-start | bytes 6152 | tf_op jit(solution)/shard_map/ppermute | solution.py:281
  86.3 1.5 %collective-permute-done.14 = f32[1,512]{1,0:T(1,128)S(1)} collective-permute-done((f32[1,512]{1,0:T(1,128)S(1)}, f32[1,512]{1,0:T(1,128)S(1)}, u32[]{:S(2)}, u32[]{:S(2)}) %collective-permute-start.14) | collective-permute-done | bytes 2080 | tf_op jit(solution)/shard_map/ppermute | solution.py:280
  87.8 0.0 collective-permute-done.15
  87.8 0.6 fusion
  (4 shorter events, 0.0 us)
Async XLA Ops:
  2.2 15.6 %collective-permute-start = (bf16[528,1024]{1,0:T(8,128)(2,1)S(1)}, bf16[528,1024]{1,0:T(8,128)(2,1)S(1)}, u32[]{:S(2)}, u32[]{:S(2)}) collective-permute-start(bf16[528,1024]{1,0:T(8,128)(2,1)S(1)} %shard_map.46.t_ref), channel_id=1, source_target_pairs={{1,0},{2,1},{3,2},{0,3},{5,4},{6,5},{7,6},{4,7},{9,8},{10,9},{11,1... | collective-permute-start | bytes 3244040 | tf_op jit(solution)/shard_map/ppermute | solution.py:252
  5.1 18.3 %collective-permute-start.1 = (bf16[528,1024]{1,0:T(8,128)(2,1)S(1)}, bf16[528,1024]{1,0:T(8,128)(2,1)S(1)}, u32[]{:S(2)}, u32[]{:S(2)}) collective-permute-start(bf16[528,1024]{1,0:T(8,128)(2,1)S(1)} %shard_map.46.t_ref), channel_id=1, source_target_pairs={{52,0},{53,1},{54,2},{55,3},{56,4},{57,5},{58,6},{59,7},{60,8},{61... | collective-permute-start | bytes 3244040 | tf_op jit(solution)/shard_map/ppermute | solution.py:252
  17.7 21.0 %collective-permute-start.2 = (bf16[528,1024]{1,0:T(8,128)(2,1)S(1)}, bf16[528,1024]{1,0:T(8,128)(2,1)S(1)}, u32[]{:S(2)}, u32[]{:S(2)}) collective-permute-start(bf16[528,1024]{1,0:T(8,128)(2,1)S(1)} %collective-permute-done.refs_0_), channel_id=1, source_target_pairs={{12,0},{13,1},{14,2},{15,3},{0,4},{1,5},{2,6},{3,7},{4,8},{5,9},{6... | collective-permute-start | bytes 3244040 | tf_op jit(solution)/shard_map/ppermute | solution.py:252
  19.3 24.5 %collective-permute-start.3 = (bf16[528,1024]{1,0:T(8,128)(2,1)S(1)}, bf16[528,1024]{1,0:T(8,128)(2,1)S(1)}, u32[]{:S(2)}, u32[]{:S(2)}) collective-permute-start(bf16[528,1024]{1,0:T(8,128)(2,1)S(1)} %shard_map.46.t_ref), channel_id=1, source_target_pairs={{51,0},{48,1},{49,2},{50,3},{55,4},{52,5},{53,6},{54,7},{59,8},{56... | collective-permute-start | bytes 3244040 | tf_op jit(solution)/shard_map/ppermute | solution.py:252
  21.9 27.7 %collective-permute-start.4 = (bf16[528,1024]{1,0:T(8,128)(2,1)S(1)}, bf16[528,1024]{1,0:T(8,128)(2,1)S(1)}, u32[]{:S(2)}, u32[]{:S(2)}) collective-permute-start(bf16[528,1024]{1,0:T(8,128)(2,1)S(1)} %shard_map.46.t_ref), channel_id=1, source_target_pairs={{16,0},{17,1},{18,2},{19,3},{20,4},{21,5},{22,6},{23,7},{24,8},{25... | collective-permute-start | bytes 3244040 | tf_op jit(solution)/shard_map/ppermute | solution.py:252
  23.4 29.9 %collective-permute-start.5 = (bf16[528,1024]{1,0:T(8,128)(2,1)S(1)}, bf16[528,1024]{1,0:T(8,128)(2,1)S(1)}, u32[]{:S(2)}, u32[]{:S(2)}) collective-permute-start(bf16[528,1024]{1,0:T(8,128)(2,1)S(1)} %collective-permute-done.1.refs_1_), channel_id=1, source_target_pairs={{3,0},{0,1},{1,2},{2,3},{7,4},{4,5},{5,6},{6,7},{11,8},{8,9},{9,10... | collective-permute-start | bytes 3244040 | tf_op jit(solution)/shard_map/ppermute | solution.py:252
  24.7 28.5 %collective-permute-start.6 = (bf16[528,1024]{1,0:T(8,128)(2,1)S(1)}, bf16[528,1024]{1,0:T(8,128)(2,1)S(1)}, u32[]{:S(2)}, u32[]{:S(2)}) collective-permute-start(bf16[528,1024]{1,0:T(8,128)(2,1)S(1)} %collective-permute-done.1.refs_1_), channel_id=1, source_target_pairs={{1,0},{2,1},{3,2},{0,3},{5,4},{6,5},{7,6},{4,7},{9,8},{10,9},{11,1... | collective-permute-start | bytes 3244040 | tf_op jit(solution)/shard_map/ppermute | solution.py:252
  38.7 21.9 %collective-permute-start.7 = (bf16[528,1024]{1,0:T(8,128)(2,1)S(1)}, bf16[528,1024]{1,0:T(8,128)(2,1)S(1)}, u32[]{:S(2)}, u32[]{:S(2)}) collective-permute-start(bf16[528,1024]{1,0:T(8,128)(2,1)S(1)} %collective-permute-done.2.refs_0_), channel_id=1, source_target_pairs={{16,0},{17,1},{18,2},{19,3},{20,4},{21,5},{22,6},{23,7},{24,8},{25... | collective-permute-start | bytes 3244040 | tf_op jit(solution)/shard_map/ppermute | solution.py:252
  43.9 17.5 %collective-permute-start.8 = (bf16[528,1024]{1,0:T(8,128)(2,1)S(1)}, bf16[528,1024]{1,0:T(8,128)(2,1)S(1)}, u32[]{:S(2)}, u32[]{:S(2)}) collective-permute-start(bf16[528,1024]{1,0:T(8,128)(2,1)S(1)} %collective-permute-done.3.refs_1_), channel_id=1, source_target_pairs={{12,0},{13,1},{14,2},{15,3},{0,4},{1,5},{2,6},{3,7},{4,8},{5,9},{6... | collective-permute-start | bytes 3244040 | tf_op jit(solution)/shard_map/ppermute | solution.py:252
  49.6 16.8 %collective-permute-start.9 = (bf16[528,1024]{1,0:T(8,128)(2,1)S(1)}, bf16[528,1024]{1,0:T(8,128)(2,1)S(1)}, u32[]{:S(2)}, u32[]{:S(2)}) collective-permute-start(bf16[528,1024]{1,0:T(8,128)(2,1)S(1)} %collective-permute-done.4.refs_0_), channel_id=1, source_target_pairs={{4,0},{5,1},{6,2},{7,3},{8,4},{9,5},{10,6},{11,7},{12,8},{13,9},{1... | collective-permute-start | bytes 3244040 | tf_op jit(solution)/shard_map/ppermute | solution.py:252
  69.2 5.1 %collective-permute-start.10 = (f32[9,512]{1,0:T(8,128)S(1)}, f32[9,512]{1,0:T(8,128)S(1)}, u32[]{:S(2)}, u32[]{:S(2)}) collective-permute-start(f32[9,512]{1,0:T(8,128)S(1)} %get-tuple-element.57), channel_id=1, source_target_pairs={{48,0},{49,1},{50,2},{51,3},{52,4},{53,5},{54,6},{55,7},{56,8},{57... | collective-permute-start | bytes 55304 | tf_op jit(solution)/shard_map/ppermute | solution.py:280
  69.2 5.1 %collective-permute-start.11 = (f32[9,512]{1,0:T(8,128)S(1)}, f32[9,512]{1,0:T(8,128)S(1)}, u32[]{:S(2)}, u32[]{:S(2)}) collective-permute-start(f32[9,512]{1,0:T(8,128)S(1)} %get-tuple-element.58), channel_id=1, source_target_pairs={{16,0},{17,1},{18,2},{19,3},{20,4},{21,5},{22,6},{23,7},{24,8},{25... | collective-permute-start | bytes 55304 | tf_op jit(solution)/shard_map/ppermute | solution.py:281
  74.4 4.9 %collective-permute-start.12 = (f32[3,512]{1,0:T(4,128)S(1)}, f32[3,512]{1,0:T(4,128)S(1)}, u32[]{:S(2)}, u32[]{:S(2)}) collective-permute-start(f32[3,512]{1,0:T(4,128)S(1)} %get-tuple-element.60), channel_id=1, source_target_pairs={{12,0},{13,1},{14,2},{15,3},{0,4},{1,5},{2,6},{3,7},{4,8},{5,9},{6... | collective-permute-start | bytes 18440 | tf_op jit(solution)/shard_map/ppermute | solution.py:280
  75.9 3.7 %collective-permute-start.13 = (f32[3,512]{1,0:T(4,128)S(1)}, f32[3,512]{1,0:T(4,128)S(1)}, u32[]{:S(2)}, u32[]{:S(2)}) collective-permute-start(f32[3,512]{1,0:T(4,128)S(1)} %get-tuple-element.59), channel_id=1, source_target_pairs={{4,0},{5,1},{6,2},{7,3},{8,4},{9,5},{10,6},{11,7},{12,8},{13,9},{1... | collective-permute-start | bytes 18440 | tf_op jit(solution)/shard_map/ppermute | solution.py:281
  79.6 8.2 %collective-permute-start.14 = (f32[1,512]{1,0:T(1,128)S(1)}, f32[1,512]{1,0:T(1,128)S(1)}, u32[]{:S(2)}, u32[]{:S(2)}) collective-permute-start(f32[1,512]{1,0:T(1,128)S(1)} %get-tuple-element.62), channel_id=1, source_target_pairs={{3,0},{0,1},{1,2},{2,3},{7,4},{4,5},{5,6},{6,7},{11,8},{8,9},{9,10... | collective-permute-start | bytes 6152 | tf_op jit(solution)/shard_map/ppermute | solution.py:280
  82.7 5.1 %collective-permute-start.15 = (f32[1,512]{1,0:T(1,128)S(1)}, f32[1,512]{1,0:T(1,128)S(1)}, u32[]{:S(2)}, u32[]{:S(2)}) collective-permute-start(f32[1,512]{1,0:T(1,128)S(1)} %get-tuple-element.61), channel_id=1, source_target_pairs={{1,0},{2,1},{3,2},{0,3},{5,4},{6,5},{7,6},{4,7},{9,8},{10,9},{11,1... | collective-permute-start | bytes 6152 | tf_op jit(solution)/shard_map/ppermute | solution.py:281

commit v5 on v4

--- a/solution.py
+++ b/solution.py
@@ -16,21 +16,21 @@
 NORM_PARTS = 2
 
 PLAN = [
-    ((0, 0, 1), (0, 0, 0)),
-    ((3, 1, 0), (0, 0, 0)),
-    ((0, 3, 1), (0, 0, 1)),
-    ((3, 0, 3), (0, 0, 0)),
+    ((0, 1, 0), (0, 0, 0)),
+    ((3, 0, 1), (0, 0, 0)),
+    ((0, 1, 3), (0, 1, 0)),
+    ((3, 3, 0), (0, 0, 0)),
     ((1, 0, 0), (0, 0, 0)),
-    ((3, 1, 3), (3, 1, 0)),
-    ((3, 1, 1), (3, 1, 0)),
-    ((1, 3, 1), (0, 3, 1)),
-    ((3, 3, 3), (3, 0, 3)),
-    ((1, 1, 0), (1, 0, 0)),
+    ((3, 3, 1), (3, 0, 1)),
+    ((3, 1, 1), (3, 0, 1)),
+    ((1, 1, 3), (0, 1, 3)),
+    ((3, 3, 3), (3, 3, 0)),
+    ((1, 0, 1), (1, 0, 0)),
 ]
 OFFSETS = [(0, 0, 0)] + [d for d, _ in PLAN]
-STAGES = [2, 4, 7, 9, 10]
-GATES = {(0, 3, 1): 0, (1, 3, 1): 1, (1, 1, 0): 2}
-AFTER = {(1, 0, 0): (0, 0, 1), (3, 0, 3): (0, 0, 1)}
+STAGES = [2, 4, 5, 7, 9, 10]
+GATES = {(0, 1, 3): 0, (1, 1, 3): 1, (1, 0, 1): 2}
+AFTER = {(1, 0, 0): (0, 1, 0), (3, 3, 0): (0, 1, 0)}
 
 
 def turned(d):

time: 89.4 us -> 89.2 us (level)
    pallas_call x5 -> x6, Pallas kernels: 22.5 us -> 23.3 us  [on_device(): pl.pallas_call(functools.partial(pair_kernel, new=new, start=start, steps...]
  transfers between devices with their start and end apart: 16 -> 16, of which waited for: 7 -> 5; matrix products, arithmetic and copies ran while one was open for 1% -> 1% of each run, Pallas kernels for 24% -> 25%
where the time goes in v5:
time: 89.2 us; the launch traced here: 88.3 us
  starting transfers between devices  39.1 us (44%)
  Pallas kernels  26 us (29%)
  waiting for transfers between devices  21.1 us (24%)
    ppermute x10, starting transfers between devices, on_device(): held[d] = lax.ppermute(sent, ('clus', 'help'), moves(sub(d, source)))  25.6 us
    pallas_call x6, Pallas kernels, on_device(): pl.pallas_call(functools.partial(pair_kernel, new=new, start=start, steps...  23.3 us
    ppermute x10, waiting for transfers between devices, on_device(): held[d] = lax.ppermute(sent, ('clus', 'help'), moves(sub(d, source)))  16 us
    ppermute x3, starting transfers between devices, on_device(): behind = lax.ppermute(behind, ('clus', 'help'), moves(step))  8.99 us
    ppermute x3, waiting for transfers between devices, on_device(): ahead = lax.ppermute(ahead, ('clus', 'help'), moves(back))  4.99 us
    ppermute x3, starting transfers between devices, on_device(): ahead = lax.ppermute(ahead, ('clus', 'help'), moves(back))  4.5 us
  transfers between devices with their start and end apart: 16, of which 5 were waited for; matrix products, arithmetic and copies ran while one was open for 1% of the time, Pallas kernels for 25%

profile of v5, /device:TPU:0, one launch (start us, length us, event | category | flops | bytes accessed | tf_op | source)
XLA Modules:
  0.0 88.3 jit_solution(10848394983694814568)
XLA Ops:
  0.7 1.5 %shard_map.46.t_ref = bf16[528,1024]{1,0:T(8,128)(2,1)S(1)} custom-call(s32[1]{0:T(128)S(6)} %convert_element_type.3.alive, bf16[512,1024]{1,0:T(8,128)(2,1)} %bitcast.7, s32[1,512]{1,0:T(1,128)} %bitcast.8), custom_call_target="tpu_custom_call" | custom-call | tf_op jit(solution)/shard_map/pallas_call | solution.py:223
  2.2 3.2 %collective-permute-start = (bf16[528,1024]{1,0:T(8,128)(2,1)S(1)}, bf16[528,1024]{1,0:T(8,128)(2,1)S(1)}, u32[]{:S(2)}, u32[]{:S(2)}) collective-permute-start(bf16[528,1024]{1,0:T(8,128)(2,1)S(1)} %shard_map.46.t_ref), channel_id=1, source_target_pairs={{4,0},{5,1},{6,2},{7,3},{8,4},{9,5},{10,6},{11,7},{12,8},{13,9},{1... | collective-permute-start | bytes 3244040 | tf_op jit(solution)/shard_map/ppermute | solution.py:252
  5.3 4.1 %collective-permute-start.1 = (bf16[528,1024]{1,0:T(8,128)(2,1)S(1)}, bf16[528,1024]{1,0:T(8,128)(2,1)S(1)}, u32[]{:S(2)}, u32[]{:S(2)}) collective-permute-start(bf16[528,1024]{1,0:T(8,128)(2,1)S(1)} %shard_map.46.t_ref), channel_id=1, source_target_pairs={{49,0},{50,1},{51,2},{48,3},{53,4},{54,5},{55,6},{52,7},{57,8},{58... | collective-permute-start | bytes 3244040 | tf_op jit(solution)/shard_map/ppermute | solution.py:252
  9.4 0.7 dynamic-slice_bitcast_fusion.tab
  10.1 1.2 %shard_map.47 = (bf16[11,512,1024]{2,1,0:T(8,128)(2,1)S(1)}, f32[11,512,128]{2,1,0:T(8,128)S(1)}, f32[11,2,8,256]{3,2,1,0:T(8,128)S(1)}, s32[8,128]{1,0:T(8,128)S(1)}) custom-call(bf16[528,1024]{1,0:T(8,128)(2,1)S(1)} %shard_map.46.t_ref, s32[105]{0:T(128)S(1)} %dynamic-slice_bitcast_fusion.tab), custom_call_target="tpu_custom_call" | custom-call | flops 1000 | bytes 1000 | tf_op jit(solution)/shard_map/pallas_call | solution.py:235
  11.4 6.6 %collective-permute-done.refs_0_ = bf16[528,1024]{1,0:T(8,128)(2,1)S(1)} collective-permute-done((bf16[528,1024]{1,0:T(8,128)(2,1)S(1)}, bf16[528,1024]{1,0:T(8,128)(2,1)S(1)}, u32[]{:S(2)}, u32[]{:S(2)}) %collective-permute-start) | collective-permute-done | bytes 1081376 | tf_op jit(solution)/shard_map/ppermute | solution.py:252
  18.0 1.5 %collective-permute-start.2 = (bf16[528,1024]{1,0:T(8,128)(2,1)S(1)}, bf16[528,1024]{1,0:T(8,128)(2,1)S(1)}, u32[]{:S(2)}, u32[]{:S(2)}) collective-permute-start(bf16[528,1024]{1,0:T(8,128)(2,1)S(1)} %collective-permute-done.refs_0_), channel_id=1, source_target_pairs={{3,0},{0,1},{1,2},{2,3},{7,4},{4,5},{5,6},{6,7},{11,8},{8,9},{9,10... | collective-permute-start | bytes 3244040 | tf_op jit(solution)/shard_map/ppermute | solution.py:252
  19.5 2.4 %collective-permute-start.3 = (bf16[528,1024]{1,0:T(8,128)(2,1)S(1)}, bf16[528,1024]{1,0:T(8,128)(2,1)S(1)}, u32[]{:S(2)}, u32[]{:S(2)}) collective-permute-start(bf16[528,1024]{1,0:T(8,128)(2,1)S(1)} %shard_map.46.t_ref), channel_id=1, source_target_pairs={{60,0},{61,1},{62,2},{63,3},{48,4},{49,5},{50,6},{51,7},{52,8},{53... | collective-permute-start | bytes 3244040 | tf_op jit(solution)/shard_map/ppermute | solution.py:252
  21.9 1.6 %collective-permute-start.4 = (bf16[528,1024]{1,0:T(8,128)(2,1)S(1)}, bf16[528,1024]{1,0:T(8,128)(2,1)S(1)}, u32[]{:S(2)}, u32[]{:S(2)}) collective-permute-start(bf16[528,1024]{1,0:T(8,128)(2,1)S(1)} %shard_map.46.t_ref), channel_id=1, source_target_pairs={{16,0},{17,1},{18,2},{19,3},{20,4},{21,5},{22,6},{23,7},{24,8},{25... | collective-permute-start | bytes 3244040 | tf_op jit(solution)/shard_map/ppermute | solution.py:252
  23.5 0.0 collective-permute-done.1.refs_1_
  23.5 1.3 %collective-permute-start.5 = (bf16[528,1024]{1,0:T(8,128)(2,1)S(1)}, bf16[528,1024]{1,0:T(8,128)(2,1)S(1)}, u32[]{:S(2)}, u32[]{:S(2)}) collective-permute-start(bf16[528,1024]{1,0:T(8,128)(2,1)S(1)} %collective-permute-done.1.refs_1_), channel_id=1, source_target_pairs={{12,0},{13,1},{14,2},{15,3},{0,4},{1,5},{2,6},{3,7},{4,8},{5,9},{6... | collective-permute-start | bytes 3244040 | tf_op jit(solution)/shard_map/ppermute | solution.py:252
  24.8 2.4 %collective-permute-start.6 = (bf16[528,1024]{1,0:T(8,128)(2,1)S(1)}, bf16[528,1024]{1,0:T(8,128)(2,1)S(1)}, u32[]{:S(2)}, u32[]{:S(2)}) collective-permute-start(bf16[528,1024]{1,0:T(8,128)(2,1)S(1)} %collective-permute-done.1.refs_1_), channel_id=1, source_target_pairs={{4,0},{5,1},{6,2},{7,3},{8,4},{9,5},{10,6},{11,7},{12,8},{13,9},{1... | collective-permute-start | bytes 3244040 | tf_op jit(solution)/shard_map/ppermute | solution.py:252
  27.2 2.5 %shard_map.48 = (bf16[11,512,1024]{2,1,0:T(8,128)(2,1)S(1)}, f32[11,512,128]{2,1,0:T(8,128)S(1)}, f32[11,2,8,256]{3,2,1,0:T(8,128)S(1)}, s32[8,128]{1,0:T(8,128)S(1)}) custom-call(s32[105]{0:T(128)S(1)} %dynamic-slice_bitcast_fusion.tab, s32[8,128]{1,0:T(8,128)S(1)} %get-tuple-element.36.turn_in, ...), custom_call_target="tpu_custom_call", output_to_operand_aliasing={{0}: (4, {}), {1}: (5, {}), {2}: (6, {})} | custom-call | flops 1000 | bytes 1000 | tf_op jit(solution)/shard_map/pallas_call | solution.py:261
  29.8 9.4 %collective-permute-done.2.refs_0_ = bf16[528,1024]{1,0:T(8,128)(2,1)S(1)} collective-permute-done((bf16[528,1024]{1,0:T(8,128)(2,1)S(1)}, bf16[528,1024]{1,0:T(8,128)(2,1)S(1)}, u32[]{:S(2)}, u32[]{:S(2)}) %collective-permute-start.2) | collective-permute-done | bytes 1081376 | tf_op jit(solution)/shard_map/ppermute | solution.py:252
  39.1 5.1 %collective-permute-start.7 = (bf16[528,1024]{1,0:T(8,128)(2,1)S(1)}, bf16[528,1024]{1,0:T(8,128)(2,1)S(1)}, u32[]{:S(2)}, u32[]{:S(2)}) collective-permute-start(bf16[528,1024]{1,0:T(8,128)(2,1)S(1)} %collective-permute-done.2.refs_0_), channel_id=1, source_target_pairs={{16,0},{17,1},{18,2},{19,3},{20,4},{21,5},{22,6},{23,7},{24,8},{25... | collective-permute-start | bytes 3244040 | tf_op jit(solution)/shard_map/ppermute | solution.py:252
  44.3 0.0 collective-permute-done.3.refs_1_
  44.3 0.6 collective-permute-start.8
  44.9 4.7 %shard_map.49 = (bf16[11,512,1024]{2,1,0:T(8,128)(2,1)S(1)}, f32[11,512,128]{2,1,0:T(8,128)S(1)}, f32[11,2,8,256]{3,2,1,0:T(8,128)S(1)}, s32[8,128]{1,0:T(8,128)S(1)}) custom-call(s32[105]{0:T(128)S(1)} %dynamic-slice_bitcast_fusion.tab, s32[8,128]{1,0:T(8,128)S(1)} %get-tuple-element.40.turn_in, ...), custom_call_target="tpu_custom_call", output_to_operand_aliasing={{0}: (4, {}), {1}: (5, {}), {2}: (6, {})} | custom-call | flops 1000 | bytes 1000 | tf_op jit(solution)/shard_map/pallas_call | solution.py:261
  49.6 0.0 collective-permute-done.4.refs_0_
  49.6 3.4 %collective-permute-start.9 = (bf16[528,1024]{1,0:T(8,128)(2,1)S(1)}, bf16[528,1024]{1,0:T(8,128)(2,1)S(1)}, u32[]{:S(2)}, u32[]{:S(2)}) collective-permute-start(bf16[528,1024]{1,0:T(8,128)(2,1)S(1)} %collective-permute-done.4.refs_0_), channel_id=1, source_target_pairs={{1,0},{2,1},{3,2},{0,3},{5,4},{6,5},{7,6},{4,7},{9,8},{10,9},{11,1... | collective-permute-start | bytes 3244040 | tf_op jit(solution)/shard_map/ppermute | solution.py:252
  53.0 3.6 %shard_map.50 = (bf16[11,512,1024]{2,1,0:T(8,128)(2,1)S(1)}, f32[11,512,128]{2,1,0:T(8,128)S(1)}, f32[11,2,8,256]{3,2,1,0:T(8,128)S(1)}, s32[8,128]{1,0:T(8,128)S(1)}) custom-call(s32[105]{0:T(128)S(1)} %dynamic-slice_bitcast_fusion.tab, s32[8,128]{1,0:T(8,128)S(1)} %get-tuple-element.46.turn_in, ...), custom_call_target="tpu_custom_call", output_to_operand_aliasing={{0}: (3, {}), {1}: (4, {}), {2}: (5, {})} | custom-call | flops 1000 | bytes 1000 | tf_op jit(solution)/shard_map/pallas_call | solution.py:261
  56.6 0.0 collective-permute-done.5.refs_0_
  56.6 0.0 collective-permute-done.6.refs_1_
  56.6 4.6 %shard_map.51 = (bf16[11,512,1024]{2,1,0:T(8,128)(2,1)S(1)}, f32[11,512,128]{2,1,0:T(8,128)S(1)}, f32[11,2,8,256]{3,2,1,0:T(8,128)S(1)}, s32[8,128]{1,0:T(8,128)S(1)}) custom-call(s32[105]{0:T(128)S(1)} %dynamic-slice_bitcast_fusion.tab, s32[8,128]{1,0:T(8,128)S(1)} %get-tuple-element.50.turn_in, ...), custom_call_target="tpu_custom_call", output_to_operand_aliasing={{0}: (4, {}), {1}: (5, {}), {2}: (6, {})} | custom-call | flops 1000 | bytes 1000 | tf_op jit(solution)/shard_map/pallas_call | solution.py:261
  61.2 0.0 collective-permute-done.7.refs_0_
  61.2 0.0 collective-permute-done.8.refs_1_
  61.2 5.1 %shard_map.52 = (bf16[11,512,1024]{2,1,0:T(8,128)(2,1)S(1)}, f32[11,512,128]{2,1,0:T(8,128)S(1)}, f32[11,2,8,256]{3,2,1,0:T(8,128)S(1)}, s32[8,128]{1,0:T(8,128)S(1)}) custom-call(s32[105]{0:T(128)S(1)} %dynamic-slice_bitcast_fusion.tab, s32[8,128]{1,0:T(8,128)S(1)} %get-tuple-element.54.turn_in, ...), custom_call_target="tpu_custom_call", output_to_operand_aliasing={{0}: (4, {}), {1}: (5, {}), {2}: (6, {})} | custom-call | flops 1000 | bytes 1000 | tf_op jit(solution)/shard_map/pallas_call | solution.py:261
  66.3 0.0 collective-permute-done.9.refs_0_
  66.3 2.8 %shard_map.53 = (bf16[11,512,1024]{2,1,0:T(8,128)(2,1)S(1)}, f32[11,512,128]{2,1,0:T(8,128)S(1)}, f32[11,2,8,256]{3,2,1,0:T(8,128)S(1)}, s32[8,128]{1,0:T(8,128)...) custom-call(s32[105]{0:T(128)S(1)} %dynamic-slice_bitcast_fusion.tab, ...), custom_call_target="tpu_custom_call", output_to_operand_aliasing={{0}: (3, {}), {1}: (4, {}), {2}: (5, {})} | custom-call | flops 1000 | bytes 1000 | tf_op jit(solution)/shard_map/pallas_call | solution.py:261
  69.1 0.0 collective-permute-start.10
  69.1 3.2 %collective-permute-start.11 = (f32[9,512]{1,0:T(8,128)S(1)}, f32[9,512]{1,0:T(8,128)S(1)}, u32[]{:S(2)}, u32[]{:S(2)}) collective-permute-start(f32[9,512]{1,0:T(8,128)S(1)} %get-tuple-element.66), channel_id=1, source_target_pairs={{16,0},{17,1},{18,2},{19,3},{20,4},{21,5},{22,6},{23,7},{24,8},{25... | collective-permute-start | bytes 55304 | tf_op jit(solution)/shard_map/ppermute | solution.py:281
  72.3 1.9 %collective-permute-done.10 = f32[9,512]{1,0:T(8,128)S(1)} collective-permute-done((f32[9,512]{1,0:T(8,128)S(1)}, f32[9,512]{1,0:T(8,128)S(1)}, u32[]{:S(2)}, u32[]{:S(2)}) %collective-permute-start.10) | collective-permute-done | bytes 18464 | tf_op jit(solution)/shard_map/ppermute | solution.py:280
  74.2 0.0 collective-permute-done.11
  74.3 3.2 %collective-permute-start.12 = (f32[3,512]{1,0:T(4,128)S(1)}, f32[3,512]{1,0:T(4,128)S(1)}, u32[]{:S(2)}, u32[]{:S(2)}) collective-permute-start(f32[3,512]{1,0:T(4,128)S(1)} %get-tuple-element.68), channel_id=1, source_target_pairs={{12,0},{13,1},{14,2},{15,3},{0,4},{1,5},{2,6},{3,7},{4,8},{5,9},{6... | collective-permute-start | bytes 18440 | tf_op jit(solution)/shard_map/ppermute | solution.py:280
  77.4 3.8 %collective-permute-start.13 = (f32[3,512]{1,0:T(4,128)S(1)}, f32[3,512]{1,0:T(4,128)S(1)}, u32[]{:S(2)}, u32[]{:S(2)}) collective-permute-start(f32[3,512]{1,0:T(4,128)S(1)} %get-tuple-element.67), channel_id=1, source_target_pairs={{4,0},{5,1},{6,2},{7,3},{8,4},{9,5},{10,6},{11,7},{12,8},{13,9},{1... | collective-permute-start | bytes 18440 | tf_op jit(solution)/shard_map/ppermute | solution.py:281
  81.2 1.5 %collective-permute-done.12 = f32[3,512]{1,0:T(4,128)S(1)} collective-permute-done((f32[3,512]{1,0:T(4,128)S(1)}, f32[3,512]{1,0:T(4,128)S(1)}, u32[]{:S(2)}, u32[]{:S(2)}) %collective-permute-start.12) | collective-permute-done | bytes 6176 | tf_op jit(solution)/shard_map/ppermute | solution.py:280
  82.8 0.0 collective-permute-done.13
  82.8 1.3 %collective-permute-start.14 = (f32[1,512]{1,0:T(1,128)S(1)}, f32[1,512]{1,0:T(1,128)S(1)}, u32[]{:S(2)}, u32[]{:S(2)}) collective-permute-start(f32[1,512]{1,0:T(1,128)S(1)} %get-tuple-element.70), channel_id=1, source_target_pairs={{3,0},{0,1},{1,2},{2,3},{7,4},{4,5},{5,6},{6,7},{11,8},{8,9},{9,10... | collective-permute-start | bytes 6152 | tf_op jit(solution)/shard_map/ppermute | solution.py:280
  84.1 2.0 %collective-permute-start.15 = (f32[1,512]{1,0:T(1,128)S(1)}, f32[1,512]{1,0:T(1,128)S(1)}, u32[]{:S(2)}, u32[]{:S(2)}) collective-permute-start(f32[1,512]{1,0:T(1,128)S(1)} %get-tuple-element.69), channel_id=1, source_target_pairs={{1,0},{2,1},{3,2},{0,3},{5,4},{6,5},{7,6},{4,7},{9,8},{10,9},{11,1... | collective-permute-start | bytes 6152 | tf_op jit(solution)/shard_map/ppermute | solution.py:281
  86.1 1.6 %collective-permute-done.14 = f32[1,512]{1,0:T(1,128)S(1)} collective-permute-done((f32[1,512]{1,0:T(1,128)S(1)}, f32[1,512]{1,0:T(1,128)S(1)}, u32[]{:S(2)}, u32[]{:S(2)}) %collective-permute-start.14) | collective-permute-done | bytes 2080 | tf_op jit(solution)/shard_map/ppermute | solution.py:280
  87.6 0.0 collective-permute-done.15
  87.7 0.6 fusion
  (4 shorter events, 0.0 us)
Async XLA Ops:
  2.2 15.8 %collective-permute-start = (bf16[528,1024]{1,0:T(8,128)(2,1)S(1)}, bf16[528,1024]{1,0:T(8,128)(2,1)S(1)}, u32[]{:S(2)}, u32[]{:S(2)}) collective-permute-start(bf16[528,1024]{1,0:T(8,128)(2,1)S(1)} %shard_map.46.t_ref), channel_id=1, source_target_pairs={{4,0},{5,1},{6,2},{7,3},{8,4},{9,5},{10,6},{11,7},{12,8},{13,9},{1... | collective-permute-start | bytes 3244040 | tf_op jit(solution)/shard_map/ppermute | solution.py:252
  5.3 18.2 %collective-permute-start.1 = (bf16[528,1024]{1,0:T(8,128)(2,1)S(1)}, bf16[528,1024]{1,0:T(8,128)(2,1)S(1)}, u32[]{:S(2)}, u32[]{:S(2)}) collective-permute-start(bf16[528,1024]{1,0:T(8,128)(2,1)S(1)} %shard_map.46.t_ref), channel_id=1, source_target_pairs={{49,0},{50,1},{51,2},{48,3},{53,4},{54,5},{55,6},{52,7},{57,8},{58... | collective-permute-start | bytes 3244040 | tf_op jit(solution)/shard_map/ppermute | solution.py:252
  18.0 21.2 %collective-permute-start.2 = (bf16[528,1024]{1,0:T(8,128)(2,1)S(1)}, bf16[528,1024]{1,0:T(8,128)(2,1)S(1)}, u32[]{:S(2)}, u32[]{:S(2)}) collective-permute-start(bf16[528,1024]{1,0:T(8,128)(2,1)S(1)} %collective-permute-done.refs_0_), channel_id=1, source_target_pairs={{3,0},{0,1},{1,2},{2,3},{7,4},{4,5},{5,6},{6,7},{11,8},{8,9},{9,10... | collective-permute-start | bytes 3244040 | tf_op jit(solution)/shard_map/ppermute | solution.py:252
  19.5 24.8 %collective-permute-start.3 = (bf16[528,1024]{1,0:T(8,128)(2,1)S(1)}, bf16[528,1024]{1,0:T(8,128)(2,1)S(1)}, u32[]{:S(2)}, u32[]{:S(2)}) collective-permute-start(bf16[528,1024]{1,0:T(8,128)(2,1)S(1)} %shard_map.46.t_ref), channel_id=1, source_target_pairs={{60,0},{61,1},{62,2},{63,3},{48,4},{49,5},{50,6},{51,7},{52,8},{53... | collective-permute-start | bytes 3244040 | tf_op jit(solution)/shard_map/ppermute | solution.py:252
  21.9 27.7 %collective-permute-start.4 = (bf16[528,1024]{1,0:T(8,128)(2,1)S(1)}, bf16[528,1024]{1,0:T(8,128)(2,1)S(1)}, u32[]{:S(2)}, u32[]{:S(2)}) collective-permute-start(bf16[528,1024]{1,0:T(8,128)(2,1)S(1)} %shard_map.46.t_ref), channel_id=1, source_target_pairs={{16,0},{17,1},{18,2},{19,3},{20,4},{21,5},{22,6},{23,7},{24,8},{25... | collective-permute-start | bytes 3244040 | tf_op jit(solution)/shard_map/ppermute | solution.py:252
  23.5 33.1 %collective-permute-start.5 = (bf16[528,1024]{1,0:T(8,128)(2,1)S(1)}, bf16[528,1024]{1,0:T(8,128)(2,1)S(1)}, u32[]{:S(2)}, u32[]{:S(2)}) collective-permute-start(bf16[528,1024]{1,0:T(8,128)(2,1)S(1)} %collective-permute-done.1.refs_1_), channel_id=1, source_target_pairs={{12,0},{13,1},{14,2},{15,3},{0,4},{1,5},{2,6},{3,7},{4,8},{5,9},{6... | collective-permute-start | bytes 3244040 | tf_op jit(solution)/shard_map/ppermute | solution.py:252
  24.8 31.8 %collective-permute-start.6 = (bf16[528,1024]{1,0:T(8,128)(2,1)S(1)}, bf16[528,1024]{1,0:T(8,128)(2,1)S(1)}, u32[]{:S(2)}, u32[]{:S(2)}) collective-permute-start(bf16[528,1024]{1,0:T(8,128)(2,1)S(1)} %collective-permute-done.1.refs_1_), channel_id=1, source_target_pairs={{4,0},{5,1},{6,2},{7,3},{8,4},{9,5},{10,6},{11,7},{12,8},{13,9},{1... | collective-permute-start | bytes 3244040 | tf_op jit(solution)/shard_map/ppermute | solution.py:252
  39.1 22.0 %collective-permute-start.7 = (bf16[528,1024]{1,0:T(8,128)(2,1)S(1)}, bf16[528,1024]{1,0:T(8,128)(2,1)S(1)}, u32[]{:S(2)}, u32[]{:S(2)}) collective-permute-start(bf16[528,1024]{1,0:T(8,128)(2,1)S(1)} %collective-permute-done.2.refs_0_), channel_id=1, source_target_pairs={{16,0},{17,1},{18,2},{19,3},{20,4},{21,5},{22,6},{23,7},{24,8},{25... | collective-permute-start | bytes 3244040 | tf_op jit(solution)/shard_map/ppermute | solution.py:252
  44.3 16.9 %collective-permute-start.8 = (bf16[528,1024]{1,0:T(8,128)(2,1)S(1)}, bf16[528,1024]{1,0:T(8,128)(2,1)S(1)}, u32[]{:S(2)}, u32[]{:S(2)}) collective-permute-start(bf16[528,1024]{1,0:T(8,128)(2,1)S(1)} %collective-permute-done.3.refs_1_), channel_id=1, source_target_pairs={{3,0},{0,1},{1,2},{2,3},{7,4},{4,5},{5,6},{6,7},{11,8},{8,9},{9,10... | collective-permute-start | bytes 3244040 | tf_op jit(solution)/shard_map/ppermute | solution.py:252
  49.6 16.7 %collective-permute-start.9 = (bf16[528,1024]{1,0:T(8,128)(2,1)S(1)}, bf16[528,1024]{1,0:T(8,128)(2,1)S(1)}, u32[]{:S(2)}, u32[]{:S(2)}) collective-permute-start(bf16[528,1024]{1,0:T(8,128)(2,1)S(1)} %collective-permute-done.4.refs_0_), channel_id=1, source_target_pairs={{1,0},{2,1},{3,2},{0,3},{5,4},{6,5},{7,6},{4,7},{9,8},{10,9},{11,1... | collective-permute-start | bytes 3244040 | tf_op jit(solution)/shard_map/ppermute | solution.py:252
  69.1 5.1 %collective-permute-start.10 = (f32[9,512]{1,0:T(8,128)S(1)}, f32[9,512]{1,0:T(8,128)S(1)}, u32[]{:S(2)}, u32[]{:S(2)}) collective-permute-start(f32[9,512]{1,0:T(8,128)S(1)} %get-tuple-element.65), channel_id=1, source_target_pairs={{48,0},{49,1},{50,2},{51,3},{52,4},{53,5},{54,6},{55,7},{56,8},{57... | collective-permute-start | bytes 55304 | tf_op jit(solution)/shard_map/ppermute | solution.py:280
  69.1 5.1 %collective-permute-start.11 = (f32[9,512]{1,0:T(8,128)S(1)}, f32[9,512]{1,0:T(8,128)S(1)}, u32[]{:S(2)}, u32[]{:S(2)}) collective-permute-start(f32[9,512]{1,0:T(8,128)S(1)} %get-tuple-element.66), channel_id=1, source_target_pairs={{16,0},{17,1},{18,2},{19,3},{20,4},{21,5},{22,6},{23,7},{24,8},{25... | collective-permute-start | bytes 55304 | tf_op jit(solution)/shard_map/ppermute | solution.py:281
  74.3 8.5 %collective-permute-start.12 = (f32[3,512]{1,0:T(4,128)S(1)}, f32[3,512]{1,0:T(4,128)S(1)}, u32[]{:S(2)}, u32[]{:S(2)}) collective-permute-start(f32[3,512]{1,0:T(4,128)S(1)} %get-tuple-element.68), channel_id=1, source_target_pairs={{12,0},{13,1},{14,2},{15,3},{0,4},{1,5},{2,6},{3,7},{4,8},{5,9},{6... | collective-permute-start | bytes 18440 | tf_op jit(solution)/shard_map/ppermute | solution.py:280
  77.4 5.3 %collective-permute-start.13 = (f32[3,512]{1,0:T(4,128)S(1)}, f32[3,512]{1,0:T(4,128)S(1)}, u32[]{:S(2)}, u32[]{:S(2)}) collective-permute-start(f32[3,512]{1,0:T(4,128)S(1)} %get-tuple-element.67), channel_id=1, source_target_pairs={{4,0},{5,1},{6,2},{7,3},{8,4},{9,5},{10,6},{11,7},{12,8},{13,9},{1... | collective-permute-start | bytes 18440 | tf_op jit(solution)/shard_map/ppermute | solution.py:281
  82.8 4.9 %collective-permute-start.14 = (f32[1,512]{1,0:T(1,128)S(1)}, f32[1,512]{1,0:T(1,128)S(1)}, u32[]{:S(2)}, u32[]{:S(2)}) collective-permute-start(f32[1,512]{1,0:T(1,128)S(1)} %get-tuple-element.70), channel_id=1, source_target_pairs={{3,0},{0,1},{1,2},{2,3},{7,4},{4,5},{5,6},{6,7},{11,8},{8,9},{9,10... | collective-permute-start | bytes 6152 | tf_op jit(solution)/shard_map/ppermute | solution.py:280
  84.1 3.6 %collective-permute-start.15 = (f32[1,512]{1,0:T(1,128)S(1)}, f32[1,512]{1,0:T(1,128)S(1)}, u32[]{:S(2)}, u32[]{:S(2)}) collective-permute-start(f32[1,512]{1,0:T(1,128)S(1)} %get-tuple-element.69), channel_id=1, source_target_pairs={{1,0},{2,1},{3,2},{0,3},{5,4},{6,5},{7,6},{4,7},{9,8},{10,9},{11,1... | collective-permute-start | bytes 6152 | tf_op jit(solution)/shard_map/ppermute | solution.py:281

commit v6 on v5

--- a/solution.py
+++ b/solution.py
@@ -28,8 +28,8 @@
     ((1, 0, 1), (1, 0, 0)),
 ]
 OFFSETS = [(0, 0, 0)] + [d for d, _ in PLAN]
-STAGES = [2, 4, 5, 7, 9, 10]
-GATES = {(0, 1, 3): 0, (1, 1, 3): 1, (1, 0, 1): 2}
+STAGES = [2, 3, 4, 5, 7, 9, 10]
+GATES = {(0, 1, 3): 0, (1, 1, 3): 1, (1, 0, 1): 3}
 AFTER = {(1, 0, 0): (0, 1, 0), (3, 3, 0): (0, 1, 0)}
 
 

time: 89.2 us -> 89.9 us (level)
    pallas_call x6 -> x7, Pallas kernels: 23.3 us -> 24 us  [on_device(): pl.pallas_call(functools.partial(pair_kernel, new=new, start=start, steps...]
  transfers between devices with their start and end apart: 16 -> 16, of which waited for: 5 -> 6; matrix products, arithmetic and copies ran while one was open for 1% -> 1% of each run, Pallas kernels for 25% -> 25%
where the time goes in v6:
time: 89.9 us; the launch traced here: 89 us
  starting transfers between devices  38.9 us (43%)
  Pallas kernels  26.7 us (30%)
  waiting for transfers between devices  21.3 us (24%)
    ppermute x10, starting transfers between devices, on_device(): held[d] = lax.ppermute(sent, ('clus', 'help'), moves(sub(d, source)))  25.7 us
    pallas_call x7, Pallas kernels, on_device(): pl.pallas_call(functools.partial(pair_kernel, new=new, start=start, steps...  24 us
    ppermute x10, waiting for transfers between devices, on_device(): held[d] = lax.ppermute(sent, ('clus', 'help'), moves(sub(d, source)))  16 us
    ppermute x3, starting transfers between devices, on_device(): behind = lax.ppermute(behind, ('clus', 'help'), moves(step))  8.98 us
    ppermute x3, waiting for transfers between devices, on_device(): ahead = lax.ppermute(ahead, ('clus', 'help'), moves(back))  5.18 us
    ppermute x3, starting transfers between devices, on_device(): ahead = lax.ppermute(ahead, ('clus', 'help'), moves(back))  4.3 us
  transfers between devices with their start and end apart: 16, of which 6 were waited for; matrix products, arithmetic and copies ran while one was open for 1% of the time, Pallas kernels for 25%

profile of v6, /device:TPU:0, one launch (start us, length us, event | category | flops | bytes accessed | tf_op | source)
XLA Modules:
  0.0 89.0 jit_solution(449137504688365638)
XLA Ops:
  0.7 1.5 %shard_map.46.t_ref = bf16[528,1024]{1,0:T(8,128)(2,1)S(1)} custom-call(s32[1]{0:T(128)S(6)} %convert_element_type.3.alive, bf16[512,1024]{1,0:T(8,128)(2,1)} %bitcast.7, s32[1,512]{1,0:T(1,128)} %bitcast.8), custom_call_target="tpu_custom_call" | custom-call | tf_op jit(solution)/shard_map/pallas_call | solution.py:223
  2.2 3.2 %collective-permute-start = (bf16[528,1024]{1,0:T(8,128)(2,1)S(1)}, bf16[528,1024]{1,0:T(8,128)(2,1)S(1)}, u32[]{:S(2)}, u32[]{:S(2)}) collective-permute-start(bf16[528,1024]{1,0:T(8,128)(2,1)S(1)} %shard_map.46.t_ref), channel_id=1, source_target_pairs={{4,0},{5,1},{6,2},{7,3},{8,4},{9,5},{10,6},{11,7},{12,8},{13,9},{1... | collective-permute-start | bytes 3244040 | tf_op jit(solution)/shard_map/ppermute | solution.py:252
  5.3 4.1 %collective-permute-start.1 = (bf16[528,1024]{1,0:T(8,128)(2,1)S(1)}, bf16[528,1024]{1,0:T(8,128)(2,1)S(1)}, u32[]{:S(2)}, u32[]{:S(2)}) collective-permute-start(bf16[528,1024]{1,0:T(8,128)(2,1)S(1)} %shard_map.46.t_ref), channel_id=1, source_target_pairs={{49,0},{50,1},{51,2},{48,3},{53,4},{54,5},{55,6},{52,7},{57,8},{58... | collective-permute-start | bytes 3244040 | tf_op jit(solution)/shard_map/ppermute | solution.py:252
  9.4 0.7 dynamic-slice_bitcast_fusion.tab
  10.1 1.2 %shard_map.47 = (bf16[11,512,1024]{2,1,0:T(8,128)(2,1)S(1)}, f32[11,512,128]{2,1,0:T(8,128)S(1)}, f32[11,2,8,256]{3,2,1,0:T(8,128)S(1)}, s32[8,128]{1,0:T(8,128)S(1)}) custom-call(bf16[528,1024]{1,0:T(8,128)(2,1)S(1)} %shard_map.46.t_ref, s32[105]{0:T(128)S(1)} %dynamic-slice_bitcast_fusion.tab), custom_call_target="tpu_custom_call" | custom-call | flops 1000 | bytes 1000 | tf_op jit(solution)/shard_map/pallas_call | solution.py:235
  11.4 6.6 %collective-permute-done.refs_0_ = bf16[528,1024]{1,0:T(8,128)(2,1)S(1)} collective-permute-done((bf16[528,1024]{1,0:T(8,128)(2,1)S(1)}, bf16[528,1024]{1,0:T(8,128)(2,1)S(1)}, u32[]{:S(2)}, u32[]{:S(2)}) %collective-permute-start) | collective-permute-done | bytes 1081376 | tf_op jit(solution)/shard_map/ppermute | solution.py:252
  18.0 1.5 %collective-permute-start.2 = (bf16[528,1024]{1,0:T(8,128)(2,1)S(1)}, bf16[528,1024]{1,0:T(8,128)(2,1)S(1)}, u32[]{:S(2)}, u32[]{:S(2)}) collective-permute-start(bf16[528,1024]{1,0:T(8,128)(2,1)S(1)} %collective-permute-done.refs_0_), channel_id=1, source_target_pairs={{3,0},{0,1},{1,2},{2,3},{7,4},{4,5},{5,6},{6,7},{11,8},{8,9},{9,10... | collective-permute-start | bytes 3244040 | tf_op jit(solution)/shard_map/ppermute | solution.py:252
  19.5 2.4 %collective-permute-start.3 = (bf16[528,1024]{1,0:T(8,128)(2,1)S(1)}, bf16[528,1024]{1,0:T(8,128)(2,1)S(1)}, u32[]{:S(2)}, u32[]{:S(2)}) collective-permute-start(bf16[528,1024]{1,0:T(8,128)(2,1)S(1)} %shard_map.46.t_ref), channel_id=1, source_target_pairs={{60,0},{61,1},{62,2},{63,3},{48,4},{49,5},{50,6},{51,7},{52,8},{53... | collective-permute-start | bytes 3244040 | tf_op jit(solution)/shard_map/ppermute | solution.py:252
  21.9 1.6 %collective-permute-start.4 = (bf16[528,1024]{1,0:T(8,128)(2,1)S(1)}, bf16[528,1024]{1,0:T(8,128)(2,1)S(1)}, u32[]{:S(2)}, u32[]{:S(2)}) collective-permute-start(bf16[528,1024]{1,0:T(8,128)(2,1)S(1)} %shard_map.46.t_ref), channel_id=1, source_target_pairs={{16,0},{17,1},{18,2},{19,3},{20,4},{21,5},{22,6},{23,7},{24,8},{25... | collective-permute-start | bytes 3244040 | tf_op jit(solution)/shard_map/ppermute | solution.py:252
  23.5 0.0 collective-permute-done.1.refs_1_
  23.5 1.3 %collective-permute-start.5 = (bf16[528,1024]{1,0:T(8,128)(2,1)S(1)}, bf16[528,1024]{1,0:T(8,128)(2,1)S(1)}, u32[]{:S(2)}, u32[]{:S(2)}) collective-permute-start(bf16[528,1024]{1,0:T(8,128)(2,1)S(1)} %collective-permute-done.1.refs_1_), channel_id=1, source_target_pairs={{12,0},{13,1},{14,2},{15,3},{0,4},{1,5},{2,6},{3,7},{4,8},{5,9},{6... | collective-permute-start | bytes 3244040 | tf_op jit(solution)/shard_map/ppermute | solution.py:252
  24.8 2.4 %collective-permute-start.6 = (bf16[528,1024]{1,0:T(8,128)(2,1)S(1)}, bf16[528,1024]{1,0:T(8,128)(2,1)S(1)}, u32[]{:S(2)}, u32[]{:S(2)}) collective-permute-start(bf16[528,1024]{1,0:T(8,128)(2,1)S(1)} %collective-permute-done.1.refs_1_), channel_id=1, source_target_pairs={{4,0},{5,1},{6,2},{7,3},{8,4},{9,5},{10,6},{11,7},{12,8},{13,9},{1... | collective-permute-start | bytes 3244040 | tf_op jit(solution)/shard_map/ppermute | solution.py:252
  27.2 2.5 %shard_map.48 = (bf16[11,512,1024]{2,1,0:T(8,128)(2,1)S(1)}, f32[11,512,128]{2,1,0:T(8,128)S(1)}, f32[11,2,8,256]{3,2,1,0:T(8,128)S(1)}, s32[8,128]{1,0:T(8,128)S(1)}) custom-call(s32[105]{0:T(128)S(1)} %dynamic-slice_bitcast_fusion.tab, s32[8,128]{1,0:T(8,128)S(1)} %get-tuple-element.40.turn_in, ...), custom_call_target="tpu_custom_call", output_to_operand_aliasing={{0}: (4, {}), {1}: (5, {}), {2}: (6, {})} | custom-call | flops 1000 | bytes 1000 | tf_op jit(solution)/shard_map/pallas_call | solution.py:261
  29.8 9.4 %collective-permute-done.2.refs_0_ = bf16[528,1024]{1,0:T(8,128)(2,1)S(1)} collective-permute-done((bf16[528,1024]{1,0:T(8,128)(2,1)S(1)}, bf16[528,1024]{1,0:T(8,128)(2,1)S(1)}, u32[]{:S(2)}, u32[]{:S(2)}) %collective-permute-start.2) | collective-permute-done | bytes 1081376 | tf_op jit(solution)/shard_map/ppermute | solution.py:252
  39.1 5.1 %collective-permute-start.7 = (bf16[528,1024]{1,0:T(8,128)(2,1)S(1)}, bf16[528,1024]{1,0:T(8,128)(2,1)S(1)}, u32[]{:S(2)}, u32[]{:S(2)}) collective-permute-start(bf16[528,1024]{1,0:T(8,128)(2,1)S(1)} %collective-permute-done.2.refs_0_), channel_id=1, source_target_pairs={{16,0},{17,1},{18,2},{19,3},{20,4},{21,5},{22,6},{23,7},{24,8},{25... | collective-permute-start | bytes 3244040 | tf_op jit(solution)/shard_map/ppermute | solution.py:252
  44.3 0.0 collective-permute-done.3.refs_0_
  44.3 0.6 collective-permute-start.8
  44.9 2.5 %shard_map.49 = (bf16[11,512,1024]{2,1,0:T(8,128)(2,1)S(1)}, f32[11,512,128]{2,1,0:T(8,128)S(1)}, f32[11,2,8,256]{3,2,1,0:T(8,128)S(1)}, s32[8,128]{1,0:T(8,128)S(1)}) custom-call(s32[105]{0:T(128)S(1)} %dynamic-slice_bitcast_fusion.tab, s32[8,128]{1,0:T(8,128)S(1)} %get-tuple-element.44.turn_in, ...), custom_call_target="tpu_custom_call", output_to_operand_aliasing={{0}: (3, {}), {1}: (4, {}), {2}: (5, {})} | custom-call | flops 1000 | bytes 1000 | tf_op jit(solution)/shard_map/pallas_call | solution.py:261
  47.3 3.0 %shard_map.50 = (bf16[11,512,1024]{2,1,0:T(8,128)(2,1)S(1)}, f32[11,512,128]{2,1,0:T(8,128)S(1)}, f32[11,2,8,256]{3,2,1,0:T(8,128)S(1)}, s32[8,128]{1,0:T(8,128)S(1)}) custom-call(s32[105]{0:T(128)S(1)} %dynamic-slice_bitcast_fusion.tab, s32[8,128]{1,0:T(8,128)S(1)} %get-tuple-element.49.turn_in, ...), custom_call_target="tpu_custom_call", output_to_operand_aliasing={{0}: (3, {}), {1}: (4, {}), {2}: (5, {})} | custom-call | flops 1000 | bytes 1000 | tf_op jit(solution)/shard_map/pallas_call | solution.py:261
  50.4 0.0 collective-permute-done.4.refs_0_
  50.4 3.4 %collective-permute-start.9 = (bf16[528,1024]{1,0:T(8,128)(2,1)S(1)}, bf16[528,1024]{1,0:T(8,128)(2,1)S(1)}, u32[]{:S(2)}, u32[]{:S(2)}) collective-permute-start(bf16[528,1024]{1,0:T(8,128)(2,1)S(1)} %collective-permute-done.4.refs_0_), channel_id=1, source_target_pairs={{1,0},{2,1},{3,2},{0,3},{5,4},{6,5},{7,6},{4,7},{9,8},{10,9},{11,1... | collective-permute-start | bytes 3244040 | tf_op jit(solution)/shard_map/ppermute | solution.py:252
  53.8 3.6 %shard_map.51 = (bf16[11,512,1024]{2,1,0:T(8,128)(2,1)S(1)}, f32[11,512,128]{2,1,0:T(8,128)S(1)}, f32[11,2,8,256]{3,2,1,0:T(8,128)S(1)}, s32[8,128]{1,0:T(8,128)S(1)}) custom-call(s32[105]{0:T(128)S(1)} %dynamic-slice_bitcast_fusion.tab, s32[8,128]{1,0:T(8,128)S(1)} %get-tuple-element.54.turn_in, ...), custom_call_target="tpu_custom_call", output_to_operand_aliasing={{0}: (3, {}), {1}: (4, {}), {2}: (5, {})} | custom-call | flops 1000 | bytes 1000 | tf_op jit(solution)/shard_map/pallas_call | solution.py:261
  57.4 0.0 collective-permute-done.5.refs_0_
  57.4 0.0 collective-permute-done.6.refs_1_
  57.4 4.6 %shard_map.52 = (bf16[11,512,1024]{2,1,0:T(8,128)(2,1)S(1)}, f32[11,512,128]{2,1,0:T(8,128)S(1)}, f32[11,2,8,256]{3,2,1,0:T(8,128)S(1)}, s32[8,128]{1,0:T(8,128)S(1)}) custom-call(s32[105]{0:T(128)S(1)} %dynamic-slice_bitcast_fusion.tab, s32[8,128]{1,0:T(8,128)S(1)} %get-tuple-element.58.turn_in, ...), custom_call_target="tpu_custom_call", output_to_operand_aliasing={{0}: (4, {}), {1}: (5, {}), {2}: (6, {})} | custom-call | flops 1000 | bytes 1000 | tf_op jit(solution)/shard_map/pallas_call | solution.py:261
  61.9 0.0 collective-permute-done.7.refs_0_
  62.0 0.0 collective-permute-done.8.refs_1_
  62.0 5.1 %shard_map.53 = (bf16[11,512,1024]{2,1,0:T(8,128)(2,1)S(1)}, f32[11,512,128]{2,1,0:T(8,128)S(1)}, f32[11,2,8,256]{3,2,1,0:T(8,128)S(1)}, s32[8,128]{1,0:T(8,128)S(1)}) custom-call(s32[105]{0:T(128)S(1)} %dynamic-slice_bitcast_fusion.tab, s32[8,128]{1,0:T(8,128)S(1)} %get-tuple-element.62.turn_in, ...), custom_call_target="tpu_custom_call", output_to_operand_aliasing={{0}: (4, {}), {1}: (5, {}), {2}: (6, {})} | custom-call | flops 1000 | bytes 1000 | tf_op jit(solution)/shard_map/pallas_call | solution.py:261
  67.1 0.0 collective-permute-done.9.refs_0_
  67.1 2.8 %shard_map.54 = (bf16[11,512,1024]{2,1,0:T(8,128)(2,1)S(1)}, f32[11,512,128]{2,1,0:T(8,128)S(1)}, f32[11,2,8,256]{3,2,1,0:T(8,128)S(1)}, s32[8,128]{1,0:T(8,128)...) custom-call(s32[105]{0:T(128)S(1)} %dynamic-slice_bitcast_fusion.tab, ...), custom_call_target="tpu_custom_call", output_to_operand_aliasing={{0}: (3, {}), {1}: (4, {}), {2}: (5, {})} | custom-call | flops 1000 | bytes 1000 | tf_op jit(solution)/shard_map/pallas_call | solution.py:261
  69.9 0.0 collective-permute-start.10
  69.9 3.2 %collective-permute-start.11 = (f32[9,512]{1,0:T(8,128)S(1)}, f32[9,512]{1,0:T(8,128)S(1)}, u32[]{:S(2)}, u32[]{:S(2)}) collective-permute-start(f32[9,512]{1,0:T(8,128)S(1)} %get-tuple-element.74), channel_id=1, source_target_pairs={{16,0},{17,1},{18,2},{19,3},{20,4},{21,5},{22,6},{23,7},{24,8},{25... | collective-permute-start | bytes 55304 | tf_op jit(solution)/shard_map/ppermute | solution.py:281
  73.1 2.1 %collective-permute-done.10 = f32[9,512]{1,0:T(8,128)S(1)} collective-permute-done((f32[9,512]{1,0:T(8,128)S(1)}, f32[9,512]{1,0:T(8,128)S(1)}, u32[]{:S(2)}, u32[]{:S(2)}) %collective-permute-start.10) | collective-permute-done | bytes 18464 | tf_op jit(solution)/shard_map/ppermute | solution.py:280
  75.2 0.0 collective-permute-done.11
  75.2 3.0 %collective-permute-start.12 = (f32[3,512]{1,0:T(4,128)S(1)}, f32[3,512]{1,0:T(4,128)S(1)}, u32[]{:S(2)}, u32[]{:S(2)}) collective-permute-start(f32[3,512]{1,0:T(4,128)S(1)} %get-tuple-element.76), channel_id=1, source_target_pairs={{12,0},{13,1},{14,2},{15,3},{0,4},{1,5},{2,6},{3,7},{4,8},{5,9},{6... | collective-permute-start | bytes 18440 | tf_op jit(solution)/shard_map/ppermute | solution.py:280
  78.2 3.8 %collective-permute-start.13 = (f32[3,512]{1,0:T(4,128)S(1)}, f32[3,512]{1,0:T(4,128)S(1)}, u32[]{:S(2)}, u32[]{:S(2)}) collective-permute-start(f32[3,512]{1,0:T(4,128)S(1)} %get-tuple-element.75), channel_id=1, source_target_pairs={{4,0},{5,1},{6,2},{7,3},{8,4},{9,5},{10,6},{11,7},{12,8},{13,9},{1... | collective-permute-start | bytes 18440 | tf_op jit(solution)/shard_map/ppermute | solution.py:281
  82.0 1.5 %collective-permute-done.12 = f32[3,512]{1,0:T(4,128)S(1)} collective-permute-done((f32[3,512]{1,0:T(4,128)S(1)}, f32[3,512]{1,0:T(4,128)S(1)}, u32[]{:S(2)}, u32[]{:S(2)}) %collective-permute-start.12) | collective-permute-done | bytes 6176 | tf_op jit(solution)/shard_map/ppermute | solution.py:280
  83.5 0.0 collective-permute-done.13
  83.5 1.3 %collective-permute-start.14 = (f32[1,512]{1,0:T(1,128)S(1)}, f32[1,512]{1,0:T(1,128)S(1)}, u32[]{:S(2)}, u32[]{:S(2)}) collective-permute-start(f32[1,512]{1,0:T(1,128)S(1)} %get-tuple-element.78), channel_id=1, source_target_pairs={{3,0},{0,1},{1,2},{2,3},{7,4},{4,5},{5,6},{6,7},{11,8},{8,9},{9,10... | collective-permute-start | bytes 6152 | tf_op jit(solution)/shard_map/ppermute | solution.py:280
  84.9 2.0 %collective-permute-start.15 = (f32[1,512]{1,0:T(1,128)S(1)}, f32[1,512]{1,0:T(1,128)S(1)}, u32[]{:S(2)}, u32[]{:S(2)}) collective-permute-start(f32[1,512]{1,0:T(1,128)S(1)} %get-tuple-element.77), channel_id=1, source_target_pairs={{1,0},{2,1},{3,2},{0,3},{5,4},{6,5},{7,6},{4,7},{9,8},{10,9},{11,1... | collective-permute-start | bytes 6152 | tf_op jit(solution)/shard_map/ppermute | solution.py:281
  86.8 1.6 %collective-permute-done.14 = f32[1,512]{1,0:T(1,128)S(1)} collective-permute-done((f32[1,512]{1,0:T(1,128)S(1)}, f32[1,512]{1,0:T(1,128)S(1)}, u32[]{:S(2)}, u32[]{:S(2)}) %collective-permute-start.14) | collective-permute-done | bytes 2080 | tf_op jit(solution)/shard_map/ppermute | solution.py:280
  88.4 0.1 collective-permute-done.15
  88.5 0.6 fusion
  (4 shorter events, 0.0 us)
Async XLA Ops:
  2.2 15.8 %collective-permute-start = (bf16[528,1024]{1,0:T(8,128)(2,1)S(1)}, bf16[528,1024]{1,0:T(8,128)(2,1)S(1)}, u32[]{:S(2)}, u32[]{:S(2)}) collective-permute-start(bf16[528,1024]{1,0:T(8,128)(2,1)S(1)} %shard_map.46.t_ref), channel_id=1, source_target_pairs={{4,0},{5,1},{6,2},{7,3},{8,4},{9,5},{10,6},{11,7},{12,8},{13,9},{1... | collective-permute-start | bytes 3244040 | tf_op jit(solution)/shard_map/ppermute | solution.py:252
  5.3 18.2 %collective-permute-start.1 = (bf16[528,1024]{1,0:T(8,128)(2,1)S(1)}, bf16[528,1024]{1,0:T(8,128)(2,1)S(1)}, u32[]{:S(2)}, u32[]{:S(2)}) collective-permute-start(bf16[528,1024]{1,0:T(8,128)(2,1)S(1)} %shard_map.46.t_ref), channel_id=1, source_target_pairs={{49,0},{50,1},{51,2},{48,3},{53,4},{54,5},{55,6},{52,7},{57,8},{58... | collective-permute-start | bytes 3244040 | tf_op jit(solution)/shard_map/ppermute | solution.py:252
  18.0 21.2 %collective-permute-start.2 = (bf16[528,1024]{1,0:T(8,128)(2,1)S(1)}, bf16[528,1024]{1,0:T(8,128)(2,1)S(1)}, u32[]{:S(2)}, u32[]{:S(2)}) collective-permute-start(bf16[528,1024]{1,0:T(8,128)(2,1)S(1)} %collective-permute-done.refs_0_), channel_id=1, source_target_pairs={{3,0},{0,1},{1,2},{2,3},{7,4},{4,5},{5,6},{6,7},{11,8},{8,9},{9,10... | collective-permute-start | bytes 3244040 | tf_op jit(solution)/shard_map/ppermute | solution.py:252
  19.5 24.8 %collective-permute-start.3 = (bf16[528,1024]{1,0:T(8,128)(2,1)S(1)}, bf16[528,1024]{1,0:T(8,128)(2,1)S(1)}, u32[]{:S(2)}, u32[]{:S(2)}) collective-permute-start(bf16[528,1024]{1,0:T(8,128)(2,1)S(1)} %shard_map.46.t_ref), channel_id=1, source_target_pairs={{60,0},{61,1},{62,2},{63,3},{48,4},{49,5},{50,6},{51,7},{52,8},{53... | collective-permute-start | bytes 3244040 | tf_op jit(solution)/shard_map/ppermute | solution.py:252
  21.9 28.5 %collective-permute-start.4 = (bf16[528,1024]{1,0:T(8,128)(2,1)S(1)}, bf16[528,1024]{1,0:T(8,128)(2,1)S(1)}, u32[]{:S(2)}, u32[]{:S(2)}) collective-permute-start(bf16[528,1024]{1,0:T(8,128)(2,1)S(1)} %shard_map.46.t_ref), channel_id=1, source_target_pairs={{16,0},{17,1},{18,2},{19,3},{20,4},{21,5},{22,6},{23,7},{24,8},{25... | collective-permute-start | bytes 3244040 | tf_op jit(solution)/shard_map/ppermute | solution.py:252
  23.5 33.8 %collective-permute-start.5 = (bf16[528,1024]{1,0:T(8,128)(2,1)S(1)}, bf16[528,1024]{1,0:T(8,128)(2,1)S(1)}, u32[]{:S(2)}, u32[]{:S(2)}) collective-permute-start(bf16[528,1024]{1,0:T(8,128)(2,1)S(1)} %collective-permute-done.1.refs_1_), channel_id=1, source_target_pairs={{12,0},{13,1},{14,2},{15,3},{0,4},{1,5},{2,6},{3,7},{4,8},{5,9},{6... | collective-permute-start | bytes 3244040 | tf_op jit(solution)/shard_map/ppermute | solution.py:252
  24.8 32.6 %collective-permute-start.6 = (bf16[528,1024]{1,0:T(8,128)(2,1)S(1)}, bf16[528,1024]{1,0:T(8,128)(2,1)S(1)}, u32[]{:S(2)}, u32[]{:S(2)}) collective-permute-start(bf16[528,1024]{1,0:T(8,128)(2,1)S(1)} %collective-permute-done.1.refs_1_), channel_id=1, source_target_pairs={{4,0},{5,1},{6,2},{7,3},{8,4},{9,5},{10,6},{11,7},{12,8},{13,9},{1... | collective-permute-start | bytes 3244040 | tf_op jit(solution)/shard_map/ppermute | solution.py:252
  39.1 22.8 %collective-permute-start.7 = (bf16[528,1024]{1,0:T(8,128)(2,1)S(1)}, bf16[528,1024]{1,0:T(8,128)(2,1)S(1)}, u32[]{:S(2)}, u32[]{:S(2)}) collective-permute-start(bf16[528,1024]{1,0:T(8,128)(2,1)S(1)} %collective-permute-done.2.refs_0_), channel_id=1, source_target_pairs={{16,0},{17,1},{18,2},{19,3},{20,4},{21,5},{22,6},{23,7},{24,8},{25... | collective-permute-start | bytes 3244040 | tf_op jit(solution)/shard_map/ppermute | solution.py:252
  44.3 17.7 %collective-permute-start.8 = (bf16[528,1024]{1,0:T(8,128)(2,1)S(1)}, bf16[528,1024]{1,0:T(8,128)(2,1)S(1)}, u32[]{:S(2)}, u32[]{:S(2)}) collective-permute-start(bf16[528,1024]{1,0:T(8,128)(2,1)S(1)} %collective-permute-done.3.refs_0_), channel_id=1, source_target_pairs={{3,0},{0,1},{1,2},{2,3},{7,4},{4,5},{5,6},{6,7},{11,8},{8,9},{9,10... | collective-permute-start | bytes 3244040 | tf_op jit(solution)/shard_map/ppermute | solution.py:252
  50.4 16.7 %collective-permute-start.9 = (bf16[528,1024]{1,0:T(8,128)(2,1)S(1)}, bf16[528,1024]{1,0:T(8,128)(2,1)S(1)}, u32[]{:S(2)}, u32[]{:S(2)}) collective-permute-start(bf16[528,1024]{1,0:T(8,128)(2,1)S(1)} %collective-permute-done.4.refs_0_), channel_id=1, source_target_pairs={{1,0},{2,1},{3,2},{0,3},{5,4},{6,5},{7,6},{4,7},{9,8},{10,9},{11,1... | collective-permute-start | bytes 3244040 | tf_op jit(solution)/shard_map/ppermute | solution.py:252
  69.9 5.3 %collective-permute-start.10 = (f32[9,512]{1,0:T(8,128)S(1)}, f32[9,512]{1,0:T(8,128)S(1)}, u32[]{:S(2)}, u32[]{:S(2)}) collective-permute-start(f32[9,512]{1,0:T(8,128)S(1)} %get-tuple-element.73), channel_id=1, source_target_pairs={{48,0},{49,1},{50,2},{51,3},{52,4},{53,5},{54,6},{55,7},{56,8},{57... | collective-permute-start | bytes 55304 | tf_op jit(solution)/shard_map/ppermute | solution.py:280
  69.9 5.3 %collective-permute-start.11 = (f32[9,512]{1,0:T(8,128)S(1)}, f32[9,512]{1,0:T(8,128)S(1)}, u32[]{:S(2)}, u32[]{:S(2)}) collective-permute-start(f32[9,512]{1,0:T(8,128)S(1)} %get-tuple-element.74), channel_id=1, source_target_pairs={{16,0},{17,1},{18,2},{19,3},{20,4},{21,5},{22,6},{23,7},{24,8},{25... | collective-permute-start | bytes 55304 | tf_op jit(solution)/shard_map/ppermute | solution.py:281
  75.2 8.3 %collective-permute-start.12 = (f32[3,512]{1,0:T(4,128)S(1)}, f32[3,512]{1,0:T(4,128)S(1)}, u32[]{:S(2)}, u32[]{:S(2)}) collective-permute-start(f32[3,512]{1,0:T(4,128)S(1)} %get-tuple-element.76), channel_id=1, source_target_pairs={{12,0},{13,1},{14,2},{15,3},{0,4},{1,5},{2,6},{3,7},{4,8},{5,9},{6... | collective-permute-start | bytes 18440 | tf_op jit(solution)/shard_map/ppermute | solution.py:280
  78.2 5.3 %collective-permute-start.13 = (f32[3,512]{1,0:T(4,128)S(1)}, f32[3,512]{1,0:T(4,128)S(1)}, u32[]{:S(2)}, u32[]{:S(2)}) collective-permute-start(f32[3,512]{1,0:T(4,128)S(1)} %get-tuple-element.75), channel_id=1, source_target_pairs={{4,0},{5,1},{6,2},{7,3},{8,4},{9,5},{10,6},{11,7},{12,8},{13,9},{1... | collective-permute-start | bytes 18440 | tf_op jit(solution)/shard_map/ppermute | solution.py:281
  83.5 4.9 %collective-permute-start.14 = (f32[1,512]{1,0:T(1,128)S(1)}, f32[1,512]{1,0:T(1,128)S(1)}, u32[]{:S(2)}, u32[]{:S(2)}) collective-permute-start(f32[1,512]{1,0:T(1,128)S(1)} %get-tuple-element.78), channel_id=1, source_target_pairs={{3,0},{0,1},{1,2},{2,3},{7,4},{4,5},{5,6},{6,7},{11,8},{8,9},{9,10... | collective-permute-start | bytes 6152 | tf_op jit(solution)/shard_map/ppermute | solution.py:280
  84.9 3.6 %collective-permute-start.15 = (f32[1,512]{1,0:T(1,128)S(1)}, f32[1,512]{1,0:T(1,128)S(1)}, u32[]{:S(2)}, u32[]{:S(2)}) collective-permute-start(f32[1,512]{1,0:T(1,128)S(1)} %get-tuple-element.77), channel_id=1, source_target_pairs={{1,0},{2,1},{3,2},{0,3},{5,4},{6,5},{7,6},{4,7},{9,8},{10,9},{11,1... | collective-permute-start | bytes 6152 | tf_op jit(solution)/shard_map/ppermute | solution.py:281

commit v7 on v5

--- a/solution.py
+++ b/solution.py
@@ -108,18 +108,18 @@
         copies[-1].start()
     copies.append(pltpu.make_async_copy(mask_hbm, mask_ref, sems.at[NORM_PARTS]))
     copies[-1].start()
+    for i in range(NORM_PARTS):
+        copies[i].wait()
+        at = slice(i * part, (i + 1) * part)
+        x = x_ref[at, :].astype(jnp.float32)
+        meansq = jnp.mean(x * x, axis=-1, keepdims=True)
+        out_ref[at, :] = (x * lax.rsqrt(meansq + EPS) * (1.0 / width**0.5)).astype(jnp.bfloat16)
     copies[-1].wait()
     live = (mask_ref[...] == 1) & (alive[0] == 1)
     bias = jnp.broadcast_to(jnp.where(live, 0.0, DEAD), (FLAG_ROWS, rows))
     top = lax.broadcasted_iota(jnp.int32, (FLAG_ROWS, rows), 0) == 0
     out_ref[rows:, :] = jnp.zeros((FLAG_ROWS, width), jnp.bfloat16)
     out_ref[rows:, :rows] = jnp.where(top, bias, 0.0).astype(jnp.bfloat16)
-    for i in range(NORM_PARTS):
-        copies[i].wait()
-        at = slice(i * part, (i + 1) * part)
-        x = x_ref[at, :].astype(jnp.float32)
-        meansq = jnp.mean(x * x, axis=-1, keepdims=True)
-        out_ref[at, :] = (x * lax.rsqrt(meansq + EPS) * (1.0 / width**0.5)).astype(jnp.bfloat16)
 
 
 def dot_t(a, b):

time: 89.2 us -> 89.2 us (level)
  no operation moved by 1% of the time
where the time goes in v7:
time: 89.2 us; the launch traced here: 88.3 us
  starting transfers between devices  39.1 us (44%)
  Pallas kernels  26 us (29%)
  waiting for transfers between devices  21.1 us (24%)
    ppermute x10, starting transfers between devices, on_device(): held[d] = lax.ppermute(sent, ('clus', 'help'), moves(sub(d, source)))  25.6 us
    pallas_call x6, Pallas kernels, on_device(): pl.pallas_call(functools.partial(pair_kernel, new=new, start=start, steps...  23.3 us
    ppermute x10, waiting for transfers between devices, on_device(): held[d] = lax.ppermute(sent, ('clus', 'help'), moves(sub(d, source)))  16 us
    ppermute x3, starting transfers between devices, on_device(): behind = lax.ppermute(behind, ('clus', 'help'), moves(step))  8.98 us
    ppermute x3, waiting for transfers between devices, on_device(): ahead = lax.ppermute(ahead, ('clus', 'help'), moves(back))  4.99 us
    ppermute x3, starting transfers between devices, on_device(): ahead = lax.ppermute(ahead, ('clus', 'help'), moves(back))  4.5 us
  transfers between devices with their start and end apart: 16, of which 5 were waited for; matrix products, arithmetic and copies ran while one was open for 1% of the time, Pallas kernels for 25%

profile of v7, /device:TPU:0, one launch (start us, length us, event | category | flops | bytes accessed | tf_op | source)
XLA Modules:
  0.0 88.3 jit_solution(16036347174864842527)
XLA Ops:
  0.7 1.5 %shard_map.46.t_ref = bf16[528,1024]{1,0:T(8,128)(2,1)S(1)} custom-call(s32[1]{0:T(128)S(6)} %convert_element_type.3.alive, bf16[512,1024]{1,0:T(8,128)(2,1)} %bitcast.7, s32[1,512]{1,0:T(1,128)} %bitcast.8), custom_call_target="tpu_custom_call" | custom-call | tf_op jit(solution)/shard_map/pallas_call | solution.py:223
  2.2 3.2 %collective-permute-start = (bf16[528,1024]{1,0:T(8,128)(2,1)S(1)}, bf16[528,1024]{1,0:T(8,128)(2,1)S(1)}, u32[]{:S(2)}, u32[]{:S(2)}) collective-permute-start(bf16[528,1024]{1,0:T(8,128)(2,1)S(1)} %shard_map.46.t_ref), channel_id=1, source_target_pairs={{4,0},{5,1},{6,2},{7,3},{8,4},{9,5},{10,6},{11,7},{12,8},{13,9},{1... | collective-permute-start | bytes 3244040 | tf_op jit(solution)/shard_map/ppermute | solution.py:252
  5.3 4.1 %collective-permute-start.1 = (bf16[528,1024]{1,0:T(8,128)(2,1)S(1)}, bf16[528,1024]{1,0:T(8,128)(2,1)S(1)}, u32[]{:S(2)}, u32[]{:S(2)}) collective-permute-start(bf16[528,1024]{1,0:T(8,128)(2,1)S(1)} %shard_map.46.t_ref), channel_id=1, source_target_pairs={{49,0},{50,1},{51,2},{48,3},{53,4},{54,5},{55,6},{52,7},{57,8},{58... | collective-permute-start | bytes 3244040 | tf_op jit(solution)/shard_map/ppermute | solution.py:252
  9.4 0.7 dynamic-slice_bitcast_fusion.tab
  10.1 1.2 %shard_map.47 = (bf16[11,512,1024]{2,1,0:T(8,128)(2,1)S(1)}, f32[11,512,128]{2,1,0:T(8,128)S(1)}, f32[11,2,8,256]{3,2,1,0:T(8,128)S(1)}, s32[8,128]{1,0:T(8,128)S(1)}) custom-call(bf16[528,1024]{1,0:T(8,128)(2,1)S(1)} %shard_map.46.t_ref, s32[105]{0:T(128)S(1)} %dynamic-slice_bitcast_fusion.tab), custom_call_target="tpu_custom_call" | custom-call | flops 1000 | bytes 1000 | tf_op jit(solution)/shard_map/pallas_call | solution.py:235
  11.4 6.6 %collective-permute-done.refs_0_ = bf16[528,1024]{1,0:T(8,128)(2,1)S(1)} collective-permute-done((bf16[528,1024]{1,0:T(8,128)(2,1)S(1)}, bf16[528,1024]{1,0:T(8,128)(2,1)S(1)}, u32[]{:S(2)}, u32[]{:S(2)}) %collective-permute-start) | collective-permute-done | bytes 1081376 | tf_op jit(solution)/shard_map/ppermute | solution.py:252
  18.0 1.5 %collective-permute-start.2 = (bf16[528,1024]{1,0:T(8,128)(2,1)S(1)}, bf16[528,1024]{1,0:T(8,128)(2,1)S(1)}, u32[]{:S(2)}, u32[]{:S(2)}) collective-permute-start(bf16[528,1024]{1,0:T(8,128)(2,1)S(1)} %collective-permute-done.refs_0_), channel_id=1, source_target_pairs={{3,0},{0,1},{1,2},{2,3},{7,4},{4,5},{5,6},{6,7},{11,8},{8,9},{9,10... | collective-permute-start | bytes 3244040 | tf_op jit(solution)/shard_map/ppermute | solution.py:252
  19.5 2.4 %collective-permute-start.3 = (bf16[528,1024]{1,0:T(8,128)(2,1)S(1)}, bf16[528,1024]{1,0:T(8,128)(2,1)S(1)}, u32[]{:S(2)}, u32[]{:S(2)}) collective-permute-start(bf16[528,1024]{1,0:T(8,128)(2,1)S(1)} %shard_map.46.t_ref), channel_id=1, source_target_pairs={{60,0},{61,1},{62,2},{63,3},{48,4},{49,5},{50,6},{51,7},{52,8},{53... | collective-permute-start | bytes 3244040 | tf_op jit(solution)/shard_map/ppermute | solution.py:252
  21.9 1.6 %collective-permute-start.4 = (bf16[528,1024]{1,0:T(8,128)(2,1)S(1)}, bf16[528,1024]{1,0:T(8,128)(2,1)S(1)}, u32[]{:S(2)}, u32[]{:S(2)}) collective-permute-start(bf16[528,1024]{1,0:T(8,128)(2,1)S(1)} %shard_map.46.t_ref), channel_id=1, source_target_pairs={{16,0},{17,1},{18,2},{19,3},{20,4},{21,5},{22,6},{23,7},{24,8},{25... | collective-permute-start | bytes 3244040 | tf_op jit(solution)/shard_map/ppermute | solution.py:252
  23.5 0.0 collective-permute-done.1.refs_1_
  23.5 1.3 %collective-permute-start.5 = (bf16[528,1024]{1,0:T(8,128)(2,1)S(1)}, bf16[528,1024]{1,0:T(8,128)(2,1)S(1)}, u32[]{:S(2)}, u32[]{:S(2)}) collective-permute-start(bf16[528,1024]{1,0:T(8,128)(2,1)S(1)} %collective-permute-done.1.refs_1_), channel_id=1, source_target_pairs={{12,0},{13,1},{14,2},{15,3},{0,4},{1,5},{2,6},{3,7},{4,8},{5,9},{6... | collective-permute-start | bytes 3244040 | tf_op jit(solution)/shard_map/ppermute | solution.py:252
  24.8 2.4 %collective-permute-start.6 = (bf16[528,1024]{1,0:T(8,128)(2,1)S(1)}, bf16[528,1024]{1,0:T(8,128)(2,1)S(1)}, u32[]{:S(2)}, u32[]{:S(2)}) collective-permute-start(bf16[528,1024]{1,0:T(8,128)(2,1)S(1)} %collective-permute-done.1.refs_1_), channel_id=1, source_target_pairs={{4,0},{5,1},{6,2},{7,3},{8,4},{9,5},{10,6},{11,7},{12,8},{13,9},{1... | collective-permute-start | bytes 3244040 | tf_op jit(solution)/shard_map/ppermute | solution.py:252
  27.2 2.5 %shard_map.48 = (bf16[11,512,1024]{2,1,0:T(8,128)(2,1)S(1)}, f32[11,512,128]{2,1,0:T(8,128)S(1)}, f32[11,2,8,256]{3,2,1,0:T(8,128)S(1)}, s32[8,128]{1,0:T(8,128)S(1)}) custom-call(s32[105]{0:T(128)S(1)} %dynamic-slice_bitcast_fusion.tab, s32[8,128]{1,0:T(8,128)S(1)} %get-tuple-element.36.turn_in, ...), custom_call_target="tpu_custom_call", output_to_operand_aliasing={{0}: (4, {}), {1}: (5, {}), {2}: (6, {})} | custom-call | flops 1000 | bytes 1000 | tf_op jit(solution)/shard_map/pallas_call | solution.py:261
  29.8 9.4 %collective-permute-done.2.refs_0_ = bf16[528,1024]{1,0:T(8,128)(2,1)S(1)} collective-permute-done((bf16[528,1024]{1,0:T(8,128)(2,1)S(1)}, bf16[528,1024]{1,0:T(8,128)(2,1)S(1)}, u32[]{:S(2)}, u32[]{:S(2)}) %collective-permute-start.2) | collective-permute-done | bytes 1081376 | tf_op jit(solution)/shard_map/ppermute | solution.py:252
  39.2 5.1 %collective-permute-start.7 = (bf16[528,1024]{1,0:T(8,128)(2,1)S(1)}, bf16[528,1024]{1,0:T(8,128)(2,1)S(1)}, u32[]{:S(2)}, u32[]{:S(2)}) collective-permute-start(bf16[528,1024]{1,0:T(8,128)(2,1)S(1)} %collective-permute-done.2.refs_0_), channel_id=1, source_target_pairs={{16,0},{17,1},{18,2},{19,3},{20,4},{21,5},{22,6},{23,7},{24,8},{25... | collective-permute-start | bytes 3244040 | tf_op jit(solution)/shard_map/ppermute | solution.py:252
  44.3 0.0 collective-permute-done.3.refs_1_
  44.3 0.6 collective-permute-start.8
  44.9 4.7 %shard_map.49 = (bf16[11,512,1024]{2,1,0:T(8,128)(2,1)S(1)}, f32[11,512,128]{2,1,0:T(8,128)S(1)}, f32[11,2,8,256]{3,2,1,0:T(8,128)S(1)}, s32[8,128]{1,0:T(8,128)S(1)}) custom-call(s32[105]{0:T(128)S(1)} %dynamic-slice_bitcast_fusion.tab, s32[8,128]{1,0:T(8,128)S(1)} %get-tuple-element.40.turn_in, ...), custom_call_target="tpu_custom_call", output_to_operand_aliasing={{0}: (4, {}), {1}: (5, {}), {2}: (6, {})} | custom-call | flops 1000 | bytes 1000 | tf_op jit(solution)/shard_map/pallas_call | solution.py:261
  49.6 0.0 collective-permute-done.4.refs_0_
  49.6 3.4 %collective-permute-start.9 = (bf16[528,1024]{1,0:T(8,128)(2,1)S(1)}, bf16[528,1024]{1,0:T(8,128)(2,1)S(1)}, u32[]{:S(2)}, u32[]{:S(2)}) collective-permute-start(bf16[528,1024]{1,0:T(8,128)(2,1)S(1)} %collective-permute-done.4.refs_0_), channel_id=1, source_target_pairs={{1,0},{2,1},{3,2},{0,3},{5,4},{6,5},{7,6},{4,7},{9,8},{10,9},{11,1... | collective-permute-start | bytes 3244040 | tf_op jit(solution)/shard_map/ppermute | solution.py:252
  53.0 3.5 %shard_map.50 = (bf16[11,512,1024]{2,1,0:T(8,128)(2,1)S(1)}, f32[11,512,128]{2,1,0:T(8,128)S(1)}, f32[11,2,8,256]{3,2,1,0:T(8,128)S(1)}, s32[8,128]{1,0:T(8,128)S(1)}) custom-call(s32[105]{0:T(128)S(1)} %dynamic-slice_bitcast_fusion.tab, s32[8,128]{1,0:T(8,128)S(1)} %get-tuple-element.46.turn_in, ...), custom_call_target="tpu_custom_call", output_to_operand_aliasing={{0}: (3, {}), {1}: (4, {}), {2}: (5, {})} | custom-call | flops 1000 | bytes 1000 | tf_op jit(solution)/shard_map/pallas_call | solution.py:261
  56.6 0.0 collective-permute-done.5.refs_0_
  56.6 0.0 collective-permute-done.6.refs_1_
  56.6 4.6 %shard_map.51 = (bf16[11,512,1024]{2,1,0:T(8,128)(2,1)S(1)}, f32[11,512,128]{2,1,0:T(8,128)S(1)}, f32[11,2,8,256]{3,2,1,0:T(8,128)S(1)}, s32[8,128]{1,0:T(8,128)S(1)}) custom-call(s32[105]{0:T(128)S(1)} %dynamic-slice_bitcast_fusion.tab, s32[8,128]{1,0:T(8,128)S(1)} %get-tuple-element.50.turn_in, ...), custom_call_target="tpu_custom_call", output_to_operand_aliasing={{0}: (4, {}), {1}: (5, {}), {2}: (6, {})} | custom-call | flops 1000 | bytes 1000 | tf_op jit(solution)/shard_map/pallas_call | solution.py:261
  61.2 0.0 collective-permute-done.7.refs_0_
  61.2 0.0 collective-permute-done.8.refs_1_
  61.2 5.1 %shard_map.52 = (bf16[11,512,1024]{2,1,0:T(8,128)(2,1)S(1)}, f32[11,512,128]{2,1,0:T(8,128)S(1)}, f32[11,2,8,256]{3,2,1,0:T(8,128)S(1)}, s32[8,128]{1,0:T(8,128)S(1)}) custom-call(s32[105]{0:T(128)S(1)} %dynamic-slice_bitcast_fusion.tab, s32[8,128]{1,0:T(8,128)S(1)} %get-tuple-element.54.turn_in, ...), custom_call_target="tpu_custom_call", output_to_operand_aliasing={{0}: (4, {}), {1}: (5, {}), {2}: (6, {})} | custom-call | flops 1000 | bytes 1000 | tf_op jit(solution)/shard_map/pallas_call | solution.py:261
  66.3 0.0 collective-permute-done.9.refs_0_
  66.3 2.8 %shard_map.53 = (bf16[11,512,1024]{2,1,0:T(8,128)(2,1)S(1)}, f32[11,512,128]{2,1,0:T(8,128)S(1)}, f32[11,2,8,256]{3,2,1,0:T(8,128)S(1)}, s32[8,128]{1,0:T(8,128)...) custom-call(s32[105]{0:T(128)S(1)} %dynamic-slice_bitcast_fusion.tab, ...), custom_call_target="tpu_custom_call", output_to_operand_aliasing={{0}: (3, {}), {1}: (4, {}), {2}: (5, {})} | custom-call | flops 1000 | bytes 1000 | tf_op jit(solution)/shard_map/pallas_call | solution.py:261
  69.1 0.0 collective-permute-start.10
  69.1 3.2 %collective-permute-start.11 = (f32[9,512]{1,0:T(8,128)S(1)}, f32[9,512]{1,0:T(8,128)S(1)}, u32[]{:S(2)}, u32[]{:S(2)}) collective-permute-start(f32[9,512]{1,0:T(8,128)S(1)} %get-tuple-element.66), channel_id=1, source_target_pairs={{16,0},{17,1},{18,2},{19,3},{20,4},{21,5},{22,6},{23,7},{24,8},{25... | collective-permute-start | bytes 55304 | tf_op jit(solution)/shard_map/ppermute | solution.py:281
  72.4 1.9 %collective-permute-done.10 = f32[9,512]{1,0:T(8,128)S(1)} collective-permute-done((f32[9,512]{1,0:T(8,128)S(1)}, f32[9,512]{1,0:T(8,128)S(1)}, u32[]{:S(2)}, u32[]{:S(2)}) %collective-permute-start.10) | collective-permute-done | bytes 18464 | tf_op jit(solution)/shard_map/ppermute | solution.py:280
  74.2 0.0 collective-permute-done.11
  74.3 3.2 %collective-permute-start.12 = (f32[3,512]{1,0:T(4,128)S(1)}, f32[3,512]{1,0:T(4,128)S(1)}, u32[]{:S(2)}, u32[]{:S(2)}) collective-permute-start(f32[3,512]{1,0:T(4,128)S(1)} %get-tuple-element.68), channel_id=1, source_target_pairs={{12,0},{13,1},{14,2},{15,3},{0,4},{1,5},{2,6},{3,7},{4,8},{5,9},{6... | collective-permute-start | bytes 18440 | tf_op jit(solution)/shard_map/ppermute | solution.py:280
  77.4 3.8 %collective-permute-start.13 = (f32[3,512]{1,0:T(4,128)S(1)}, f32[3,512]{1,0:T(4,128)S(1)}, u32[]{:S(2)}, u32[]{:S(2)}) collective-permute-start(f32[3,512]{1,0:T(4,128)S(1)} %get-tuple-element.67), channel_id=1, source_target_pairs={{4,0},{5,1},{6,2},{7,3},{8,4},{9,5},{10,6},{11,7},{12,8},{13,9},{1... | collective-permute-start | bytes 18440 | tf_op jit(solution)/shard_map/ppermute | solution.py:281
  81.2 1.5 %collective-permute-done.12 = f32[3,512]{1,0:T(4,128)S(1)} collective-permute-done((f32[3,512]{1,0:T(4,128)S(1)}, f32[3,512]{1,0:T(4,128)S(1)}, u32[]{:S(2)}, u32[]{:S(2)}) %collective-permute-start.12) | collective-permute-done | bytes 6176 | tf_op jit(solution)/shard_map/ppermute | solution.py:280
  82.8 0.0 collective-permute-done.13
  82.8 1.3 %collective-permute-start.14 = (f32[1,512]{1,0:T(1,128)S(1)}, f32[1,512]{1,0:T(1,128)S(1)}, u32[]{:S(2)}, u32[]{:S(2)}) collective-permute-start(f32[1,512]{1,0:T(1,128)S(1)} %get-tuple-element.70), channel_id=1, source_target_pairs={{3,0},{0,1},{1,2},{2,3},{7,4},{4,5},{5,6},{6,7},{11,8},{8,9},{9,10... | collective-permute-start | bytes 6152 | tf_op jit(solution)/shard_map/ppermute | solution.py:280
  84.1 2.0 %collective-permute-start.15 = (f32[1,512]{1,0:T(1,128)S(1)}, f32[1,512]{1,0:T(1,128)S(1)}, u32[]{:S(2)}, u32[]{:S(2)}) collective-permute-start(f32[1,512]{1,0:T(1,128)S(1)} %get-tuple-element.69), channel_id=1, source_target_pairs={{1,0},{2,1},{3,2},{0,3},{5,4},{6,5},{7,6},{4,7},{9,8},{10,9},{11,1... | collective-permute-start | bytes 6152 | tf_op jit(solution)/shard_map/ppermute | solution.py:281
  86.1 1.6 %collective-permute-done.14 = f32[1,512]{1,0:T(1,128)S(1)} collective-permute-done((f32[1,512]{1,0:T(1,128)S(1)}, f32[1,512]{1,0:T(1,128)S(1)}, u32[]{:S(2)}, u32[]{:S(2)}) %collective-permute-start.14) | collective-permute-done | bytes 2080 | tf_op jit(solution)/shard_map/ppermute | solution.py:280
  87.6 0.0 collective-permute-done.15
  87.7 0.6 fusion
  (4 shorter events, 0.0 us)
Async XLA Ops:
  2.2 15.8 %collective-permute-start = (bf16[528,1024]{1,0:T(8,128)(2,1)S(1)}, bf16[528,1024]{1,0:T(8,128)(2,1)S(1)}, u32[]{:S(2)}, u32[]{:S(2)}) collective-permute-start(bf16[528,1024]{1,0:T(8,128)(2,1)S(1)} %shard_map.46.t_ref), channel_id=1, source_target_pairs={{4,0},{5,1},{6,2},{7,3},{8,4},{9,5},{10,6},{11,7},{12,8},{13,9},{1... | collective-permute-start | bytes 3244040 | tf_op jit(solution)/shard_map/ppermute | solution.py:252
  5.3 18.2 %collective-permute-start.1 = (bf16[528,1024]{1,0:T(8,128)(2,1)S(1)}, bf16[528,1024]{1,0:T(8,128)(2,1)S(1)}, u32[]{:S(2)}, u32[]{:S(2)}) collective-permute-start(bf16[528,1024]{1,0:T(8,128)(2,1)S(1)} %shard_map.46.t_ref), channel_id=1, source_target_pairs={{49,0},{50,1},{51,2},{48,3},{53,4},{54,5},{55,6},{52,7},{57,8},{58... | collective-permute-start | bytes 3244040 | tf_op jit(solution)/shard_map/ppermute | solution.py:252
  18.0 21.2 %collective-permute-start.2 = (bf16[528,1024]{1,0:T(8,128)(2,1)S(1)}, bf16[528,1024]{1,0:T(8,128)(2,1)S(1)}, u32[]{:S(2)}, u32[]{:S(2)}) collective-permute-start(bf16[528,1024]{1,0:T(8,128)(2,1)S(1)} %collective-permute-done.refs_0_), channel_id=1, source_target_pairs={{3,0},{0,1},{1,2},{2,3},{7,4},{4,5},{5,6},{6,7},{11,8},{8,9},{9,10... | collective-permute-start | bytes 3244040 | tf_op jit(solution)/shard_map/ppermute | solution.py:252
  19.5 24.8 %collective-permute-start.3 = (bf16[528,1024]{1,0:T(8,128)(2,1)S(1)}, bf16[528,1024]{1,0:T(8,128)(2,1)S(1)}, u32[]{:S(2)}, u32[]{:S(2)}) collective-permute-start(bf16[528,1024]{1,0:T(8,128)(2,1)S(1)} %shard_map.46.t_ref), channel_id=1, source_target_pairs={{60,0},{61,1},{62,2},{63,3},{48,4},{49,5},{50,6},{51,7},{52,8},{53... | collective-permute-start | bytes 3244040 | tf_op jit(solution)/shard_map/ppermute | solution.py:252
  21.9 27.7 %collective-permute-start.4 = (bf16[528,1024]{1,0:T(8,128)(2,1)S(1)}, bf16[528,1024]{1,0:T(8,128)(2,1)S(1)}, u32[]{:S(2)}, u32[]{:S(2)}) collective-permute-start(bf16[528,1024]{1,0:T(8,128)(2,1)S(1)} %shard_map.46.t_ref), channel_id=1, source_target_pairs={{16,0},{17,1},{18,2},{19,3},{20,4},{21,5},{22,6},{23,7},{24,8},{25... | collective-permute-start | bytes 3244040 | tf_op jit(solution)/shard_map/ppermute | solution.py:252
  23.5 33.1 %collective-permute-start.5 = (bf16[528,1024]{1,0:T(8,128)(2,1)S(1)}, bf16[528,1024]{1,0:T(8,128)(2,1)S(1)}, u32[]{:S(2)}, u32[]{:S(2)}) collective-permute-start(bf16[528,1024]{1,0:T(8,128)(2,1)S(1)} %collective-permute-done.1.refs_1_), channel_id=1, source_target_pairs={{12,0},{13,1},{14,2},{15,3},{0,4},{1,5},{2,6},{3,7},{4,8},{5,9},{6... | collective-permute-start | bytes 3244040 | tf_op jit(solution)/shard_map/ppermute | solution.py:252
  24.8 31.8 %collective-permute-start.6 = (bf16[528,1024]{1,0:T(8,128)(2,1)S(1)}, bf16[528,1024]{1,0:T(8,128)(2,1)S(1)}, u32[]{:S(2)}, u32[]{:S(2)}) collective-permute-start(bf16[528,1024]{1,0:T(8,128)(2,1)S(1)} %collective-permute-done.1.refs_1_), channel_id=1, source_target_pairs={{4,0},{5,1},{6,2},{7,3},{8,4},{9,5},{10,6},{11,7},{12,8},{13,9},{1... | collective-permute-start | bytes 3244040 | tf_op jit(solution)/shard_map/ppermute | solution.py:252
  39.2 22.0 %collective-permute-start.7 = (bf16[528,1024]{1,0:T(8,128)(2,1)S(1)}, bf16[528,1024]{1,0:T(8,128)(2,1)S(1)}, u32[]{:S(2)}, u32[]{:S(2)}) collective-permute-start(bf16[528,1024]{1,0:T(8,128)(2,1)S(1)} %collective-permute-done.2.refs_0_), channel_id=1, source_target_pairs={{16,0},{17,1},{18,2},{19,3},{20,4},{21,5},{22,6},{23,7},{24,8},{25... | collective-permute-start | bytes 3244040 | tf_op jit(solution)/shard_map/ppermute | solution.py:252
  44.3 16.9 %collective-permute-start.8 = (bf16[528,1024]{1,0:T(8,128)(2,1)S(1)}, bf16[528,1024]{1,0:T(8,128)(2,1)S(1)}, u32[]{:S(2)}, u32[]{:S(2)}) collective-permute-start(bf16[528,1024]{1,0:T(8,128)(2,1)S(1)} %collective-permute-done.3.refs_1_), channel_id=1, source_target_pairs={{3,0},{0,1},{1,2},{2,3},{7,4},{4,5},{5,6},{6,7},{11,8},{8,9},{9,10... | collective-permute-start | bytes 3244040 | tf_op jit(solution)/shard_map/ppermute | solution.py:252
  49.6 16.7 %collective-permute-start.9 = (bf16[528,1024]{1,0:T(8,128)(2,1)S(1)}, bf16[528,1024]{1,0:T(8,128)(2,1)S(1)}, u32[]{:S(2)}, u32[]{:S(2)}) collective-permute-start(bf16[528,1024]{1,0:T(8,128)(2,1)S(1)} %collective-permute-done.4.refs_0_), channel_id=1, source_target_pairs={{1,0},{2,1},{3,2},{0,3},{5,4},{6,5},{7,6},{4,7},{9,8},{10,9},{11,1... | collective-permute-start | bytes 3244040 | tf_op jit(solution)/shard_map/ppermute | solution.py:252
  69.1 5.1 %collective-permute-start.10 = (f32[9,512]{1,0:T(8,128)S(1)}, f32[9,512]{1,0:T(8,128)S(1)}, u32[]{:S(2)}, u32[]{:S(2)}) collective-permute-start(f32[9,512]{1,0:T(8,128)S(1)} %get-tuple-element.65), channel_id=1, source_target_pairs={{48,0},{49,1},{50,2},{51,3},{52,4},{53,5},{54,6},{55,7},{56,8},{57... | collective-permute-start | bytes 55304 | tf_op jit(solution)/shard_map/ppermute | solution.py:280
  69.1 5.1 %collective-permute-start.11 = (f32[9,512]{1,0:T(8,128)S(1)}, f32[9,512]{1,0:T(8,128)S(1)}, u32[]{:S(2)}, u32[]{:S(2)}) collective-permute-start(f32[9,512]{1,0:T(8,128)S(1)} %get-tuple-element.66), channel_id=1, source_target_pairs={{16,0},{17,1},{18,2},{19,3},{20,4},{21,5},{22,6},{23,7},{24,8},{25... | collective-permute-start | bytes 55304 | tf_op jit(solution)/shard_map/ppermute | solution.py:281
  74.3 8.5 %collective-permute-start.12 = (f32[3,512]{1,0:T(4,128)S(1)}, f32[3,512]{1,0:T(4,128)S(1)}, u32[]{:S(2)}, u32[]{:S(2)}) collective-permute-start(f32[3,512]{1,0:T(4,128)S(1)} %get-tuple-element.68), channel_id=1, source_target_pairs={{12,0},{13,1},{14,2},{15,3},{0,4},{1,5},{2,6},{3,7},{4,8},{5,9},{6... | collective-permute-start | bytes 18440 | tf_op jit(solution)/shard_map/ppermute | solution.py:280
  77.4 5.3 %collective-permute-start.13 = (f32[3,512]{1,0:T(4,128)S(1)}, f32[3,512]{1,0:T(4,128)S(1)}, u32[]{:S(2)}, u32[]{:S(2)}) collective-permute-start(f32[3,512]{1,0:T(4,128)S(1)} %get-tuple-element.67), channel_id=1, source_target_pairs={{4,0},{5,1},{6,2},{7,3},{8,4},{9,5},{10,6},{11,7},{12,8},{13,9},{1... | collective-permute-start | bytes 18440 | tf_op jit(solution)/shard_map/ppermute | solution.py:281
  82.8 4.9 %collective-permute-start.14 = (f32[1,512]{1,0:T(1,128)S(1)}, f32[1,512]{1,0:T(1,128)S(1)}, u32[]{:S(2)}, u32[]{:S(2)}) collective-permute-start(f32[1,512]{1,0:T(1,128)S(1)} %get-tuple-element.70), channel_id=1, source_target_pairs={{3,0},{0,1},{1,2},{2,3},{7,4},{4,5},{5,6},{6,7},{11,8},{8,9},{9,10... | collective-permute-start | bytes 6152 | tf_op jit(solution)/shard_map/ppermute | solution.py:280
  84.1 3.6 %collective-permute-start.15 = (f32[1,512]{1,0:T(1,128)S(1)}, f32[1,512]{1,0:T(1,128)S(1)}, u32[]{:S(2)}, u32[]{:S(2)}) collective-permute-start(f32[1,512]{1,0:T(1,128)S(1)} %get-tuple-element.69), channel_id=1, source_target_pairs={{1,0},{2,1},{3,2},{0,3},{5,4},{6,5},{7,6},{4,7},{9,8},{10,9},{11,1... | collective-permute-start | bytes 6152 | tf_op jit(solution)/shard_map/ppermute | solution.py:281
